TPU v7x, 128 devices: a whole 4x4x4 slice. The times are simulated.
128 devices in a mesh: dp: 8 (over x, core), label: 16 (over y, z).
Axes of the slice: x: 4, y: 4, z: 4, core: 2. Of those that a mesh axis runs over, the one named last changes fastest.
Arguments:
- queries: bfloat16 [65536, 768], P(('dp', 'label')), may hold values from -6 to 6
- cluster_dest: int32 [65536], P(('dp', 'label')), may hold values from 0 to 4095, as said below
- panels: bfloat16 [2048, 256, 768], P(('dp', 'label')), may hold values from -0.21875 to 0.21875
- scales: bfloat16 [2048, 256], P(('dp', 'label')), may hold values from 0.25 to 4
- shortlist: int32 [128, 24], P(('dp', 'label')), may hold values from 0 to 255, as said below
- positives: int32 [65536, 4], P(('dp', 'label')), may hold values from 0 to 6143
Outputs:
- query_grad: bfloat16 [65536, 768], P(('dp', 'label'))
- panel_grad: bfloat16 [2048, 256, 768], P(('dp', 'label'))
Inputs may be any that keep to these rules, and one draw needn't show every extreme that they name: `cluster_dest`: within one label index, the 8 shards' values together take each of 0 to 4095 once; one shard gives one batch a multiple of 32 rows, at most 96, and exactly 96 for some pairs in every draw. `shortlist`: value v of a batch names panel v % 16 of the device with the batch's dp index and label index v // 16; a batch's 24 values are distinct, at most 2 of them share a label index, and exactly 2 do for some label index in every batch.
All inputs are finite; a program needn't handle non-finite values.
Results may differ from a plain program's by a relative error of at most 0.0053.
Values may be sent and summed in bfloat16 or wider, within the bound.
No kernel may reach another device: no remote copies, remote signals or barrier semaphores. Data moves between devices by JAX's collectives and lax.ppermute only.
A program may use at most 192 MiB of HBM per device.

v0:
```python
import jax
import jax.numpy as jnp
from jax import lax
from jax.sharding import PartitionSpec as P

CAP = 2


def rank_within(labels, count_total):
    onehot = (labels[:, None] == jnp.arange(count_total, dtype=jnp.int32)[None, :]).astype(
        jnp.int32
    )
    return jnp.sum((jnp.cumsum(onehot, axis=0) - 1) * onehot, axis=1)


def label_hits(batch_pos, label_ids):
    return jnp.any(batch_pos[:, :, None, None] == label_ids[None, None, :, :], axis=1).astype(
        jnp.float32
    )


def shards(queries, cluster_dest, panels, scales, shortlist, positives):
    rows_here, feature_width = queries.shape
    pan_count, lane_count = (panels.shape[0], panels.shape[1])
    group_size = lax.axis_size("dp")
    owners = lax.axis_size("label")
    slot_cap = 3 * rows_here // (2 * group_size)
    target = cluster_dest // rows_here
    send_slot = target * slot_cap + rank_within(target, group_size)
    outgoing = (
        jnp.zeros((group_size * slot_cap, feature_width), jnp.bfloat16).at[send_slot].set(queries)
    )
    placed = (
        jnp.full((group_size * slot_cap,), -1, jnp.int32)
        .at[send_slot]
        .set(cluster_dest % rows_here)
    )
    arrived = lax.all_to_all(
        outgoing.reshape(group_size, slot_cap, feature_width),
        "dp",
        split_axis=0,
        concat_axis=0,
        tiled=True,
    )
    arrived_at = lax.all_to_all(
        placed.reshape(group_size, slot_cap), "dp", split_axis=0, concat_axis=0, tiled=True
    )
    landing = jnp.where(arrived_at >= 0, arrived_at, rows_here).reshape(-1)
    batch_input_rows = (
        jnp.zeros((rows_here + 1, feature_width), jnp.bfloat16)
        .at[landing]
        .set(arrived.reshape(-1, feature_width))[:rows_here]
    )
    wanted = shortlist[0]
    slot_total = wanted.shape[0]
    owner_of = wanted // pan_count
    request_slot = owner_of * CAP + rank_within(owner_of, owners)
    requests = (
        jnp.full((owners * CAP,), -1, jnp.int32)
        .at[request_slot]
        .set(wanted % pan_count)
        .reshape(owners, CAP)
    )
    lane_ids = jnp.arange(lane_count, dtype=jnp.int32)
    asked_ids = lax.all_to_all(requests, "label", split_axis=0, concat_axis=0, tiled=True)
    is_used = asked_ids >= 0
    safe_ids = jnp.where(is_used, asked_ids, 0)
    packed = panels[safe_ids]
    packed_scale = jnp.where(is_used[:, :, None], scales[safe_ids], jnp.zeros((), jnp.bfloat16))
    fetched, fetched_scale = (
        lax.all_to_all(packed, "label", split_axis=0, concat_axis=0, tiled=True),
        lax.all_to_all(packed_scale, "label", split_axis=0, concat_axis=0, tiled=True),
    )
    selected_panel = fetched.reshape(owners * CAP, lane_count, feature_width)[request_slot]
    selected_scale = fetched_scale.reshape(owners * CAP, lane_count)[request_slot].astype(
        jnp.float32
    )
    label_scores = (
        jnp.einsum(
            "rp,wjp->rwj", batch_input_rows, selected_panel, preferred_element_type=jnp.float32
        )
        * selected_scale[None]
    )
    label_ids = jnp.arange(slot_total, dtype=jnp.int32)[:, None] * lane_count + lane_ids[None, :]
    error_signal = (
        (jax.nn.sigmoid(label_scores) - label_hits(positives, label_ids)) * selected_scale[None]
    ).astype(jnp.bfloat16)
    query_factor = jnp.einsum(
        "rzp,zpc->rc", error_signal, selected_panel, preferred_element_type=jnp.float32
    )
    gradient_share = jnp.einsum(
        "zbt,zp->btp", error_signal, batch_input_rows, preferred_element_type=jnp.float32
    ).astype(jnp.bfloat16)
    returned = (
        jnp.zeros((owners * CAP, lane_count, feature_width), jnp.bfloat16)
        .at[request_slot]
        .set(gradient_share)
    )
    received = lax.all_to_all(
        returned.reshape(owners, CAP, lane_count, feature_width),
        "label",
        split_axis=0,
        concat_axis=0,
        tiled=True,
    )
    grad_rows = query_factor.astype(jnp.bfloat16)
    picker = (
        asked_ids.reshape(-1)[:, None] == jnp.arange(pan_count, dtype=jnp.int32)[None, :]
    ).astype(jnp.bfloat16)
    panel_grad = jnp.einsum(
        "ip,ild->pld",
        picker,
        received.reshape(owners * CAP, lane_count, feature_width),
        preferred_element_type=jnp.float32,
    ).astype(jnp.bfloat16)
    gathered_back = grad_rows[jnp.where(arrived_at >= 0, arrived_at, 0)]
    sent_home = lax.all_to_all(gathered_back, "dp", split_axis=0, concat_axis=0, tiled=True)
    query_grad = sent_home.reshape(group_size * slot_cap, feature_width)[send_slot]
    return (query_grad, panel_grad)


def solution(mesh):
    placed = (
        P(("dp", "label"), None),
        P(("dp", "label")),
        P(("dp", "label"), None, None),
        P(("dp", "label"), None),
        P(("dp", "label"), None),
        P(("dp", "label"), None),
    )
    return jax.shard_map(
        shards,
        mesh=mesh,
        in_specs=placed,
        out_specs=(P(("dp", "label"), None), P(("dp", "label"), None, None)),
        check_vma=False,
    )
```

profile of v0, /device:TPU:1, one launch (start us, length us, event | category | flops | bytes accessed | tf_op | source)
XLA Modules:
  0.0 677.6 jit_solution(16033082538889056807)
XLA Ops:
  0.6 0.0 copy-start
  0.6 0.7 and_select_fusion
  1.3 0.1 fusion.6
  1.4 0.2 select_reduce_fusion
  1.6 0.7 fusion.14
  2.3 0.6 scatter_custom_fusion.3
  2.9 0.7 all_to_all.37
  3.6 8.6 %all-to-all-start.2 = ((s32[16,1,2]{2,1,0:T(1,128)}), s32[16,1,2]{2,1,0:T(1,128)S(1)}, u32[]{:S(2)}, u32[]{:S(2)}) async-start(s32[16,1,2]{2,1,0:T(1,128)} %bitcast.10), calls=%async_computation.2 | async-start | bytes 16384 | tf_op jit(solution)/shard_map/all_to_all | solution.py:65
  12.2 0.7 add_select_fusion
  12.9 1.1 reduce-window.6
  14.1 0.2 slice_reduce_fusion
  14.3 0.1 fusion.4
  14.5 2.4 scatter_custom_fusion
  16.9 0.7 all_to_all.33
  17.6 1.0 all-to-all-done.2
  18.6 6.4 all-to-all-start
  25.0 0.1 copy.45
  25.1 0.1 copy.48
  25.2 0.1 copy.46
  25.3 0.1 reshape.280
  25.4 0.0 copy-done
  25.4 0.6 gather_fusion.2
  26.0 0.7 broadcast_select_fusion
  26.7 2.8 all-to-all-done
  29.5 4.8 all-to-all-start.4
  34.3 4.2 scatter_custom_fusion.1
  38.4 2.3 all-to-all-done.4
  40.7 5.6 all-to-all-start.1
  46.3 9.4 %gather_fusion = bf16[32,256,768]{2,1,0:T(8,128)(2,1)} fusion(bf16[16,256,768]{2,1,0:T(8,128)(2,1)} %param.8, s32[1024]{0:T(1024)S(1)} %pad_clamp_fusion.3), kind=kCustom, calls=%fused_computation | custom fusion | bytes 25165952 | tf_op jit(solution)/shard_map/gather | solution.py:68
  55.7 7.1 %all-to-all-done.1 = bf16[8,96,768]{2,1,0:T(8,128)(2,1)S(1)} async-done(((bf16[8,96,768]{2,1,0:T(8,128)(2,1)}), bf16[8,96,768]{2,1,0:T(8,128)(2,1)S(1)}, u32[]{:S(2)}, u32[]{:S(2)}) %all-to-all-start.1) | async-done | bytes 1179680 | tf_op jit(solution)/shard_map/all_to_all | solution.py:38
  62.8 1.0 copy-done.2
  63.8 5.1 all-to-all-start.3
  69.0 0.1 copy.49
  69.2 0.1 iota_add_fusion
  69.2 15.2 %compare_reduce_fusion = pred[512,24,256]{2,1,0:T(8,128)(4,1)S(1)} fusion(s32[24,256]{1,0:T(8,128)S(1)} %iota_add_fusion, s32[512,4]{1,0:T(8,128)S(1)} %copy.49), kind=kLoop, calls=%fused_computation.11 | loop fusion | flops 22020096 | bytes 3178496 | tf_op jit(solution)/shard_map/reduce_or | solution.py:17
  84.4 0.5 broadcast.375
  84.9 0.7 reduce.10
  85.6 0.1 all_to_all.35
  85.7 0.1 reshape.312
  85.8 0.6 gather_fusion.3
  86.4 7.2 %scatter_custom_fusion.2 = bf16[513,768]{1,0:T(8,128)(2,1)} fusion(s32[768]{0:T(1024)S(1)} %fusion.10, bf16[768,768]{1,0:T(8,128)(2,1)} %bitcast.79, bf16[]{:T(256)} %constant.79.clone.1), kind=kCustom, calls=%fused_computation.19 | custom fusion | bytes 788480 | tf_op jit(solution)/shard_map/scatter | solution.py:52
  93.6 188.6 %all-to-all-done.3 = bf16[16,2,256,768]{3,2,1,0:T(8,128)(2,1)} async-done(((bf16[16,2,256,768]{3,2,1,0:T(8,128)(2,1)}), bf16[16,2,256,768]{3,2,1,0:T(8,128)(2,1)}, u32[]{:S(2)}, u32[]{:S(2)}) %all-to-all-start.3) | async-done | bytes 12582944 | tf_op jit(solution)/shard_map/all_to_all | solution.py:71
  282.2 10.4 %gather_fusion.1 = bf16[24,256,768]{2,1,0:T(8,128)(2,1)} fusion(bf16[32,256,768]{2,1,0:T(8,128)(2,1)} %bitcast.13, s32[1024]{0:T(1024)S(1)} %pad_clamp_fusion.2), kind=kCustom, calls=%fused_computation.1 | custom fusion | bytes 18874464 | tf_op jit(solution)/shard_map/gather | solution.py:74
  292.6 10.0 %multiply_convert_fusion = bf16[512,24,256]{2,0,1:T(8,128)(2,1)S(1)} fusion(pred[512,24,256]{2,1,0:T(8,128)(4,1)S(1)} %compare_reduce_fusion, f32[24,256]{1,0:T(8,128)S(1)} %convert_element_type.33, bf16[24,256,768]{2,1,0:T(8,128)(2,1)} %gather_fusion.1, bf16[513,768]{1,0:T(8,128)(2,1)} %scatter_custom_fusion.2), kind=kOutput, calls=%fused_computation.12 | convolution fusion | flops 4857004032 | bytes 19685376 | tf_op jit(solution)/shard_map/rp,wjp->rwj/dot_general | solution.py:79
  302.6 0.0 copy-start.5
  302.6 2.7 copy-done.5
  305.3 7.6 %bitcast_convert_fusion = bf16[512,768]{1,0:T(8,128)(2,1)S(1)} fusion(bf16[512,24,256]{2,0,1:T(8,128)(2,1)S(1)} %multiply_convert_fusion, bf16[24,256,768]{2,1,0:T(8,128)(2,1)} %gather_fusion.1), kind=kOutput, calls=%fused_computation.15 | convolution fusion | flops 4832231424 | bytes 16515072 | tf_op jit(solution)/shard_map/rzp,zpc->rc/dot_general | solution.py:88
  312.9 3.5 gather_fusion.4
  316.4 4.9 all-to-all-start.5
  321.3 0.0 copy-done.3
  321.3 10.3 %convolution_convert_fusion = bf16[24,256,768]{2,1,0:T(8,128)(2,1)} fusion(bf16[512,24,256]{2,0,1:T(8,128)(2,1)} %copy-done.5, bf16[513,768]{1,0:T(8,128)(2,1)S(1)} %copy-done.3), kind=kOutput, calls=%fused_computation.13 | convolution fusion | flops 4836556800 | bytes 16515072 | tf_op jit(solution)/shard_map/zbt,zp->btp/dot_general | solution.py:91
  331.6 5.9 broadcast_in_dim.70
  337.5 28.3 %scatter_fusion = bf16[32,256,768]{2,1,0:T(8,128)(2,1)} fusion(bf16[32,256,768]{2,1,0:T(8,128)(2,1)} %broadcast_in_dim.70, s32[24]{0:T(128)S(1)} %fusion.14, bf16[24,256,768]{2,1,0:T(8,128)(2,1)} %convolution_convert_fusion), kind=kCustom, calls=%fused_computation.10 | custom fusion | bytes 28311648 | tf_op jit(solution)/shard_map/scatter | solution.py:97
  365.8 23.6 %copy.52 = bf16[16,2,256,768]{3,1,2,0:T(2,128)(2,1)} copy(bf16[16,2,256,768]{3,2,1,0:T(8,128)(2,1)} %bitcast.76) | data formatting | bytes 25165824 | tf_op jit(solution)/shard_map/reshape | solution.py:100
  389.4 0.0 all-to-all-done.5
  389.4 17.0 %all-to-all-start.6 = ((bf16[16,2,256,768]{3,1,2,0:T(2,128)(2,1)}), bf16[16,2,256,768]{3,1,2,0:T(2,128)(2,1)}, u32[]{:S(2)}, u32[]{:S(2)}) async-start(bf16[16,2,256,768]{3,1,2,0:T(2,128)(2,1)} %copy.52), calls=%async_computation.6 | async-start | bytes 25165824 | tf_op jit(solution)/shard_map/all_to_all | solution.py:99
  406.4 0.7 reduce.11
  407.1 0.1 eq.81
  407.2 2.7 gather_fusion.5
  409.9 214.7 %all-to-all-done.6 = bf16[16,2,256,768]{3,1,2,0:T(2,128)(2,1)} async-done(((bf16[16,2,256,768]{3,1,2,0:T(2,128)(2,1)}), bf16[16,2,256,768]{3,1,2,0:T(2,128)(2,1)}, u32[]{:S(2)}, u32[]{:S(2)}) %all-to-all-start.6) | async-done | bytes 12582944 | tf_op jit(solution)/shard_map/all_to_all | solution.py:99
  624.6 15.6 %copy.53 = bf16[16,2,256,768]{3,1,0,2:T(2,128)(2,1)} copy(bf16[16,2,256,768]{3,1,2,0:T(2,128)(2,1)} %all-to-all-done.6) | data formatting | bytes 25165824 | tf_op jit(solution)/shard_map/all_to_all | solution.py:99
  640.2 26.2 %reshape.277 = bf16[32,256,768]{2,0,1:T(8,128)(2,1)} reshape(bf16[16,2,256,768]{3,1,0,2:T(2,128)(2,1)} %copy.53) | data formatting | bytes 25165824 | tf_op jit(solution)/shard_map/reshape | solution.py:113
  666.4 6.4 convolution_convert_fusion.1
  672.8 4.8 copy.54
  (23 shorter events, 0.2 us)
Async XLA Ops:
  0.6 24.7 %copy-start = (bf16[16,256]{1,0:T(8,128)(2,1)S(1)}, bf16[16,256]{1,0:T(8,128)(2,1)}, u32[]{:S(2)}) copy-start(bf16[16,256]{1,0:T(8,128)(2,1)} %param.9) | copy-start | bytes 24580
  3.6 14.9 %all-to-all-start.2 = ((s32[16,1,2]{2,1,0:T(1,128)}), s32[16,1,2]{2,1,0:T(1,128)S(1)}, u32[]{:S(2)}, u32[]{:S(2)}) async-start(s32[16,1,2]{2,1,0:T(1,128)} %bitcast.10), calls=%async_computation.2 | async-start | bytes 16384 | tf_op jit(solution)/shard_map/all_to_all | solution.py:65
  18.6 10.9 %all-to-all-start = ((s32[8,1,96]{2,1,0:T(1,128)}), s32[8,1,96]{2,1,0:T(1,128)S(1)}, u32[]{:S(2)}, u32[]{:S(2)}) async-start(s32[8,1,96]{2,1,0:T(1,128)} %all_to_all.33), calls=%async_computation | async-start | bytes 8192 | tf_op jit(solution)/shard_map/all_to_all | solution.py:45
  29.5 11.2 %all-to-all-start.4 = ((bf16[16,2,256]{2,1,0:T(2,128)(2,1)}), bf16[16,2,256]{2,1,0:T(2,128)(2,1)S(1)}, u32[]{:S(2)}, u32[]{:S(2)}) async-start(bf16[16,2,256]{2,1,0:T(2,128)(2,1)} %broadcast_select_fusion), calls=%async_computation.4 | async-start | bytes 32768 | tf_op jit(solution)/shard_map/all_to_all | solution.py:72
  40.7 22.1 %all-to-all-start.1 = ((bf16[8,96,768]{2,1,0:T(8,128)(2,1)}), bf16[8,96,768]{2,1,0:T(8,128)(2,1)S(1)}, u32[]{:S(2)}, u32[]{:S(2)}) async-start(bf16[8,96,768]{2,1,0:T(8,128)(2,1)} %bitcast.3), calls=%async_computation.1 | async-start | bytes 2359296 | tf_op jit(solution)/shard_map/all_to_all | solution.py:38
  62.8 1.0 copy-start.2
  62.8 6.1 copy-start.4
  63.8 218.4 %all-to-all-start.3 = ((bf16[16,2,256,768]{3,2,1,0:T(8,128)(2,1)}), bf16[16,2,256,768]{3,2,1,0:T(8,128)(2,1)}, u32[]{:S(2)}, u32[]{:S(2)}) async-start(bf16[16,2,256,768]{3,2,1,0:T(8,128)(2,1)} %bitcast.77), calls=%async_computation.3 | async-start | bytes 25165824 | tf_op jit(solution)/shard_map/all_to_all | solution.py:71
  302.6 2.7 copy-start.5
  312.9 8.4 %copy-start.3 = (bf16[513,768]{1,0:T(8,128)(2,1)S(1)}, bf16[513,768]{1,0:T(8,128)(2,1)}, u32[]{:S(2)}) copy-start(bf16[513,768]{1,0:T(8,128)(2,1)} %scatter_custom_fusion.2) | copy-start | bytes 2363908
  316.4 73.0 %all-to-all-start.5 = ((bf16[8,96,768]{2,1,0:T(8,128)(2,1)}), bf16[8,96,768]{2,1,0:T(8,128)(2,1)S(1)}, u32[]{:S(2)}, u32[]{:S(2)}) async-start(bf16[8,96,768]{2,1,0:T(8,128)(2,1)} %bitcast.17), calls=%async_computation.5 | async-start | bytes 2359296 | tf_op jit(solution)/shard_map/all_to_all | solution.py:117
  389.4 235.2 %all-to-all-start.6 = ((bf16[16,2,256,768]{3,1,2,0:T(2,128)(2,1)}), bf16[16,2,256,768]{3,1,2,0:T(2,128)(2,1)}, u32[]{:S(2)}, u32[]{:S(2)}) async-start(bf16[16,2,256,768]{3,1,2,0:T(2,128)(2,1)} %copy.52), calls=%async_computation.6 | async-start | bytes 25165824 | tf_op jit(solution)/shard_map/all_to_all | solution.py:99
  666.4 11.3 %copy-start.1 = (bf16[16,256]{1,0:T(8,128)(2,1)S(1)}, bf16[16,256]{1,0:T(8,128)(2,1)}, u32[]{:S(2)}) copy-start(bf16[16,256]{1,0:T(8,128)(2,1)} %param.9) | copy-start | bytes 24580
where the time goes:
time: 681 us; the launch traced here: 678 us
  waiting for transfers between devices  416 us (61%)
  local copies, waits for them, and re-layouts  153 us (22%)
  starting transfers between devices  52.3 us (8%)
  matrix products  34.3 us (5%)
  other arithmetic  21 us (3%)
    all_to_all x1, waiting for transfers between devices, shards(): lax.all_to_all(returned.reshape(owners, CAP, lane_count, feature_width),...  215 us
    all_to_all x1, waiting for transfers between devices, shards(): lax.all_to_all(packed, 'label', split_axis=0, concat_axis=0, tiled=True)  189 us
    scatter x1, local copies, waits for them, and re-layouts, shards(): returned = jnp.zeros((owners * CAP, lane_count, feature_width), jnp.bfloa...  28.3 us
    reshape x1, local copies, waits for them, and re-layouts, shards(): received.reshape(owners * CAP, lane_count, feature_width)  26.2 us
    reshape x1, local copies, waits for them, and re-layouts, shards(): returned.reshape(owners, CAP, lane_count, feature_width)  23.6 us
    all_to_all x1, starting transfers between devices, shards(): lax.all_to_all(returned.reshape(owners, CAP, lane_count, feature_width),...  17 us
    all_to_all x1, local copies, waits for them, and re-layouts, shards(): lax.all_to_all(returned.reshape(owners, CAP, lane_count, feature_width),...  15.6 us
    reduce_or x1, other arithmetic, label_hits(): jnp.any(batch_pos[:, :, None, None] == label_ids[None, None, :, :], axis=1)  15.2 us
  transfers between devices with their start and end apart: 7, of which 6 were waited for; matrix products, arithmetic and copies ran while one was open for 17% of the time, Pallas kernels for 0%

commit v1 on v0

v1 whole, which is shorter than its diff:
```python
import functools
import jax
import jax.numpy as jnp
from jax import lax
from jax.experimental import pallas as pl
from jax.experimental.pallas import tpu as pltpu
from jax.sharding import PartitionSpec as P

CAP = 2
CODE = 16
BF = jnp.bfloat16
F32 = jnp.float32


def iota(shape, axis):
    return lax.broadcasted_iota(jnp.int32, shape, axis)


def dot(a, b, dims):
    return lax.dot_general(a, b, (dims, ((), ())), preferred_element_type=F32)


NN = ((1,), (0,))
NT = ((1,), (1,))
TN = ((0,), (0,))


def params(limit):
    return pltpu.CompilerParams(vmem_limit_bytes=limit)


def pack_body(groups, slots, x_ref, dest_ref, out_ref, rank_ref):
    rows = x_ref.shape[0]
    dest = dest_ref[...]
    target = dest // rows
    place = dest % rows
    member = jnp.where(iota((16, rows), 0) == target, 1.0, 0.0)
    earlier = jnp.where(iota((rows, rows), 0) < iota((rows, rows), 1), 1.0, 0.0).astype(BF)
    rank = jnp.sum(dot(member.astype(BF), earlier, NN) * member, axis=0, keepdims=True)
    rank = rank.astype(jnp.int32)
    rank_ref[...] = rank + target * slots
    kind = iota((CODE, rows), 0)
    code = jnp.where(kind == 0, place // 16, jnp.where(kind == 1, place % 16, 1))
    code = code.astype(F32).astype(BF)
    out_ref[:, slots:, :] = jnp.zeros((groups, CODE, x_ref.shape[1]), BF)
    for t in range(groups):
        pick = jnp.where(iota((slots, rows), 0) == jnp.where(target == t, rank, -1), 1.0, 0.0).astype(BF)
        out_ref[t, :slots, :] = dot(pick, x_ref[...], NN).astype(BF)
        out_ref[t, slots:, :slots] = dot(code, pick, NT).astype(BF)


def pack(x, dest, groups, slots):
    rows, width = x.shape
    return pl.pallas_call(
        functools.partial(pack_body, groups, slots),
        out_shape=(
            jax.ShapeDtypeStruct((groups, slots + CODE, width), BF),
            jax.ShapeDtypeStruct((1, rows), jnp.int32),
        ),
        compiler_params=params(32 << 20),
        name="pack_rows",
    )(x, dest)


def places(coded, slots):
    code = coded[:, :slots].astype(F32)
    place = (code[0:1] * 16.0 + code[1:2]).astype(jnp.int32)
    return jnp.where(code[2:3] > 0.5, place, -1)


def land_body(groups, slots, arrived_ref, code_ref, out_ref, place_ref):
    rows = out_ref.shape[0] - CODE
    total = jnp.zeros((rows, out_ref.shape[1]), F32)
    for s in range(groups):
        place = places(arrived_ref[s, slots:, :], slots)
        place_ref[s : s + 1, :] = place
        put = jnp.where(iota((rows, slots), 0) == place, 1.0, 0.0).astype(BF)
        total += dot(put, arrived_ref[s, :slots, :], NN)
    out_ref[:rows, :] = total.astype(BF)
    out_ref[rows:, :] = code_ref[...]


def land(arrived, code, rows, slots):
    groups, _, width = arrived.shape
    return pl.pallas_call(
        functools.partial(land_body, groups, slots),
        out_shape=(
            jax.ShapeDtypeStruct((rows + CODE, width), BF),
            jax.ShapeDtypeStruct((groups, slots), jnp.int32),
        ),
        compiler_params=params(32 << 20),
        name="land_rows",
    )(arrived, code)


def leave_body(groups, slots, grad_ref, place_ref, out_ref):
    rows = grad_ref.shape[0]
    for s in range(groups):
        put = jnp.where(iota((rows, slots), 0) == place_ref[s : s + 1, :], 1.0, 0.0).astype(BF)
        out_ref[s] = dot(put, grad_ref[...], TN).astype(BF)


def leave(grad, place):
    groups, slots = place.shape
    return pl.pallas_call(
        functools.partial(leave_body, groups, slots),
        out_shape=jax.ShapeDtypeStruct((groups, slots, grad.shape[1]), BF),
        compiler_params=params(32 << 20),
        name="leave_rows",
    )(grad, place)


def home_body(groups, slots, back_ref, rank_ref, out_ref):
    rows = out_ref.shape[0]
    total = jnp.zeros(out_ref.shape, F32)
    for t in range(groups):
        pick = jnp.where(iota((slots, rows), 0) + t * slots == rank_ref[...], 1.0, 0.0).astype(BF)
        total += dot(pick, back_ref[t], TN)
    out_ref[...] = total.astype(BF)


def home(back, rank):
    groups, slots, width = back.shape
    return pl.pallas_call(
        functools.partial(home_body, groups, slots),
        out_shape=jax.ShapeDtypeStruct((rank.shape[1], width), BF),
        compiler_params=params(32 << 20),
        name="home_rows",
    )(back, rank)


def work_body(table_ref, x_ref, w_ref, scale_ref, part_ref, grad_ref, total_ref, lane_scale_ref):
    b = pl.program_id(0)
    count, lanes, width = w_ref.shape
    rows = part_ref.shape[1]

    @pl.when(b == 0)
    def _():
        total_ref[...] = jnp.zeros(total_ref.shape, F32)
        columns = jnp.transpose(scale_ref[...].astype(F32))
        for p in range(count):
            lane_scale_ref[p] = jnp.broadcast_to(columns[:, p : p + 1], (lanes, 128))

    x = x_ref[0, :rows, :]
    code = x_ref[0, rows:, :rows].astype(F32).astype(jnp.int32)

    def one(c):
        slot = table_ref[b, 2 * c]
        panel = table_ref[b, 2 * c + 1]
        w = w_ref[panel]
        scale = jnp.concatenate([lane_scale_ref[panel]] * (rows // 128), axis=1)
        score = dot(w, x, NT) * scale
        lane = iota((lanes, rows), 0)
        hit = lane == jnp.where(code[0:1] == slot, code[4:5], -1)
        for k in range(1, 4):
            hit |= lane == jnp.where(code[k : k + 1] == slot, code[4 + k : 5 + k], -1)
        signal = ((jax.nn.sigmoid(score) - jnp.where(hit, 1.0, 0.0)) * scale).astype(BF)
        total_ref[panel] += dot(signal, x, NN)
        return dot(signal, w, TN)

    first = table_ref[b, 0] >= 0
    second = table_ref[b, 2] >= 0

    @pl.when(jnp.logical_not(first))
    def _():
        part_ref[...] = jnp.zeros(part_ref.shape, BF)

    @pl.when(first & jnp.logical_not(second))
    def _():
        part_ref[0] = one(0).astype(BF)

    @pl.when(second)
    def _():
        part_ref[0] = (one(0) + one(1)).astype(BF)

    @pl.when(b == pl.num_programs(0) - 1)
    def _():
        grad_ref[...] = total_ref[...].astype(BF)


def work(table, x, panels, scales):
    batches, long_rows, width = x.shape
    rows = long_rows - CODE
    count, lanes, _ = panels.shape
    once = pl.Buffered(1)
    return pl.pallas_call(
        work_body,
        grid_spec=pltpu.PrefetchScalarGridSpec(
            num_scalar_prefetch=1,
            grid=(batches,),
            in_specs=[
                pl.BlockSpec((1, long_rows, width), lambda b, t: (b, 0, 0)),
                pl.BlockSpec((count, lanes, width), lambda b, t: (0, 0, 0), pipeline_mode=once),
                pl.BlockSpec((count, lanes), lambda b, t: (0, 0)),
            ],
            out_specs=[
                pl.BlockSpec((1, rows, width), lambda b, t: (b, 0, 0)),
                pl.BlockSpec((count, lanes, width), lambda b, t: (0, 0, 0)),
            ],
            scratch_shapes=[
                pltpu.VMEM((count, lanes, width), F32),
                pltpu.VMEM((count, lanes, 128), F32),
            ],
        ),
        out_shape=(
            jax.ShapeDtypeStruct((batches, rows, width), BF),
            jax.ShapeDtypeStruct(panels.shape, BF),
        ),
        compiler_params=params(58 << 20),
        name="owner_work",
    )(table, x, panels, scales)


def shards(queries, cluster_dest, panels, scales, shortlist, positives):
    rows, width = queries.shape
    count, lanes = scales.shape
    groups = lax.axis_size("dp")
    owners = lax.axis_size("label")
    slots = 3 * rows // (2 * groups)

    wanted = shortlist[0]
    slot_total = wanted.shape[0]
    slot_ids = jnp.arange(slot_total, dtype=jnp.int32)[None, :]
    mine = (wanted // count)[None, :] == jnp.arange(owners, dtype=jnp.int32)[:, None]
    first = jnp.min(jnp.where(mine, slot_ids, slot_total), axis=1, keepdims=True)
    last = jnp.max(jnp.where(mine, slot_ids, -1), axis=1, keepdims=True)
    local = (wanted % count)[None, :]
    first_panel = jnp.max(jnp.where(slot_ids == first, local, -1), axis=1, keepdims=True)
    last_panel = jnp.max(jnp.where(slot_ids == last, local, -1), axis=1, keepdims=True)
    none = first_panel < 0
    single = last == first
    request = jnp.concatenate(
        [
            jnp.where(none, -1, first),
            first_panel,
            jnp.where(none | single, -1, last),
            jnp.where(none | single, -1, last_panel),
        ],
        axis=1,
    )
    table = lax.all_to_all(request, "label", split_axis=0, concat_axis=0, tiled=True)

    marks = positives.T
    code = jnp.concatenate([marks // lanes, marks % lanes], axis=0).astype(F32).astype(BF)
    code = jnp.pad(code, ((0, CODE - code.shape[0]), (0, width - rows)))

    outgoing, rank = pack(queries, cluster_dest.reshape(1, rows), groups, slots)
    arrived = lax.all_to_all(outgoing, "dp", split_axis=0, concat_axis=0, tiled=True)
    batch, place = land(arrived, code, rows, slots)
    gathered = lax.all_gather(batch, "label")
    part, panel_grad = work(table, gathered, panels, scales)
    grad = lax.psum_scatter(part, "label", scatter_dimension=0, tiled=False)
    back = lax.all_to_all(leave(grad, place), "dp", split_axis=0, concat_axis=0, tiled=True)
    return home(back, rank), panel_grad


def solution(mesh):
    placed = (
        P(("dp", "label"), None),
        P(("dp", "label")),
        P(("dp", "label"), None, None),
        P(("dp", "label"), None),
        P(("dp", "label"), None),
        P(("dp", "label"), None),
    )
    return jax.shard_map(
        shards,
        mesh=mesh,
        in_specs=placed,
        out_specs=(P(("dp", "label"), None), P(("dp", "label"), None, None)),
        check_vma=False,
    )
```

time: 681 us -> 301 us (0.44)
  waiting for transfers between devices: 416 us -> 189 us
  local copies, waits for them, and re-layouts: 153 us -> 3.03 us
  Pallas kernels: 0 us -> 50.8 us
  starting transfers between devices: 52.3 us -> 5.84 us
  blocking collectives: 0 us -> 35.6 us
  matrix products: 34.3 us -> 0 us
  other arithmetic: 21 us -> 1.72 us
  between operations: 0.87 us -> 14.1 us
    all_to_all x7 -> x1, waiting for transfers between devices: 416 us -> 17.9 us  [shards(): lax.all_to_all(outgoing, 'dp', split_axis=0, concat_axis=0, tiled=True)]
    unnamed x0 -> x3, waiting for transfers between devices: none -> 93.8 us
    all_gather x0 -> x1, waiting for transfers between devices: none -> 77.7 us  [shards(): gathered = lax.all_gather(batch, 'label')]
    pallas_call x0 -> x5, Pallas kernels: none -> 50.8 us  [the longest x1 41.7 us: work(): pl.pallas_call(work_body, grid_spec=pltpu.PrefetchScalarGridSpec(num_scal...]
    reshape x3 -> x0, local copies, waits for them, and re-layouts: 49.8 us -> none  [the longest x1 26.2 us: shards(): received.reshape(owners * CAP, lane_count, feature_width)]
    all_to_all x7 -> x1, starting transfers between devices: 52.3 us -> 5.8 us  [shards(): lax.all_to_all(outgoing, 'dp', split_axis=0, concat_axis=0, tiled=True)]
    scatter x5 -> x0, local copies, waits for them, and re-layouts: 42.8 us -> none  [the longest x1 28.3 us: shards(): returned = jnp.zeros((owners * CAP, lane_count, feature_width), jnp.bfloa...]
    all_to_all x0 -> x2, blocking collectives: none -> 35.6 us  [the longest x1 21.6 us: shards(): lax.all_to_all(leave(grad, place), 'dp', split_axis=0, concat_axis=0, til...]
  transfers between devices with their start and end apart: 7 -> 3, of which waited for: 6 -> 3; matrix products, arithmetic and copies ran while one was open for 17% -> 1% of each run, Pallas kernels for 0% -> 0%
where the time goes in v1:
time: 301 us; the launch traced here: 300 us
  waiting for transfers between devices  189 us (63%)
  Pallas kernels  50.8 us (17%)
  blocking collectives  35.6 us (12%)
  between operations  14.1 us (5%)
  starting transfers between devices  5.84 us (2%)
  local copies, waits for them, and re-layouts  3.03 us (1%)
    unnamed x3, waiting for transfers between devices  93.8 us
    all_gather x1, waiting for transfers between devices, shards(): gathered = lax.all_gather(batch, 'label')  77.7 us
    pallas_call x1, Pallas kernels, work(): pl.pallas_call(work_body, grid_spec=pltpu.PrefetchScalarGridSpec(num_scal...  41.7 us
    all_to_all x1, blocking collectives, shards(): lax.all_to_all(leave(grad, place), 'dp', split_axis=0, concat_axis=0, til...  21.6 us
    all_to_all x1, waiting for transfers between devices, shards(): lax.all_to_all(outgoing, 'dp', split_axis=0, concat_axis=0, tiled=True)  17.9 us
    all_to_all x1, blocking collectives, shards(): lax.all_to_all(request, 'label', split_axis=0, concat_axis=0, tiled=True)  14.1 us
  transfers between devices with their start and end apart: 3, of which 3 were waited for; matrix products, arithmetic and copies ran while one was open for 1% of the time, Pallas kernels for 0%

profile of v1, /device:TPU:1, one launch (start us, length us, event | category | flops | bytes accessed | tf_op | source)
XLA Modules:
  0.0 300.4 jit_solution(7118346131191515556)
XLA Ops:
  7.2 0.0 copy-start
  7.2 1.1 copy-done
  8.3 0.0 copy-start.2
  8.3 0.7 copy-done.2
  9.0 2.5 pack_rows.1
  11.5 5.8 %all-to-all-start.1 = ((bf16[8,112,768]{2,1,0:T(8,128)(2,1)}), bf16[8,112,768]{2,1,0:T(8,128)(2,1)S(1)}, u32[]{:S(2)}, u32[]{:S(2)}) async-start(bf16[8,112,768]{2,1,0:T(8,128)(2,1)} %get-tuple-element.8), calls=%async_computation.1 | async-start | bytes 2752512 | tf_op jit(solution)/shard_map/all_to_all | solution.py:248
  17.3 0.0 all-gather.3.cloned.1.call-start
  17.3 0.7 add_select_fusion.1
  18.1 17.9 %all-to-all-done.1.arrived_ref = bf16[8,112,768]{2,1,0:T(8,128)(2,1)S(1)} async-done(((bf16[8,112,768]{2,1,0:T(8,128)(2,1)}), bf16[8,112,768]{2,1,0:T(8,128)(2,1)S(1)}, u32[]{:S(2)}, u32[]{:S(2)}) %all-to-all-start.1) | async-done | bytes 1376288 | tf_op jit(solution)/shard_map/all_to_all | solution.py:248
  35.9 2.7 land_rows.1
  38.6 0.0 all-gather.3.cloned.1.call-update
  38.6 0.0 reduce-scatter.4.cloned.1.call-start
  38.7 0.7 fusion.4
  39.3 0.1 select_reduce_fusion.3
  39.5 0.2 select_reduce_fusion.2
  39.7 0.1 copy.12
  39.8 14.1 %all_to_all.21 = s32[16,1,4]{2,1,0:T(1,128)} all-to-all(s32[16,1,4]{2,1,0:T(1,128)S(1)} %copy.12), channel_id=1, replica_groups=mesh['dp'=8,'label'=16] {'label'}, dimensions={0} | all-to-all | bytes 512 | tf_op jit(solution)/shard_map/all_to_all | solution.py:241
  53.8 77.7 %all-gather.3.cloned.1.call-done = bf16[8448,768]{1,0:T(8,128)(2,1)} async-done(((bf16[528,768]{1,0:T(8,128)(2,1)}), bf16[8448,768]{1,0:T(8,128)(2,1)}) %all-gather.3.cloned.1.call-update) | async-done | bytes 12976144 | tf_op jit(solution)/shard_map/all_gather | solution.py:250
  131.5 41.7 %owner_work.1 = (bf16[16,512,768]{2,1,0:T(8,128)(2,1)}, bf16[16,256,768]{2,1,0:T(8,128)(2,1)}) custom-call(s32[16,4]{1,0:T(8,128)} %bitcast.59, bf16[16,528,768]{2,1,0:T(8,128)(2,1)} %bitcast.58, bf16[16,256,768]{2,1,0:T(8,128)(2,1)} %w_ref.1, bf16[16,256]{1,0:T(8,128)(2,1)} %scale_ref.1), custom_call_target="tpu_custom_call" | custom-call | tf_op jit(solution)/shard_map/owner_work/pallas_call | solution.py:186
  173.3 0.0 reduce-scatter.4.cloned.1.call-update
  173.3 93.7 %reduce-scatter.4.cloned.1.call-done = bf16[1,512,768]{2,1,0:T(8,128)(2,1)} async-done(((bf16[16,512,768]{2,1,0:T(8,128)(2,1)}), bf16[1,512,768]{2,1,0:T(8,128)(2,1)}) %reduce-scatter.4.cloned.1.call-update) | async-done | bytes 786448
  267.0 0.0 copy-start.1
  267.0 1.1 copy-done.1
  268.2 1.1 leave_rows.1
  269.3 21.6 %all_to_all.22.back_ref = bf16[8,96,768]{2,1,0:T(8,128)(2,1)S(1)} all-to-all(bf16[8,96,768]{2,1,0:T(8,128)(2,1)S(1)} %leave_rows.1), channel_id=1, replica_groups=mesh['dp'=8,'label'=16] {'dp'}, dimensions={0} | all-to-all | bytes 2359296 | tf_op jit(solution)/shard_map/all_to_all | solution.py:253
  290.9 2.7 home_rows.1
  (4 shorter events, 0.0 us)
Async XLA Ops:
  7.2 1.1 copy-start
  8.3 0.7 copy-start.2
  11.5 24.4 %all-to-all-start.1 = ((bf16[8,112,768]{2,1,0:T(8,128)(2,1)}), bf16[8,112,768]{2,1,0:T(8,128)(2,1)S(1)}, u32[]{:S(2)}, u32[]{:S(2)}) async-start(bf16[8,112,768]{2,1,0:T(8,128)(2,1)} %get-tuple-element.8), calls=%async_computation.1 | async-start | bytes 2752512 | tf_op jit(solution)/shard_map/all_to_all | solution.py:248
  17.3 114.2 %all-gather.3.cloned.1.call-start = ((), (), s32[]{:S(2)}) async-start(), calls=%async_computation.4 | async-start | bytes 13787136 | tf_op jit(solution)/shard_map/all_gather | solution.py:250
  38.6 228.4 %reduce-scatter.4.cloned.1.call-start = ((), (), s32[]{:S(2)}) async-start(), calls=%async_computation.5 | async-start | bytes 13369344
  267.0 1.1 copy-start.1
Sparse Core Ops, SparseCore 0:
  38.7 92.7 all-gather.2
  173.4 93.5 reduce-scatter.3

commit v2 on v1

v2 whole, which is shorter than its diff:
```python
import functools
import jax
import jax.numpy as jnp
from jax import lax
from jax.experimental import pallas as pl
from jax.experimental.pallas import tpu as pltpu
from jax.sharding import PartitionSpec as P

CAP = 2
CODE = 16
LIMIT = 60 << 20
BF = jnp.bfloat16
F32 = jnp.float32


def iota(shape, axis):
    return lax.broadcasted_iota(jnp.int32, shape, axis)


def dot(a, b, dims):
    return lax.dot_general(a, b, (dims, ((), ())), preferred_element_type=F32)


NN = ((1,), (0,))
NT = ((1,), (1,))
TN = ((0,), (0,))


def params(limit):
    return pltpu.CompilerParams(vmem_limit_bytes=limit)


def pack_body(groups, slots, x_ref, dest_ref, out_ref, rank_ref):
    rows = x_ref.shape[0]
    dest = dest_ref[...]
    target = dest // rows
    place = dest % rows
    member = jnp.where(iota((16, rows), 0) == target, 1.0, 0.0)
    earlier = jnp.where(iota((rows, rows), 0) < iota((rows, rows), 1), 1.0, 0.0).astype(BF)
    rank = jnp.sum(dot(member.astype(BF), earlier, NN) * member, axis=0, keepdims=True)
    rank = rank.astype(jnp.int32)
    rank_ref[...] = rank + target * slots
    kind = iota((CODE, rows), 0)
    code = jnp.where(kind == 0, place // 16, jnp.where(kind == 1, place % 16, 1))
    code = code.astype(F32).astype(BF)
    out_ref[:, slots:, :] = jnp.zeros((groups, CODE, x_ref.shape[1]), BF)
    for t in range(groups):
        pick = jnp.where(iota((slots, rows), 0) == jnp.where(target == t, rank, -1), 1.0, 0.0).astype(BF)
        out_ref[t, :slots, :] = dot(pick, x_ref[...], NN).astype(BF)
        out_ref[t, slots:, :slots] = dot(code, pick, NT).astype(BF)


def pack(x, dest, groups, slots):
    rows, width = x.shape
    return pl.pallas_call(
        functools.partial(pack_body, groups, slots),
        out_shape=(
            jax.ShapeDtypeStruct((groups, slots + CODE, width), BF),
            jax.ShapeDtypeStruct((1, rows), jnp.int32),
        ),
        compiler_params=params(LIMIT),
        name="pack_rows",
    )(x, dest)


def places(coded, slots):
    code = coded[:, :slots].astype(F32)
    place = (code[0:1] * 16.0 + code[1:2]).astype(jnp.int32)
    return jnp.where(code[2:3] > 0.5, place, -1)


def land_body(groups, slots, arrived_ref, place_ref, *pair_refs):
    part = pair_refs[0].shape[1]
    rows = 2 * part * len(pair_refs)
    total = jnp.zeros((rows, arrived_ref.shape[2]), F32)
    for s in range(groups):
        place = places(arrived_ref[s, slots:, :], slots)
        place_ref[s : s + 1, :] = place
        put = jnp.where(iota((rows, slots), 0) == place, 1.0, 0.0).astype(BF)
        total += dot(put, arrived_ref[s, :slots, :], NN)
    for k in range(2 * len(pair_refs)):
        pair_refs[k // 2][k % 2] = total[k * part : (k + 1) * part].astype(BF)


def land(arrived, rows, slots):
    groups, _, width = arrived.shape
    pair = jax.ShapeDtypeStruct((2, rows // STREAMS, width), BF)
    return pl.pallas_call(
        functools.partial(land_body, groups, slots),
        out_shape=(jax.ShapeDtypeStruct((groups, slots), jnp.int32), pair, pair),
        compiler_params=params(LIMIT),
        name="land_rows",
    )(arrived)


def leave_body(groups, slots, terms, *refs):
    place_ref, out_ref = refs[0], refs[-1]
    streams = []
    for k in range(STREAMS):
        total = refs[1 + k * terms][0].astype(F32)
        for ref in refs[2 + k * terms : 1 + (k + 1) * terms]:
            total += ref[0].astype(F32)
        streams.append(total.astype(BF))
    grad = jnp.concatenate(streams, axis=0)
    rows = grad.shape[0]
    for s in range(groups):
        put = jnp.where(iota((rows, slots), 0) == place_ref[s : s + 1, :], 1.0, 0.0).astype(BF)
        out_ref[s] = dot(put, grad, TN).astype(BF)


def one_block(array, index, part):
    _, rows, width = array.shape
    return pl.BlockSpec((1, part, width), lambda i: (index, i, 0))


def leave(place, terms):
    groups, slots = place.shape
    flat = [term for stream in terms for term in stream]
    width = flat[0][0].shape[2]
    return pl.pallas_call(
        functools.partial(leave_body, groups, slots, len(terms[0])),
        grid=(1,),
        in_specs=[pl.BlockSpec((groups, slots), lambda i: (0, 0))]
        + [one_block(a, index, a.shape[1]) for a, index in flat],
        out_specs=pl.BlockSpec((groups, slots, width), lambda i: (0, 0, 0)),
        out_shape=jax.ShapeDtypeStruct((groups, slots, width), BF),
        compiler_params=params(LIMIT),
        name="leave_rows",
    )(place, *[a for a, _ in flat])


def merge_body(sums, *refs):
    outs = refs[-STREAMS:]
    at = 0
    for k, blocks in enumerate(sums):
        for j, terms in enumerate(blocks):
            total = refs[at][0].astype(F32)
            for ref in refs[at + 1 : at + len(terms)]:
                total += ref[0].astype(F32)
            outs[k][j] = total.astype(BF)
            at += len(terms)


def merge(sums, name):
    flat = [term for blocks in sums for terms in blocks for term in terms]
    _, rows, width = flat[0][0].shape
    count = len(sums[0])
    steps = 2
    part = rows // steps
    return pl.pallas_call(
        functools.partial(merge_body, [[[0] * len(t) for t in b] for b in sums]),
        grid=(steps,),
        in_specs=[one_block(a, index, part) for a, index in flat],
        out_specs=[pl.BlockSpec((count, part, width), lambda i: (0, i, 0))] * STREAMS,
        out_shape=[jax.ShapeDtypeStruct((count, rows, width), BF)] * STREAMS,
        compiler_params=params(LIMIT),
        cost_estimate=pl.CostEstimate(
            flops=0, transcendentals=0, bytes_accessed=2 * rows * width * (len(flat) + count * STREAMS)
        ),
        name=name,
    )(*[a for a, _ in flat])


def home_body(groups, slots, back_ref, rank_ref, out_ref):
    rows = out_ref.shape[0]
    total = jnp.zeros(out_ref.shape, F32)
    for t in range(groups):
        pick = jnp.where(iota((slots, rows), 0) + t * slots == rank_ref[...], 1.0, 0.0).astype(BF)
        total += dot(pick, back_ref[t], TN)
    out_ref[...] = total.astype(BF)


def home(back, rank):
    groups, slots, width = back.shape
    return pl.pallas_call(
        functools.partial(home_body, groups, slots),
        out_shape=jax.ShapeDtypeStruct((rank.shape[1], width), BF),
        compiler_params=params(LIMIT),
        name="home_rows",
    )(back, rank)


def work_body(units, n_in, n_out, *refs):
    table_ref, meta_ref, code_ref, w_hbm, scale_ref = refs[:5]
    x_refs = refs[5 : 5 + n_in]
    out_refs = refs[5 + n_in : 5 + n_in + n_out]
    signal_ref = refs[5 + n_in + n_out]
    scratch = refs[6 + n_in + n_out :]
    x_buf, out_buf, signal_buf, w_ref, lane_scale_ref, ready_ref, in_sem, out_sem, signal_sem, w_sem = scratch
    total = len(units)
    count, lanes, width = w_ref.shape
    rows = x_buf.shape[1]
    part = rows // 2

    def store(u):
        copies = [pltpu.make_async_copy(signal_buf.at[u], signal_ref.at[u], signal_sem.at[u])]
        for h, (array, block) in enumerate(units[u][1]):
            cut = out_buf.at[u, pl.ds(h * part, part)]
            copies.append(pltpu.make_async_copy(cut, out_refs[array].at[block], out_sem.at[2 * u + h]))
        return copies

    def fetch(u):
        for h, (array, index) in enumerate(units[u][0]):
            cut = x_buf.at[u, pl.ds(h * part, part)]
            pltpu.make_async_copy(x_refs[array].at[index], cut, in_sem.at[u]).start()

    def panel_copy(p):
        return pltpu.make_async_copy(w_hbm.at[p], w_ref.at[p], w_sem.at[p])

    fetch(0)
    for p in range(count):
        panel_copy(p).start()
        ready_ref[p] = 0
    for u in range(1, total):
        fetch(u)
    columns = jnp.transpose(scale_ref[...].astype(F32))
    for p in range(count):
        lane_scale_ref[p] = jnp.broadcast_to(columns[:, p : p + 1], (lanes, 128))

    def need(panel):
        @pl.when(ready_ref[panel] == 0)
        def _():
            panel_copy(panel).wait()
            ready_ref[panel] = 1

    def unit(u, carry):
        pltpu.make_async_copy(x_buf.at[u], x_buf.at[u], in_sem.at[u]).wait()
        batch = meta_ref[0, u]
        x = x_buf[u]
        code = code_ref[batch, meta_ref[1, u]].astype(F32).astype(jnp.int32)

        def one(c):
            slot = table_ref[batch, 2 * c]
            panel = table_ref[batch, 2 * c + 1]
            w = w_ref[panel]
            scale = jnp.concatenate([lane_scale_ref[panel]] * (rows // 128), axis=1)
            score = dot(w, x, NT) * scale
            lane = iota((lanes, rows), 0)
            hit = lane == jnp.where(code[0:1] == slot, code[4:5], -1)
            for k in range(1, 4):
                hit |= lane == jnp.where(code[k : k + 1] == slot, code[4 + k : 5 + k], -1)
            signal = ((jax.nn.sigmoid(score) - jnp.where(hit, 1.0, 0.0)) * scale).astype(BF)
            signal_buf[u, c] = signal
            return dot(signal, w, TN)

        first = table_ref[batch, 0] >= 0
        second = table_ref[batch, 2] >= 0

        @pl.when(jnp.logical_not(first))
        def _():
            out_buf[u] = jnp.zeros((rows, width), BF)

        @pl.when(first & jnp.logical_not(second))
        def _():
            need(table_ref[batch, 1])
            out_buf[u] = one(0).astype(BF)

        @pl.when(second)
        def _():
            need(table_ref[batch, 1])
            need(table_ref[batch, 3])
            out_buf[u] = (one(0) + one(1)).astype(BF)

        for v in range(total):

            @pl.when(u == v)
            def _():
                for copy in store(v):
                    copy.start()

        return carry

    lax.fori_loop(0, total, unit, 0)
    for p in range(count):
        need(p)
    for u in range(total):
        for copy in store(u):
            copy.wait()


def work(table, batches, codes, panels, scales, arrays, units, out_blocks, name):
    count, lanes, width = panels.shape
    part = codes.shape[3] // 2
    rows = 2 * part
    meta = jnp.stack([batches, jnp.array([u[2] for u in units], jnp.int32)])
    total = len(units)
    whole = pl.BlockSpec(memory_space=pltpu.VMEM)
    scalar = pl.BlockSpec(memory_space=pltpu.SMEM)
    loose = pl.BlockSpec(memory_space=pltpu.HBM)
    outs = pl.pallas_call(
        functools.partial(work_body, units, len(arrays), len(out_blocks)),
        in_specs=[scalar, scalar, whole, loose, whole] + [loose] * len(arrays),
        out_specs=[loose] * len(out_blocks) + [loose],
        out_shape=[jax.ShapeDtypeStruct((n, part, width), BF) for n in out_blocks]
        + [jax.ShapeDtypeStruct((total, CAP, lanes, rows), BF)],
        scratch_shapes=[
            pltpu.VMEM((total, rows, width), BF),
            pltpu.VMEM((total, rows, width), BF),
            pltpu.VMEM((total, CAP, lanes, rows), BF),
            pltpu.VMEM(panels.shape, BF),
            pltpu.VMEM((count, lanes, 128), F32),
            pltpu.SMEM((count,), jnp.int32),
            pltpu.SemaphoreType.DMA((total,)),
            pltpu.SemaphoreType.DMA((2 * total,)),
            pltpu.SemaphoreType.DMA((total,)),
            pltpu.SemaphoreType.DMA((count,)),
        ],
        compiler_params=params(LIMIT),
        cost_estimate=pl.CostEstimate(
            flops=total * 3 * lanes * rows * width * 4,
            transcendentals=0,
            bytes_accessed=panels.size * 2 + total * rows * (width * 4 + lanes * 2),
        ),
        name=name,
    )(table, meta, codes, panels, scales, *arrays)
    return outs[:-1], outs[-1]


def panel_body(parts, n_arrays, n_signals, *refs):
    table_ref, batch_ref = refs[:2]
    x_refs = refs[2 : 2 + n_arrays]
    s_refs = refs[2 + n_arrays : 2 + n_arrays + n_signals]
    grad_ref, x_all, s_all, total_ref, x_sem, s_sem = refs[2 + n_arrays + n_signals :]
    rows = x_all.shape[1] // STREAMS
    for rel, pieces in enumerate(parts):
        for pair, (sources, signal, unit) in enumerate(pieces):
            wide = pl.ds(2 * pair * rows, 2 * rows)
            for h, (array, index) in enumerate(sources):
                cut = pl.ds((2 * pair + h) * rows, rows)
                pltpu.make_async_copy(x_refs[array].at[index], x_all.at[rel, cut], x_sem.at[rel]).start()
            pltpu.make_async_copy(s_refs[signal].at[unit], s_all.at[rel, :, :, wide], s_sem.at[rel]).start()
    total_ref[...] = jnp.zeros(total_ref.shape, F32)

    def batch(rel, carry):
        pltpu.make_async_copy(x_all.at[rel], x_all.at[rel], x_sem.at[rel]).wait()
        pltpu.make_async_copy(s_all.at[rel], s_all.at[rel], s_sem.at[rel]).wait()
        for c in range(CAP):
            panel = table_ref[batch_ref[rel], 2 * c + 1]

            @pl.when(panel >= 0)
            def _():
                total_ref[panel] += dot(s_all[rel, c], x_all[rel], NN)

        return carry

    lax.fori_loop(0, len(parts), batch, 0)
    grad_ref[...] = total_ref[...].astype(BF)


def panel_sum(table, batches, arrays, signals, parts, shape):
    count, lanes, width = shape
    rows = arrays[0].shape[2] * STREAMS
    scalar = pl.BlockSpec(memory_space=pltpu.SMEM)
    loose = pl.BlockSpec(memory_space=pltpu.HBM)
    return pl.pallas_call(
        functools.partial(panel_body, parts, len(arrays), len(signals)),
        in_specs=[scalar, scalar] + [loose] * (len(arrays) + len(signals)),
        out_specs=pl.BlockSpec(memory_space=pltpu.VMEM),
        out_shape=jax.ShapeDtypeStruct(shape, BF),
        scratch_shapes=[
            pltpu.VMEM((len(parts), rows, width), BF),
            pltpu.VMEM((len(parts), CAP, lanes, rows), BF),
            pltpu.VMEM(shape, F32),
            pltpu.SemaphoreType.DMA((len(parts),)),
            pltpu.SemaphoreType.DMA((len(parts),)),
        ],
        compiler_params=params(LIMIT),
        cost_estimate=pl.CostEstimate(
            flops=len(parts) * CAP * lanes * rows * width * 2,
            transcendentals=0,
            bytes_accessed=len(parts) * rows * (width + CAP * lanes) * 2 + count * lanes * width * 2,
        ),
        name="panel_grad",
    )(table, batches, *arrays, *signals)


ORDERS = ((1, 3, 4, 12), (3, 1, 12, 4), (4, 12, 1, 3), (12, 4, 3, 1))
STREAMS = len(ORDERS)
RINGS = ((1, 3), (4, 12))


def swap(array, mask, owners):
    return lax.ppermute(array, "label", [(i, i ^ mask) for i in range(owners)])


def shards(queries, cluster_dest, panels, scales, shortlist, positives):
    rows, width = queries.shape
    count, lanes = scales.shape
    groups = lax.axis_size("dp")
    owners = lax.axis_size("label")
    slots = 3 * rows // (2 * groups)
    part = rows // STREAMS
    me = lax.axis_index("label").astype(jnp.int32)

    marks = positives.T
    code = jnp.concatenate([marks // lanes, marks % lanes], axis=0).astype(F32).astype(BF)
    wanted_row = jnp.pad(shortlist.astype(F32).astype(BF), ((0, 0), (0, rows - shortlist.shape[1])))
    code = jnp.concatenate([code, wanted_row, jnp.zeros((CODE - code.shape[0] - 1, rows), BF)], axis=0)
    codes = lax.all_to_all(
        jnp.broadcast_to(code, (owners, *code.shape)), "label", split_axis=0, concat_axis=0, tiled=True
    )
    wanted = codes[:, 8, : shortlist.shape[1]].astype(F32).astype(jnp.int32)
    codes = jnp.transpose(codes.reshape(owners, CODE, STREAMS // 2, 2 * part), (0, 2, 1, 3))
    slot_ids = jnp.arange(wanted.shape[1], dtype=jnp.int32)[None, :]
    mine = wanted // count == me
    local = wanted % count
    first = jnp.min(jnp.where(mine, slot_ids, wanted.shape[1]), axis=1, keepdims=True)
    last = jnp.max(jnp.where(mine, slot_ids, -1), axis=1, keepdims=True)
    first_panel = jnp.max(jnp.where(slot_ids == first, local, -1), axis=1, keepdims=True)
    last_panel = jnp.max(jnp.where(slot_ids == last, local, -1), axis=1, keepdims=True)
    none = first_panel < 0
    single = none | (last == first)
    table = jnp.concatenate(
        [
            jnp.where(none, -1, first),
            first_panel,
            jnp.where(single, -1, last),
            jnp.where(single, -1, last_panel),
        ],
        axis=1,
    )

    outgoing, rank = pack(queries, cluster_dest.reshape(1, rows), groups, slots)
    arrived = lax.all_to_all(outgoing, "dp", split_axis=0, concat_axis=0, tiled=True)
    place, *own = land(arrived, rows, slots)

    every = range(STREAMS)
    order = ORDERS
    arrays = []
    for pair, (one, three) in zip(own, RINGS):
        by1, by3 = swap(pair, one, owners), swap(pair, three, owners)
        low, high = swap(by1[0], three, owners), swap(by3[1], one, owners)
        near = jnp.stack([pair, by1, jnp.stack([low, high]), by3], axis=1)
        arrays.append([near])
    for group, (one, three) in zip(arrays, RINGS[::-1]):
        by1, by3 = swap(group[0], one, owners), swap(group[0], three, owners)
        group += [by1, by3, swap(by1[0], three, owners), swap(by3[1], one, owners)]

    def rel(k, bits):
        out = 0
        for s in range(4):
            if bits >> s & 1:
                out ^= order[k][s]
        return out

    where = {}

    def bits_of(k, r):
        return next(b for b in range(owners) if rel(k, b) == r)

    def stage(name, index, members):
        outs_of, units, ids, used = {}, [], [], []

        def source(array):
            if array not in used:
                used.append(array)
            return used.index(array)

        for pair, far, spot in members:
            r = 4 * far + spot if pair == 0 else 4 * spot + far
            legs = [(k, bits_of(k, r)) for k in (2 * pair, 2 * pair + 1)]
            if far == 2:
                origin = (((pair, 3), spot), ((pair, 4), spot))
            else:
                array = (pair, (0, 1, None, 2)[far])
                origin = ((array, (0, spot)), (array, (1, spot)))
            for k, b in legs:
                outs_of.setdefault((k, b & 1), []).append(b)
            where[pair, r] = (origin, index, len(units))
            units.append((tuple((source(a), i) for a, i in origin), legs, pair))
            ids.append(r)
        keys = sorted(outs_of)
        for key in keys:
            outs_of[key].sort(key=lambda b: (b >> 1 & 1, b))
        units = [
            (origin, tuple((keys.index((k, b & 1)), outs_of[k, b & 1].index(b)) for k, b in legs), pair)
            for origin, legs, pair in units
        ]
        batches = jnp.array(ids, jnp.int32) ^ me
        blocks = [len(outs_of[key]) for key in keys]
        ins = [arrays[pair][a] for pair, a in used]
        outs, signals = work(table, batches, codes, panels, scales, ins, units, blocks, name)
        outs = dict(zip(keys, outs))
        for key in keys:
            for n, b in enumerate(outs_of[key]):
                made[key[0], b] = (outs[key], n)
            if key[1]:
                got = swap(outs[key], order[key[0]][0], owners)
                for n, b in enumerate(outs_of[key]):
                    back[key[0], b ^ 1] = (got, n)
        return signals

    made = {}
    back = {}

    ahead = (1, 2, 3)
    signals = [
        stage("work_near", 0, [(q, 0, p) for p in ahead for q in (0, 1)]),
        stage("work_far", 1, [(q, f, p) for f in (1, 3) for p in ahead for q in (0, 1)]),
        stage("work_last", 2, [(q, 2, p) for p in ahead for q in (0, 1)]),
        stage("work_kept", 3, [(q, f, 0) for f in (0, 1, 3, 2) for q in (0, 1)]),
    ]

    def terms(k, b):
        return [made[k, b], back[k, b]] + [(got, bits.index(b)) for got, bits in later[k] if b in bits]

    later = {k: [] for k in every}
    for step in (1, 2, 3):
        bit = 1 << step
        sent = [b for b in range(owners) if b & bit and not b & (bit - 1)]
        sums = merge([[terms(k, b) for b in sent] for k in every], f"merge_{step}")
        for k in every:
            got = swap(sums[k], order[k][step], owners)
            later[k].append((got, [b ^ bit for b in sent]))
    leaving = leave(place, [terms(k, 0) for k in every])
    returned = lax.all_to_all(leaving, "dp", split_axis=0, concat_axis=0, tiled=True)

    flat = [(pair, a) for pair in (0, 1) for a in range(5)]
    parts = []
    for r in range(owners):
        parts.append([])
        for pair in (0, 1):
            origin, signal, unit = where[pair, r]
            parts[r].append((tuple((flat.index(a), i) for a, i in origin), signal, unit))
    panel_grad = panel_sum(
        table,
        jnp.arange(owners, dtype=jnp.int32) ^ me,
        [arrays[pair][a] for pair, a in flat],
        signals,
        parts,
        panels.shape,
    )
    return home(returned, rank), panel_grad


def solution(mesh):
    placed = (
        P(("dp", "label"), None),
        P(("dp", "label")),
        P(("dp", "label"), None, None),
        P(("dp", "label"), None),
        P(("dp", "label"), None),
        P(("dp", "label"), None),
    )
    return jax.shard_map(
        shards,
        mesh=mesh,
        in_specs=placed,
        out_specs=(P(("dp", "label"), None), P(("dp", "label"), None, None)),
        check_vma=False,
    )
```

time: 301 us -> 260 us (0.86)
  waiting for transfers between devices: 189 us -> 68.2 us
  starting transfers between devices: 5.84 us -> 70.4 us
  Pallas kernels: 50.8 us -> 98.9 us
  blocking collectives: 35.6 us -> 0 us
  between operations: 14.1 us -> 1.23 us
  local copies, waits for them, and re-layouts: 3.03 us -> 15.3 us
    unnamed x3 -> x0, waiting for transfers between devices: 93.8 us -> none
    all_gather x1 -> x0, waiting for transfers between devices: 77.7 us -> none  [shards(): gathered = lax.all_gather(batch, 'label')]
    ppermute x0 -> x40, waiting for transfers between devices: none -> 49.9 us  [swap(): return lax.ppermute(array, 'label', [(i, i ^ mask) for i in range(owners)])]
    pallas_call x2 -> x9, Pallas kernels: 42.9 us -> 87.3 us  [the longest x4 54.1 us: work(): pl.pallas_call(functools.partial(work_body, units, len(arrays), len(out_b...]
    ppermute x0 -> x40, starting transfers between devices: none -> 41.8 us  [swap(): return lax.ppermute(array, 'label', [(i, i ^ mask) for i in range(owners)])]
    all_to_all x2 -> x0, blocking collectives: 35.6 us -> none  [the longest x1 21.6 us: shards(): lax.all_to_all(leave(grad, place), 'dp', split_axis=0, concat_axis=0, til...]
    all_to_all x0 -> x2, starting transfers between devices: none -> 22.7 us  [the longest x1 14.9 us: shards(): lax.all_to_all(leaving, 'dp', split_axis=0, concat_axis=0, tiled=True)]
    squeeze x0 -> x8, local copies, waits for them, and re-layouts: none -> 8.32 us  [the longest x4 8.26 us: shards(): group += [by1, by3, swap(by1[0], three, owners), swap(by3[1], one, owners)]]
  transfers between devices with their start and end apart: 3 -> 43, of which waited for: 3 -> 13; matrix products, arithmetic and copies ran while one was open for 1% -> 5% of each run, Pallas kernels for 0% -> 29%
where the time goes in v2:
time: 260 us; the launch traced here: 257 us
  Pallas kernels  98.9 us (38%)
  starting transfers between devices  70.4 us (27%)
  waiting for transfers between devices  68.2 us (26%)
  local copies, waits for them, and re-layouts  15.3 us (6%)
  other arithmetic  3.2 us (1%)
    pallas_call x4, Pallas kernels, work(): pl.pallas_call(functools.partial(work_body, units, len(arrays), len(out_b...  54.1 us
    ppermute x40, waiting for transfers between devices, swap(): return lax.ppermute(array, 'label', [(i, i ^ mask) for i in range(owners)])  49.9 us
    ppermute x40, starting transfers between devices, swap(): return lax.ppermute(array, 'label', [(i, i ^ mask) for i in range(owners)])  41.8 us
    all_to_all x1, waiting for transfers between devices, shards(): lax.all_to_all(outgoing, 'dp', split_axis=0, concat_axis=0, tiled=True)  18.4 us
    pallas_call x1, Pallas kernels, panel_sum(): pl.pallas_call(functools.partial(panel_body, parts, len(arrays), len(sign...  17.5 us
    all_to_all x1, starting transfers between devices, shards(): lax.all_to_all(leaving, 'dp', split_axis=0, concat_axis=0, tiled=True)  14.9 us
    pallas_call x3, Pallas kernels, merge(): pl.pallas_call(functools.partial(merge_body, [[[0] * len(t) for t in b] f...  11.1 us
    squeeze x4, local copies, waits for them, and re-layouts, shards(): group += [by1, by3, swap(by1[0], three, owners), swap(by3[1], one, owners)]  8.26 us
  transfers between devices with their start and end apart: 43, of which 13 were waited for; matrix products, arithmetic and copies ran while one was open for 5% of the time, Pallas kernels for 29%

profile of v2, /device:TPU:1, one launch (start us, length us, event | category | flops | bytes accessed | tf_op | source)
XLA Modules:
  0.0 257.2 jit_solution(12432028546510870918)
XLA Ops:
  0.6 3.7 %pack_rows.1 = (bf16[8,112,768]{2,1,0:T(8,128)(2,1)}, s32[1,512]{1,0:T(1,128)}) custom-call(bf16[512,768]{1,0:T(8,128)(2,1)} %x_ref.1, s32[1,512]{1,0:T(1,128)} %bitcast.118), custom_call_target="tpu_custom_call" | custom-call | tf_op jit(solution)/shard_map/pack_rows/pallas_call | solution.py:55
  4.3 5.9 %all-to-all-start = ((bf16[8,112,768]{2,1,0:T(8,128)(2,1)}), bf16[8,112,768]{2,1,0:T(8,128)(2,1)S(1)}, u32[]{:S(2)}, u32[]{:S(2)}) async-start(bf16[8,112,768]{2,1,0:T(8,128)(2,1)} %get-tuple-element.51), calls=%async_computation | async-start | bytes 2752512 | tf_op jit(solution)/shard_map/all_to_all | solution.py:424
  10.5 18.4 %all-to-all-done.arrived_ref = bf16[8,112,768]{2,1,0:T(8,128)(2,1)S(1)} async-done(((bf16[8,112,768]{2,1,0:T(8,128)(2,1)}), bf16[8,112,768]{2,1,0:T(8,128)(2,1)S(1)}, u32[]{:S(2)}, u32[]{:S(2)}) %all-to-all-start) | async-done | bytes 1376288 | tf_op jit(solution)/shard_map/all_to_all | solution.py:424
  28.9 0.8 broadcast_in_dim.35
  29.6 7.8 %all-to-all-start.1 = ((bf16[16,16,512]{2,1,0:T(8,128)(2,1)}), bf16[16,16,512]{2,1,0:T(8,128)(2,1)S(1)}, u32[]{:S(2)}, u32[]{:S(2)}) async-start(bf16[16,16,512]{2,1,0:T(8,128)(2,1)} %broadcast_in_dim.35), calls=%async_computation.1 | async-start | bytes 524288 | tf_op jit(solution)/shard_map/all_to_all | solution.py:399
  37.4 3.9 %land_rows.1 = (s32[8,96]{1,0:T(8,128)}, bf16[2,128,768]{2,1,0:T(8,128)(2,1)}, bf16[2,128,768]{2,1,0:T(8,128)(2,1)}) custom-call(bf16[8,112,768]{2,1,0:T(8,128)(2,1)} %copy-done.10), custom_call_target="tpu_custom_call" | custom-call | tf_op jit(solution)/shard_map/land_rows/pallas_call | solution.py:88
  41.4 2.6 collective-permute-start.2
  44.1 2.5 collective-permute-start.6
  46.5 6.8 %collective-permute-done.2 = bf16[2,128,768]{2,1,0:T(8,128)(2,1)S(1)} collective-permute-done((bf16[2,128,768]{2,1,0:T(8,128)(2,1)}, bf16[2,128,768]{2,1,0:T(8,128)(2,1)S(1)}, u32[]{:S(2)}, u32[]{:S(2)}) %collective-permute-start.2) | collective-permute-done | bytes 393248 | tf_op jit(solution)/shard_map/ppermute | solution.py:383
  53.5 1.3 collective-permute-start.1
  54.8 1.3 collective-permute-start.7
  56.1 1.9 collective-permute-start.5
  58.3 1.0 collective-permute-done.1
  59.6 1.0 collective-permute-start.8
  60.5 0.6 pad_add_fusion.4.refs_1_
  61.1 0.6 pad_add_fusion.1
  61.7 1.8 collective-permute-start.10
  64.0 2.1 collective-permute-start.11
  66.3 0.7 copy.44.refs_0_
  67.0 0.7 copy.51
  67.8 11.4 %work_near.1 = (bf16[1,128,768]{2,1,0:T(8,128)(2,1)}, bf16[2,128,768]{2,1,0:T(8,128)(2,1)}, bf16[1,128,768]{2,1,0:T(8,128)(2,1)}, bf16[2,128,768]{2,1,0:T(8,128)...) custom-call(s32[16,4]{1,0:T(8,128)} %copy.44.refs_0_, ...), custom_call_target="tpu_custom_call" | custom-call | flops 3623878656 | bytes 11796480 | tf_op jit(solution)/shard_map/work_near/pallas_call | solution.py:290
  79.3 13.7 %collective-permute-done.8.refs_7_.refs_5_.refs_3_ = bf16[2,4,128,768]{3,2,1,0:T(8,128)(2,1)} collective-permute-done((bf16[2,4,128,768]{3,2,1,0:T(8,128)(2,1)S(1)}, bf16[2,4,128,768]{3,2,1,0:T(8,128)(2,1)}, u32[]{:S(2)}, u32[]{:S(2)}) %collective-permute-start.8) | collective-permute-done | bytes 1572896 | tf_op jit(solution)/shard_map/ppermute | solution.py:383
  93.0 1.6 collective-permute-start.19
  94.6 2.1 slice_bitcast_fusion.3
  96.7 1.9 collective-permute-start.22
  98.6 2.1 slice_bitcast_fusion.2
  100.6 1.8 collective-permute-start.12
  102.4 2.1 slice_bitcast_fusion.1
  104.8 2.1 slice_bitcast_fusion
  106.9 2.0 collective-permute-start.15
  108.9 18.2 %work_far.1 = (bf16[2,128,768]{2,1,0:T(8,128)(2,1)}, bf16[4,128,768]{2,1,0:T(8,128)(2,1)}, bf16[2,128,768]{2,1,0:T(8,128)(2,1)}, bf16[4,128,768]{2,1,0:T(8,128)(...) custom-call(s32[16,4]{1,0:T(8,128)} %copy.44.refs_0_, ...), custom_call_target="tpu_custom_call" | custom-call | flops 7247757312 | bytes 17301504 | tf_op jit(solution)/shard_map/work_far/pallas_call | solution.py:290
  127.2 0.9 copy-done.12
  128.1 1.3 collective-permute-start.20
  129.4 2.9 %collective-permute-start.23 = (bf16[4,128,768]{2,1,0:T(8,128)(2,1)}, bf16[4,128,768]{2,1,0:T(8,128)(2,1)S(1)}, u32[]{:S(2)}, u32[]{:S(2)}) collective-permute-start(bf16[4,128,768]{2,1,0:T(8,128)(2,1)} %get-tuple-element.71), channel_id=1, source_target_pairs={{0,4},{1,5},{2,6},{3,7},{4,0},{5,1},{6,2},{7,3},{8,12},{9,13},{10,... | collective-permute-start | bytes 2359304 | tf_op jit(solution)/shard_map/ppermute | solution.py:383
  132.3 1.0 collective-permute-start.25
  133.3 1.7 collective-permute-start.26
  135.0 11.6 %work_last.1 = (bf16[1,128,768]{2,1,0:T(8,128)(2,1)}, bf16[2,128,768]{2,1,0:T(8,128)(2,1)}, bf16[1,128,768]{2,1,0:T(8,128)(2,1)}, bf16[2,128,768]{2,1,0:T(8,128)...) custom-call(s32[16,4]{1,0:T(8,128)} %copy.44.refs_0_, ...), custom_call_target="tpu_custom_call" | custom-call | flops 3623878656 | bytes 11796480 | tf_op jit(solution)/shard_map/work_last/pallas_call | solution.py:290
  146.8 1.3 collective-permute-start.24
  148.1 1.1 collective-permute-start.27
  149.3 7.1 %collective-permute-done.26.refs_27_.refs_29_.refs_19_.refs_13_ = bf16[4,128,768]{2,1,0:T(8,128)(2,1)S(1)} collective-permute-done((bf16[4,128,768]{2,1,0:T(8,128)(2,1)}, bf16[4,128,768]{2,1,0:T(8,128)(2,1)S(1)}, u32[]{:S(2)}, u32[]{:S(2)}) %collective-permute-start.26) | collective-permute-done | bytes 786464 | tf_op jit(solution)/shard_map/ppermute | solution.py:383
  156.4 8.4 %collective-permute-done.27.refs_31_.refs_22_ = bf16[2,128,768]{2,1,0:T(8,128)(2,1)} collective-permute-done((bf16[2,128,768]{2,1,0:T(8,128)(2,1)}, bf16[2,128,768]{2,1,0:T(8,128)(2,1)}, u32[]{:S(2)}, u32[]{:S(2)}) %collective-permute-start.27) | collective-permute-done | bytes 393248 | tf_op jit(solution)/shard_map/ppermute | solution.py:383
  164.9 4.6 %merge_1.1 = (bf16[4,128,768]{2,1,0:T(8,128)(2,1)}, bf16[4,128,768]{2,1,0:T(8,128)(2,1)}, bf16[4,128,768]{2,1,0:T(8,128)(2,1)}, bf16[4,128,768]{2,1,0:T(8,128)(2,1)}) custom-call(bf16[1,128,768]{2,1,0:T(8,128)(2,1)} %get-tuple-element.57.refs_0_, bf16[2,128,768]{2,1,0:T(8,128)(2,1)} %collective-permute-done.16.refs_1_.refs_2_, ...), custom_call_target="tpu_custom_call" | custom-call | bytes 9437184 | tf_op jit(solution)/shard_map/merge_1/pallas_call | solution.py:150
  169.6 1.3 collective-permute-start.29
  171.9 12.9 %work_kept.1 = (bf16[4,128,768]{2,1,0:T(8,128)(2,1)}, bf16[4,128,768]{2,1,0:T(8,128)(2,1)}, bf16[4,128,768]{2,1,0:T(8,128)(2,1)}, bf16[4,128,768]{2,1,0:T(8,128)(2,1)}, bf16[8,2,256,256]{3,2,1,0:T(8,128)(2,1)}) custom-call(s32[16,4]{1,0:T(8,128)} %copy.44.refs_0_, s32[2,8]{1,0:T(2,128)} %pad_add_fusion.3.refs_1_, bf16[16,2,16,256]{3,2,1,0:T(8,128)(2,1)} %bitcast.104, ...), custom_call_target="tpu_custom_call" | custom-call | flops 4831838208 | bytes 13631488 | tf_op jit(solution)/shard_map/work_kept/pallas_call | solution.py:290
  184.9 1.0 collective-permute-done.30.refs_14_.refs_17_.refs_10_.refs_13_
  186.0 0.8 copy-done.8
  187.1 3.6 %merge_2.1 = (bf16[2,128,768]{2,1,0:T(8,128)(2,1)}, bf16[2,128,768]{2,1,0:T(8,128)(2,1)}, bf16[2,128,768]{2,1,0:T(8,128)(2,1)}, bf16[2,128,768]{2,1,0:T(8,128)(2,1)}) custom-call(bf16[4,128,768]{2,1,0:T(8,128)(2,1)} %get-tuple-element.55.refs_0_.refs_3_.refs_1_, bf16[4,128,768]{2,1,0:T(8,128)(2,1)} %copy-done.2, bf16[4,128,768]{2,1,0:T(8,128)(2,1)} %copy-done.6, ...), custom_call_target="tpu_custom_call" | custom-call | bytes 6291456 | tf_op jit(solution)/shard_map/merge_2/pallas_call | solution.py:150
  190.7 2.0 collective-permute-start.32
  192.7 2.6 %collective-permute-start.34 = (bf16[2,128,768]{2,1,0:T(8,128)(2,1)}, bf16[2,128,768]{2,1,0:T(8,128)(2,1)S(1)}, u32[]{:S(2)}, u32[]{:S(2)}) collective-permute-start(bf16[2,128,768]{2,1,0:T(8,128)(2,1)} %get-tuple-element.89), channel_id=1, source_target_pairs={{0,1},{1,0},{2,3},{3,2},{4,5},{5,4},{6,7},{7,6},{8,9},{9,8},{10,11... | collective-permute-start | bytes 1179656 | tf_op jit(solution)/shard_map/ppermute | solution.py:383
  195.3 1.2 collective-permute-start.35
  196.6 1.6 collective-permute-done.32.refs_3_.refs_4_
  198.1 2.7 %collective-permute-done.33.refs_7_.refs_9_ = bf16[2,128,768]{2,1,0:T(8,128)(2,1)S(1)} collective-permute-done((bf16[2,128,768]{2,1,0:T(8,128)(2,1)}, bf16[2,128,768]{2,1,0:T(8,128)(2,1)S(1)}, u32[]{:S(2)}, u32[]{:S(2)}) %collective-permute-start.33) | collective-permute-done | bytes 393248 | tf_op jit(solution)/shard_map/ppermute | solution.py:383
  200.8 2.6 collective-permute-done.35.refs_15_.refs_19_
  203.4 0.8 copy-done.21
  204.1 2.8 %merge_3.1 = (bf16[1,128,768]{2,1,0:T(8,128)(2,1)}, bf16[1,128,768]{2,1,0:T(8,128)(2,1)}, bf16[1,128,768]{2,1,0:T(8,128)(2,1)}, bf16[1,128,768]{2,1,0:T(8,128)(2,1)}) custom-call(bf16[4,128,768]{2,1,0:T(8,128)(2,1)} %get-tuple-element.55.refs_0_.refs_3_.refs_1_, bf16[4,128,768]{2,1,0:T(8,128)(2,1)} %copy-done.2, bf16[4,128,768]{2,1,0:T(8,128)(2,1)} %copy-done.6, ...), custom_call_target="tpu_custom_call" | custom-call | bytes 3932160 | tf_op jit(solution)/shard_map/merge_3/pallas_call | solution.py:150
  207.9 1.2 collective-permute-start.38
  209.2 3.8 %collective-permute-done.36.refs_5_ = bf16[1,128,768]{2,1,0:T(8,128)(2,1)S(1)} collective-permute-done((bf16[1,128,768]{2,1,0:T(8,128)(2,1)}, bf16[1,128,768]{2,1,0:T(8,128)(2,1)S(1)}, u32[]{:S(2)}, u32[]{:S(2)}) %collective-permute-start.36) | collective-permute-done | bytes 196640 | tf_op jit(solution)/shard_map/ppermute | solution.py:383
  213.0 0.9 collective-permute-done.38.refs_15_
  213.9 0.6 copy-done.26
  214.6 4.6 %leave_rows.1 = bf16[8,96,768]{2,1,0:T(8,128)(2,1)} custom-call(s32[8,96]{1,0:T(8,128)} %get-tuple-element.52.refs_0_, bf16[4,128,768]{2,1,0:T(8,128)(2,1)} %get-tuple-element.55.refs_0_.refs_3_.refs_1_, bf16[2,128,768]{2,1,0:T(8,128)(2,1)} %collective-permute-done.16.refs_1_.refs_2_, bf16[4,128,768]{2,1,0:T(8,128)(2,1)} %copy-done.6, ...), custom_call_target="tpu_custom_call" | custom-call | tf_op jit(solution)/shard_map/leave_rows/pallas_call | solution.py:120
  219.2 14.9 %all-to-all-start.2 = ((bf16[8,96,768]{2,1,0:T(8,128)(2,1)}), bf16[8,96,768]{2,1,0:T(8,128)(2,1)S(1)}, u32[]{:S(2)}, u32[]{:S(2)}) async-start(bf16[8,96,768]{2,1,0:T(8,128)(2,1)} %leave_rows.1), calls=%async_computation.2 | async-start | bytes 2359296 | tf_op jit(solution)/shard_map/all_to_all | solution.py:516
  234.7 17.5 %panel_grad.1 = bf16[16,256,768]{2,1,0:T(8,128)(2,1)} custom-call(s32[16,4]{1,0:T(8,128)} %copy.44.refs_0_, s32[16]{0:T(128)} %iota_xor_fusion.refs_1_, bf16[2,4,128,768]{3,2,1,0:T(8,128)(2,1)} %copy-done, bf16[2,4,128,768]{3,2,1,0:T(8,128)(2,1)} %collective-permute-done.8.refs_7_.refs_5_.refs_3_, ...), custom_call_target="tpu_custom_call" | custom-call | flops 6442450944 | bytes 27262976 | tf_op jit(solution)/shard_map/panel_grad/pallas_call | solution.py:355
  252.2 1.0 copy-done.11
  253.3 4.0 %home_rows.1 = bf16[512,768]{1,0:T(8,128)(2,1)} custom-call(bf16[8,96,768]{2,1,0:T(8,128)(2,1)} %copy-done.11, s32[1,512]{1,0:T(1,128)} %get-tuple-element.95.rank_ref), custom_call_target="tpu_custom_call" | custom-call | tf_op jit(solution)/shard_map/home_rows/pallas_call | solution.py:175
  (143 shorter events, 5.7 us)
Async XLA Ops:
  4.3 6.0 %copy-start.28 = (s32[512,4]{0,1:T(4,128)S(1)}, s32[512,4]{0,1:T(4,128)}, u32[]{:S(2)}) copy-start(s32[512,4]{0,1:T(4,128)} %param.19) | copy-start | bytes 24580
  4.3 6.1 %copy-start.35 = (s32[1,24]{1,0:T(1,128)S(1)}, s32[1,24]{1,0:T(1,128)}, u32[]{:S(2)}) copy-start(s32[1,24]{1,0:T(1,128)} %param.18) | copy-start | bytes 292
  4.3 24.5 %all-to-all-start = ((bf16[8,112,768]{2,1,0:T(8,128)(2,1)}), bf16[8,112,768]{2,1,0:T(8,128)(2,1)S(1)}, u32[]{:S(2)}, u32[]{:S(2)}) async-start(bf16[8,112,768]{2,1,0:T(8,128)(2,1)} %get-tuple-element.51), calls=%async_computation | async-start | bytes 2752512 | tf_op jit(solution)/shard_map/all_to_all | solution.py:424
  10.2 33.7 %copy-start.30 = (s32[6]{0:T(128)S(1)}, s32[6]{0:T(128)}, u32[]{:S(2)}) copy-start(s32[6]{0:T(128)} %constant.87.clone) | copy-start | bytes 76
  10.2 33.7 %copy-start.31 = (s32[6]{0:T(128)S(1)}, s32[6]{0:T(128)}, u32[]{:S(2)}) copy-start(s32[6]{0:T(128)} %constant.83.clone) | copy-start | bytes 76
  10.3 33.8 %copy-start.37 = (s32[12]{0:T(128)S(1)}, s32[12]{0:T(128)}, u32[]{:S(2)}) copy-start(s32[12]{0:T(128)} %constant.85.clone) | copy-start | bytes 148
  28.9 8.5 %copy-start.10 = (bf16[8,112,768]{2,1,0:T(8,128)(2,1)}, bf16[8,112,768]{2,1,0:T(8,128)(2,1)S(1)}, u32[]{:S(2)}) copy-start(bf16[8,112,768]{2,1,0:T(8,128)(2,1)S(1)} %all-to-all-done.arrived_ref) | copy-start | bytes 4128772
  29.6 34.2 %all-to-all-start.1 = ((bf16[16,16,512]{2,1,0:T(8,128)(2,1)}), bf16[16,16,512]{2,1,0:T(8,128)(2,1)S(1)}, u32[]{:S(2)}, u32[]{:S(2)}) async-start(bf16[16,16,512]{2,1,0:T(8,128)(2,1)} %broadcast_in_dim.35), calls=%async_computation.1 | async-start | bytes 524288 | tf_op jit(solution)/shard_map/all_to_all | solution.py:399
  41.4 18.0 %copy-start.23 = (bf16[2,128,768]{2,1,0:T(8,128)(2,1)S(1)}, bf16[2,128,768]{2,1,0:T(8,128)(2,1)}, u32[]{:S(2)}) copy-start(bf16[2,128,768]{2,1,0:T(8,128)(2,1)} %get-tuple-element.53) | copy-start | bytes 1179652
  41.4 12.0 %collective-permute-start.2 = (bf16[2,128,768]{2,1,0:T(8,128)(2,1)}, bf16[2,128,768]{2,1,0:T(8,128)(2,1)S(1)}, u32[]{:S(2)}, u32[]{:S(2)}) collective-permute-start(bf16[2,128,768]{2,1,0:T(8,128)(2,1)} %get-tuple-element.53), channel_id=1, source_target_pairs={{0,3},{1,2},{2,1},{3,0},{4,7},{5,6},{6,5},{7,4},{8,11},{9,10},{10,... | collective-permute-start | bytes 1179656 | tf_op jit(solution)/shard_map/ppermute | solution.py:383
  43.9 9.5 %collective-permute-start = (bf16[2,128,768]{2,1,0:T(8,128)(2,1)}, bf16[2,128,768]{2,1,0:T(8,128)(2,1)S(1)}, u32[]{:S(2)}, u32[]{:S(2)}) collective-permute-start(bf16[2,128,768]{2,1,0:T(8,128)(2,1)} %get-tuple-element.53), channel_id=1, source_target_pairs={{0,1},{1,0},{2,3},{3,2},{4,5},{5,4},{6,7},{7,6},{8,9},{9,8},{10,11... | collective-permute-start | bytes 1179656 | tf_op jit(solution)/shard_map/ppermute | solution.py:383
  44.1 10.7 %collective-permute-start.6 = (bf16[2,128,768]{2,1,0:T(8,128)(2,1)}, bf16[2,128,768]{2,1,0:T(8,128)(2,1)S(1)}, u32[]{:S(2)}, u32[]{:S(2)}) collective-permute-start(bf16[2,128,768]{2,1,0:T(8,128)(2,1)} %get-tuple-element.54), channel_id=1, source_target_pairs={{0,12},{1,13},{2,14},{3,15},{4,8},{5,9},{6,10},{7,11},{8,4},{9,5},... | collective-permute-start | bytes 1179656 | tf_op jit(solution)/shard_map/ppermute | solution.py:383
  46.5 9.5 %collective-permute-start.4 = (bf16[2,128,768]{2,1,0:T(8,128)(2,1)}, bf16[2,128,768]{2,1,0:T(8,128)(2,1)S(1)}, u32[]{:S(2)}, u32[]{:S(2)}) collective-permute-start(bf16[2,128,768]{2,1,0:T(8,128)(2,1)} %get-tuple-element.54), channel_id=1, source_target_pairs={{0,4},{1,5},{2,6},{3,7},{4,0},{5,1},{6,2},{7,3},{8,12},{9,13},{10,... | collective-permute-start | bytes 1179656 | tf_op jit(solution)/shard_map/ppermute | solution.py:383
  53.3 4.9 %collective-permute-start.3 = (bf16[128,768]{1,0:T(8,128)(2,1)S(1)}, bf16[128,768]{1,0:T(8,128)(2,1)S(1)}, u32[]{:S(2)}, u32[]{:S(2)}) collective-permute-start(bf16[128,768]{1,0:T(8,128)(2,1)S(1)} %slice_bitcast_fusion.6), channel_id=1, source_target_pairs={{0,1},{1,0},{2,3},{3,2},{4,5},{5,4},{6,7},{7,6},{8,9},{9,8},{10,11... | collective-permute-start | bytes 589832 | tf_op jit(solution)/shard_map/ppermute | solution.py:383
  53.5 5.8 %collective-permute-start.1 = (bf16[128,768]{1,0:T(8,128)(2,1)S(1)}, bf16[128,768]{1,0:T(8,128)(2,1)S(1)}, u32[]{:S(2)}, u32[]{:S(2)}) collective-permute-start(bf16[128,768]{1,0:T(8,128)(2,1)S(1)} %slice_bitcast_fusion.7), channel_id=1, source_target_pairs={{0,3},{1,2},{2,1},{3,0},{4,7},{5,6},{6,5},{7,4},{8,11},{9,10},{10,... | collective-permute-start | bytes 589832 | tf_op jit(solution)/shard_map/ppermute | solution.py:383
  54.8 8.7 %collective-permute-start.7 = (bf16[128,768]{1,0:T(8,128)(2,1)S(1)}, bf16[128,768]{1,0:T(8,128)(2,1)S(1)}, u32[]{:S(2)}, u32[]{:S(2)}) collective-permute-start(bf16[128,768]{1,0:T(8,128)(2,1)S(1)} %slice_bitcast_fusion.4), channel_id=1, source_target_pairs={{0,4},{1,5},{2,6},{3,7},{4,0},{5,1},{6,2},{7,3},{8,12},{9,13},{10,... | collective-permute-start | bytes 589832 | tf_op jit(solution)/shard_map/ppermute | solution.py:383
  56.1 7.4 %collective-permute-start.5 = (bf16[128,768]{1,0:T(8,128)(2,1)S(1)}, bf16[128,768]{1,0:T(8,128)(2,1)S(1)}, u32[]{:S(2)}, u32[]{:S(2)}) collective-permute-start(bf16[128,768]{1,0:T(8,128)(2,1)S(1)} %slice_bitcast_fusion.5), channel_id=1, source_target_pairs={{0,12},{1,13},{2,14},{3,15},{4,8},{5,9},{6,10},{7,11},{8,4},{9,5},... | collective-permute-start | bytes 589832 | tf_op jit(solution)/shard_map/ppermute | solution.py:383
  59.4 4.2 %copy-start.22 = (bf16[2,128,768]{2,1,0:T(8,128)(2,1)S(1)}, bf16[2,128,768]{2,1,0:T(8,128)(2,1)}, u32[]{:S(2)}) copy-start(bf16[2,128,768]{2,1,0:T(8,128)(2,1)} %get-tuple-element.54) | copy-start | bytes 1179652
  59.6 4.2 %copy-start = (bf16[2,4,128,768]{3,2,1,0:T(8,128)(2,1)}, bf16[2,4,128,768]{3,2,1,0:T(8,128)(2,1)S(1)}, u32[]{:S(2)}) copy-start(bf16[2,4,128,768]{3,2,1,0:T(8,128)(2,1)S(1)} %pad_maximum_fusion.refs_5_.refs_2_) | copy-start | bytes 4718596
  59.6 33.4 %collective-permute-start.8 = (bf16[2,4,128,768]{3,2,1,0:T(8,128)(2,1)S(1)}, bf16[2,4,128,768]{3,2,1,0:T(8,128)(2,1)}, u32[]{:S(2)}, u32[]{:S(2)}) collective-permute-start(bf16[2,4,128,768]{3,2,1,0:T(8,128)(2,1)S(1)} %pad_maximum_fusion.refs_5_.refs_2_), channel_id=1, source_target_pairs={{0,4},{1,5},{2,6},{3,7},{4,0},{5,1},{6,2},{7,3},{8,12},{9,13},{10,... | collective-permute-start | bytes 4718600 | tf_op jit(solution)/shard_map/ppermute | solution.py:383
  61.7 35.0 %collective-permute-start.10 = (bf16[2,4,128,768]{3,2,1,0:T(8,128)(2,1)S(1)}, bf16[2,4,128,768]{3,2,1,0:T(8,128)(2,1)}, u32[]{:S(2)}, u32[]{:S(2)}) collective-permute-start(bf16[2,4,128,768]{3,2,1,0:T(8,128)(2,1)S(1)} %pad_maximum_fusion.refs_5_.refs_2_), channel_id=1, source_target_pairs={{0,12},{1,13},{2,14},{3,15},{4,8},{5,9},{6,10},{7,11},{8,4},{9,5},... | collective-permute-start | bytes 4718600 | tf_op jit(solution)/shard_map/ppermute | solution.py:383
  63.8 4.0 %copy-start.1 = (bf16[2,4,128,768]{3,2,1,0:T(8,128)(2,1)}, bf16[2,4,128,768]{3,2,1,0:T(8,128)(2,1)S(1)}, u32[]{:S(2)}) copy-start(bf16[2,4,128,768]{3,2,1,0:T(8,128)(2,1)S(1)} %pad_maximum_fusion.1.refs_6_.refs_7_) | copy-start | bytes 4718596
  63.8 36.9 %collective-permute-start.9 = (bf16[2,4,128,768]{3,2,1,0:T(8,128)(2,1)S(1)}, bf16[2,4,128,768]{3,2,1,0:T(8,128)(2,1)}, u32[]{:S(2)}, u32[]{:S(2)}) collective-permute-start(bf16[2,4,128,768]{3,2,1,0:T(8,128)(2,1)S(1)} %pad_maximum_fusion.1.refs_6_.refs_7_), channel_id=1, source_target_pairs={{0,1},{1,0},{2,3},{3,2},{4,5},{5,4},{6,7},{7,6},{8,9},{9,8},{10,11... | collective-permute-start | bytes 4718600 | tf_op jit(solution)/shard_map/ppermute | solution.py:383
  64.0 40.5 %collective-permute-start.11 = (bf16[2,4,128,768]{3,2,1,0:T(8,128)(2,1)S(1)}, bf16[2,4,128,768]{3,2,1,0:T(8,128)(2,1)}, u32[]{:S(2)}, u32[]{:S(2)}) collective-permute-start(bf16[2,4,128,768]{3,2,1,0:T(8,128)(2,1)S(1)} %pad_maximum_fusion.1.refs_6_.refs_7_), channel_id=1, source_target_pairs={{0,3},{1,2},{2,1},{3,0},{4,7},{5,6},{6,5},{7,4},{8,11},{9,10},{10,... | collective-permute-start | bytes 4718600 | tf_op jit(solution)/shard_map/ppermute | solution.py:383
  79.2 17.5 %copy-start.34 = (bf16[2,128,768]{2,1,0:T(8,128)(2,1)S(1)}, bf16[2,128,768]{2,1,0:T(8,128)(2,1)}, u32[]{:S(2)}) copy-start(bf16[2,128,768]{2,1,0:T(8,128)(2,1)} %get-tuple-element.69) | copy-start | bytes 1179652
  79.2 27.6 %collective-permute-start.16 = (bf16[2,128,768]{2,1,0:T(8,128)(2,1)}, bf16[2,128,768]{2,1,0:T(8,128)(2,1)}, u32[]{:S(2)}, u32[]{:S(2)}) collective-permute-start(bf16[2,128,768]{2,1,0:T(8,128)(2,1)} %get-tuple-element.56), channel_id=1, source_target_pairs={{0,1},{1,0},{2,3},{3,2},{4,5},{5,4},{6,7},{7,6},{8,9},{9,8},{10,11... | collective-permute-start | bytes 1179656 | tf_op jit(solution)/shard_map/ppermute | solution.py:383
  93.0 13.9 %collective-permute-start.19 = (bf16[2,128,768]{2,1,0:T(8,128)(2,1)}, bf16[2,128,768]{2,1,0:T(8,128)(2,1)}, u32[]{:S(2)}, u32[]{:S(2)}) collective-permute-start(bf16[2,128,768]{2,1,0:T(8,128)(2,1)} %get-tuple-element.63), channel_id=1, source_target_pairs={{0,3},{1,2},{2,1},{3,0},{4,7},{5,6},{6,5},{7,4},{8,11},{9,10},{10,... | collective-permute-start | bytes 1179656 | tf_op jit(solution)/shard_map/ppermute | solution.py:383
  96.7 30.4 %collective-permute-start.22 = (bf16[2,128,768]{2,1,0:T(8,128)(2,1)S(1)}, bf16[2,128,768]{2,1,0:T(8,128)(2,1)S(1)}, u32[]{:S(2)}, u32[]{:S(2)}) collective-permute-start(bf16[2,128,768]{2,1,0:T(8,128)(2,1)S(1)} %copy-done.34), channel_id=1, source_target_pairs={{0,4},{1,5},{2,6},{3,7},{4,0},{5,1},{6,2},{7,3},{8,12},{9,13},{10,... | collective-permute-start | bytes 1179656 | tf_op jit(solution)/shard_map/ppermute | solution.py:383
  100.6 26.5 %collective-permute-start.12 = (bf16[4,128,768]{2,1,0:T(8,128)(2,1)}, bf16[4,128,768]{2,1,0:T(8,128)(2,1)S(1)}, u32[]{:S(2)}, u32[]{:S(2)}) collective-permute-start(bf16[4,128,768]{2,1,0:T(8,128)(2,1)} %slice_bitcast_fusion.3), channel_id=1, source_target_pairs={{0,12},{1,13},{2,14},{3,15},{4,8},{5,9},{6,10},{7,11},{8,4},{9,5},... | collective-permute-start | bytes 2359304 | tf_op jit(solution)/shard_map/ppermute | solution.py:383
  104.5 24.9 %collective-permute-start.13 = (bf16[4,128,768]{2,1,0:T(8,128)(2,1)}, bf16[4,128,768]{2,1,0:T(8,128)(2,1)S(1)}, u32[]{:S(2)}, u32[]{:S(2)}) collective-permute-start(bf16[4,128,768]{2,1,0:T(8,128)(2,1)} %slice_bitcast_fusion.2), channel_id=1, source_target_pairs={{0,4},{1,5},{2,6},{3,7},{4,0},{5,1},{6,2},{7,3},{8,12},{9,13},{10,... | collective-permute-start | bytes 2359304 | tf_op jit(solution)/shard_map/ppermute | solution.py:383
  106.9 25.4 %collective-permute-start.14 = (bf16[4,128,768]{2,1,0:T(8,128)(2,1)}, bf16[4,128,768]{2,1,0:T(8,128)(2,1)S(1)}, u32[]{:S(2)}, u32[]{:S(2)}) collective-permute-start(bf16[4,128,768]{2,1,0:T(8,128)(2,1)} %slice_bitcast_fusion.1), channel_id=1, source_target_pairs={{0,3},{1,2},{2,1},{3,0},{4,7},{5,6},{6,5},{7,4},{8,11},{9,10},{10,... | collective-permute-start | bytes 2359304 | tf_op jit(solution)/shard_map/ppermute | solution.py:383
  106.9 26.4 %collective-permute-start.15 = (bf16[4,128,768]{2,1,0:T(8,128)(2,1)}, bf16[4,128,768]{2,1,0:T(8,128)(2,1)}, u32[]{:S(2)}, u32[]{:S(2)}) collective-permute-start(bf16[4,128,768]{2,1,0:T(8,128)(2,1)} %slice_bitcast_fusion), channel_id=1, source_target_pairs={{0,1},{1,0},{2,3},{3,2},{4,5},{5,4},{6,7},{7,6},{8,9},{9,8},{10,11... | collective-permute-start | bytes 2359304 | tf_op jit(solution)/shard_map/ppermute | solution.py:383
  127.1 19.6 %collective-permute-start.17 = (bf16[4,128,768]{2,1,0:T(8,128)(2,1)}, bf16[4,128,768]{2,1,0:T(8,128)(2,1)S(1)}, u32[]{:S(2)}, u32[]{:S(2)}) collective-permute-start(bf16[4,128,768]{2,1,0:T(8,128)(2,1)} %get-tuple-element.59), channel_id=1, source_target_pairs={{0,1},{1,0},{2,3},{3,2},{4,5},{5,4},{6,7},{7,6},{8,9},{9,8},{10,11... | collective-permute-start | bytes 2359304 | tf_op jit(solution)/shard_map/ppermute | solution.py:383
  128.1 18.7 %collective-permute-start.20 = (bf16[4,128,768]{2,1,0:T(8,128)(2,1)}, bf16[4,128,768]{2,1,0:T(8,128)(2,1)S(1)}, u32[]{:S(2)}, u32[]{:S(2)}) collective-permute-start(bf16[4,128,768]{2,1,0:T(8,128)(2,1)} %get-tuple-element.65), channel_id=1, source_target_pairs={{0,3},{1,2},{2,1},{3,0},{4,7},{5,6},{6,5},{7,4},{8,11},{9,10},{10,... | collective-permute-start | bytes 2359304 | tf_op jit(solution)/shard_map/ppermute | solution.py:383
  129.4 5.6 %copy-start.13 = (bf16[4,128,768]{2,1,0:T(8,128)(2,1)}, bf16[4,128,768]{2,1,0:T(8,128)(2,1)S(1)}, u32[]{:S(2)}) copy-start(bf16[4,128,768]{2,1,0:T(8,128)(2,1)S(1)} %collective-permute-done.13.refs_12_.refs_6_) | copy-start | bytes 2359300
  129.4 18.7 %collective-permute-start.23 = (bf16[4,128,768]{2,1,0:T(8,128)(2,1)}, bf16[4,128,768]{2,1,0:T(8,128)(2,1)S(1)}, u32[]{:S(2)}, u32[]{:S(2)}) collective-permute-start(bf16[4,128,768]{2,1,0:T(8,128)(2,1)} %get-tuple-element.71), channel_id=1, source_target_pairs={{0,4},{1,5},{2,6},{3,7},{4,0},{5,1},{6,2},{7,3},{8,12},{9,13},{10,... | collective-permute-start | bytes 2359304 | tf_op jit(solution)/shard_map/ppermute | solution.py:383
  132.3 14.3 %collective-permute-start.25 = (bf16[2,128,768]{2,1,0:T(8,128)(2,1)}, bf16[2,128,768]{2,1,0:T(8,128)(2,1)}, u32[]{:S(2)}, u32[]{:S(2)}) collective-permute-start(bf16[2,128,768]{2,1,0:T(8,128)(2,1)} %get-tuple-element.75), channel_id=1, source_target_pairs={{0,12},{1,13},{2,14},{3,15},{4,8},{5,9},{6,10},{7,11},{8,4},{9,5},... | collective-permute-start | bytes 1179656 | tf_op jit(solution)/shard_map/ppermute | solution.py:383
  133.3 23.1 %collective-permute-start.26 = (bf16[4,128,768]{2,1,0:T(8,128)(2,1)}, bf16[4,128,768]{2,1,0:T(8,128)(2,1)S(1)}, u32[]{:S(2)}, u32[]{:S(2)}) collective-permute-start(bf16[4,128,768]{2,1,0:T(8,128)(2,1)} %get-tuple-element.77), channel_id=1, source_target_pairs={{0,12},{1,13},{2,14},{3,15},{4,8},{5,9},{6,10},{7,11},{8,4},{9,5},... | collective-permute-start | bytes 2359304 | tf_op jit(solution)/shard_map/ppermute | solution.py:383
  146.6 9.8 %collective-permute-start.18 = (bf16[2,128,768]{2,1,0:T(8,128)(2,1)}, bf16[2,128,768]{2,1,0:T(8,128)(2,1)S(1)}, u32[]{:S(2)}, u32[]{:S(2)}) collective-permute-start(bf16[2,128,768]{2,1,0:T(8,128)(2,1)} %get-tuple-element.61), channel_id=1, source_target_pairs={{0,1},{1,0},{2,3},{3,2},{4,5},{5,4},{6,7},{7,6},{8,9},{9,8},{10,11... | collective-permute-start | bytes 1179656 | tf_op jit(solution)/shard_map/ppermute | solution.py:383
  146.7 18.1 %copy-start.2 = (bf16[4,128,768]{2,1,0:T(8,128)(2,1)}, bf16[4,128,768]{2,1,0:T(8,128)(2,1)S(1)}, u32[]{:S(2)}) copy-start(bf16[4,128,768]{2,1,0:T(8,128)(2,1)S(1)} %collective-permute-done.17.refs_3_.refs_5_.refs_1_) | copy-start | bytes 2359300
  146.7 9.7 %collective-permute-start.21 = (bf16[2,128,768]{2,1,0:T(8,128)(2,1)}, bf16[2,128,768]{2,1,0:T(8,128)(2,1)S(1)}, u32[]{:S(2)}, u32[]{:S(2)}) collective-permute-start(bf16[2,128,768]{2,1,0:T(8,128)(2,1)} %get-tuple-element.67), channel_id=1, source_target_pairs={{0,3},{1,2},{2,1},{3,0},{4,7},{5,6},{6,5},{7,4},{8,11},{9,10},{10,... | collective-permute-start | bytes 1179656 | tf_op jit(solution)/shard_map/ppermute | solution.py:383
  146.8 18.0 %copy-start.3 = (bf16[4,128,768]{2,1,0:T(8,128)(2,1)}, bf16[4,128,768]{2,1,0:T(8,128)(2,1)S(1)}, u32[]{:S(2)}) copy-start(bf16[4,128,768]{2,1,0:T(8,128)(2,1)S(1)} %collective-permute-done.20.refs_11_.refs_13_.refs_7_.refs_5_) | copy-start | bytes 2359300
  146.8 9.6 %collective-permute-start.24 = (bf16[2,128,768]{2,1,0:T(8,128)(2,1)}, bf16[2,128,768]{2,1,0:T(8,128)(2,1)}, u32[]{:S(2)}, u32[]{:S(2)}) collective-permute-start(bf16[2,128,768]{2,1,0:T(8,128)(2,1)} %get-tuple-element.73), channel_id=1, source_target_pairs={{0,4},{1,5},{2,6},{3,7},{4,0},{5,1},{6,2},{7,3},{8,12},{9,13},{10,... | collective-permute-start | bytes 1179656 | tf_op jit(solution)/shard_map/ppermute | solution.py:383
  148.1 16.7 %copy-start.4 = (bf16[4,128,768]{2,1,0:T(8,128)(2,1)}, bf16[4,128,768]{2,1,0:T(8,128)(2,1)S(1)}, u32[]{:S(2)}) copy-start(bf16[4,128,768]{2,1,0:T(8,128)(2,1)S(1)} %collective-permute-done.23.refs_19_.refs_21_.refs_13_.refs_9_) | copy-start | bytes 2359300
  148.1 16.6 %collective-permute-start.27 = (bf16[2,128,768]{2,1,0:T(8,128)(2,1)}, bf16[2,128,768]{2,1,0:T(8,128)(2,1)}, u32[]{:S(2)}, u32[]{:S(2)}) collective-permute-start(bf16[2,128,768]{2,1,0:T(8,128)(2,1)} %get-tuple-element.79), channel_id=1, source_target_pairs={{0,12},{1,13},{2,14},{3,15},{4,8},{5,9},{6,10},{7,11},{8,4},{9,5},... | collective-permute-start | bytes 1179656 | tf_op jit(solution)/shard_map/ppermute | solution.py:383
  156.4 8.4 %copy-start.5 = (bf16[4,128,768]{2,1,0:T(8,128)(2,1)}, bf16[4,128,768]{2,1,0:T(8,128)(2,1)S(1)}, u32[]{:S(2)}) copy-start(bf16[4,128,768]{2,1,0:T(8,128)(2,1)S(1)} %collective-permute-done.26.refs_27_.refs_29_.refs_19_.refs_13_) | copy-start | bytes 2359300
  156.4 8.4 %copy-start.16 = (bf16[2,128,768]{2,1,0:T(8,128)(2,1)}, bf16[2,128,768]{2,1,0:T(8,128)(2,1)S(1)}, u32[]{:S(2)}) copy-start(bf16[2,128,768]{2,1,0:T(8,128)(2,1)S(1)} %collective-permute-done.18.refs_7_.refs_4_) | copy-start | bytes 1179652
  156.4 8.4 %copy-start.17 = (bf16[2,128,768]{2,1,0:T(8,128)(2,1)}, bf16[2,128,768]{2,1,0:T(8,128)(2,1)S(1)}, u32[]{:S(2)}) copy-start(bf16[2,128,768]{2,1,0:T(8,128)(2,1)S(1)} %collective-permute-done.21.refs_15_.refs_10_) | copy-start | bytes 1179652
  164.8 6.6 %copy-start.36 = (s32[8]{0:T(128)S(1)}, s32[8]{0:T(128)}, u32[]{:S(2)}) copy-start(s32[8]{0:T(128)} %constant.88.clone) | copy-start | bytes 100
  164.8 6.5 %copy-start.32 = (s32[1,8]{1,0:T(1,128)S(1)}, s32[1,8]{1,0:T(1,128)}, u32[]{:S(2)}) copy-start(s32[1,8]{1,0:T(1,128)} %constant.95) | copy-start | bytes 100
  169.5 15.3 %collective-permute-start.28 = (bf16[4,128,768]{2,1,0:T(8,128)(2,1)}, bf16[4,128,768]{2,1,0:T(8,128)(2,1)S(1)}, u32[]{:S(2)}, u32[]{:S(2)}) collective-permute-start(bf16[4,128,768]{2,1,0:T(8,128)(2,1)} %get-tuple-element.80), channel_id=1, source_target_pairs={{0,3},{1,2},{2,1},{3,0},{4,7},{5,6},{6,5},{7,4},{8,11},{9,10},{10,... | collective-permute-start | bytes 2359304 | tf_op jit(solution)/shard_map/ppermute | solution.py:383
  169.6 15.3 %collective-permute-start.29 = (bf16[4,128,768]{2,1,0:T(8,128)(2,1)}, bf16[4,128,768]{2,1,0:T(8,128)(2,1)S(1)}, u32[]{:S(2)}, u32[]{:S(2)}) collective-permute-start(bf16[4,128,768]{2,1,0:T(8,128)(2,1)} %get-tuple-element.82), channel_id=1, source_target_pairs={{0,1},{1,0},{2,3},{3,2},{4,5},{5,4},{6,7},{7,6},{8,9},{9,8},{10,11... | collective-permute-start | bytes 2359304 | tf_op jit(solution)/shard_map/ppermute | solution.py:383
  170.9 15.0 %collective-permute-start.30 = (bf16[4,128,768]{2,1,0:T(8,128)(2,1)}, bf16[4,128,768]{2,1,0:T(8,128)(2,1)S(1)}, u32[]{:S(2)}, u32[]{:S(2)}) collective-permute-start(bf16[4,128,768]{2,1,0:T(8,128)(2,1)} %get-tuple-element.84), channel_id=1, source_target_pairs={{0,12},{1,13},{2,14},{3,15},{4,8},{5,9},{6,10},{7,11},{8,4},{9,5},... | collective-permute-start | bytes 2359304 | tf_op jit(solution)/shard_map/ppermute | solution.py:383
  170.9 15.0 %collective-permute-start.31 = (bf16[4,128,768]{2,1,0:T(8,128)(2,1)}, bf16[4,128,768]{2,1,0:T(8,128)(2,1)S(1)}, u32[]{:S(2)}, u32[]{:S(2)}) collective-permute-start(bf16[4,128,768]{2,1,0:T(8,128)(2,1)} %get-tuple-element.86), channel_id=1, source_target_pairs={{0,4},{1,5},{2,6},{3,7},{4,0},{5,1},{6,2},{7,3},{8,12},{9,13},{10,... | collective-permute-start | bytes 2359304 | tf_op jit(solution)/shard_map/ppermute | solution.py:383
  190.7 7.4 %collective-permute-start.32 = (bf16[2,128,768]{2,1,0:T(8,128)(2,1)}, bf16[2,128,768]{2,1,0:T(8,128)(2,1)S(1)}, u32[]{:S(2)}, u32[]{:S(2)}) collective-permute-start(bf16[2,128,768]{2,1,0:T(8,128)(2,1)} %get-tuple-element.87), channel_id=1, source_target_pairs={{0,4},{1,5},{2,6},{3,7},{4,0},{5,1},{6,2},{7,3},{8,12},{9,13},{10,... | collective-permute-start | bytes 1179656 | tf_op jit(solution)/shard_map/ppermute | solution.py:383
  192.7 8.0 %collective-permute-start.33 = (bf16[2,128,768]{2,1,0:T(8,128)(2,1)}, bf16[2,128,768]{2,1,0:T(8,128)(2,1)S(1)}, u32[]{:S(2)}, u32[]{:S(2)}) collective-permute-start(bf16[2,128,768]{2,1,0:T(8,128)(2,1)} %get-tuple-element.88), channel_id=1, source_target_pairs={{0,12},{1,13},{2,14},{3,15},{4,8},{5,9},{6,10},{7,11},{8,4},{9,5},... | collective-permute-start | bytes 1179656 | tf_op jit(solution)/shard_map/ppermute | solution.py:383
  192.7 8.1 %collective-permute-start.34 = (bf16[2,128,768]{2,1,0:T(8,128)(2,1)}, bf16[2,128,768]{2,1,0:T(8,128)(2,1)S(1)}, u32[]{:S(2)}, u32[]{:S(2)}) collective-permute-start(bf16[2,128,768]{2,1,0:T(8,128)(2,1)} %get-tuple-element.89), channel_id=1, source_target_pairs={{0,1},{1,0},{2,3},{3,2},{4,5},{5,4},{6,7},{7,6},{8,9},{9,8},{10,11... | collective-permute-start | bytes 1179656 | tf_op jit(solution)/shard_map/ppermute | solution.py:383
  195.3 8.0 %collective-permute-start.35 = (bf16[2,128,768]{2,1,0:T(8,128)(2,1)}, bf16[2,128,768]{2,1,0:T(8,128)(2,1)S(1)}, u32[]{:S(2)}, u32[]{:S(2)}) collective-permute-start(bf16[2,128,768]{2,1,0:T(8,128)(2,1)} %get-tuple-element.90), channel_id=1, source_target_pairs={{0,3},{1,2},{2,1},{3,0},{4,7},{5,6},{6,5},{7,4},{8,11},{9,10},{10,... | collective-permute-start | bytes 1179656 | tf_op jit(solution)/shard_map/ppermute | solution.py:383
  198.1 5.3 %copy-start.18 = (bf16[2,128,768]{2,1,0:T(8,128)(2,1)}, bf16[2,128,768]{2,1,0:T(8,128)(2,1)S(1)}, u32[]{:S(2)}) copy-start(bf16[2,128,768]{2,1,0:T(8,128)(2,1)S(1)} %collective-permute-done.32.refs_3_.refs_4_) | copy-start | bytes 1179652
  207.0 6.0 %collective-permute-start.36 = (bf16[1,128,768]{2,1,0:T(8,128)(2,1)}, bf16[1,128,768]{2,1,0:T(8,128)(2,1)S(1)}, u32[]{:S(2)}, u32[]{:S(2)}) collective-permute-start(bf16[1,128,768]{2,1,0:T(8,128)(2,1)} %get-tuple-element.91), channel_id=1, source_target_pairs={{0,12},{1,13},{2,14},{3,15},{4,8},{5,9},{6,10},{7,11},{8,4},{9,5},... | collective-permute-start | bytes 589832 | tf_op jit(solution)/shard_map/ppermute | solution.py:383
  207.4 5.6 %collective-permute-start.37 = (bf16[1,128,768]{2,1,0:T(8,128)(2,1)}, bf16[1,128,768]{2,1,0:T(8,128)(2,1)S(1)}, u32[]{:S(2)}, u32[]{:S(2)}) collective-permute-start(bf16[1,128,768]{2,1,0:T(8,128)(2,1)} %get-tuple-element.92), channel_id=1, source_target_pairs={{0,4},{1,5},{2,6},{3,7},{4,0},{5,1},{6,2},{7,3},{8,12},{9,13},{10,... | collective-permute-start | bytes 589832 | tf_op jit(solution)/shard_map/ppermute | solution.py:383
  207.9 5.9 %collective-permute-start.38 = (bf16[1,128,768]{2,1,0:T(8,128)(2,1)}, bf16[1,128,768]{2,1,0:T(8,128)(2,1)S(1)}, u32[]{:S(2)}, u32[]{:S(2)}) collective-permute-start(bf16[1,128,768]{2,1,0:T(8,128)(2,1)} %get-tuple-element.93), channel_id=1, source_target_pairs={{0,3},{1,2},{2,1},{3,0},{4,7},{5,6},{6,5},{7,4},{8,11},{9,10},{10,... | collective-permute-start | bytes 589832 | tf_op jit(solution)/shard_map/ppermute | solution.py:383
  209.2 4.7 %collective-permute-start.39 = (bf16[1,128,768]{2,1,0:T(8,128)(2,1)}, bf16[1,128,768]{2,1,0:T(8,128)(2,1)S(1)}, u32[]{:S(2)}, u32[]{:S(2)}) collective-permute-start(bf16[1,128,768]{2,1,0:T(8,128)(2,1)} %get-tuple-element.94), channel_id=1, source_target_pairs={{0,1},{1,0},{2,3},{3,2},{4,5},{5,4},{6,7},{7,6},{8,9},{9,8},{10,11... | collective-permute-start | bytes 589832 | tf_op jit(solution)/shard_map/ppermute | solution.py:383
  219.2 33.0 %all-to-all-start.2 = ((bf16[8,96,768]{2,1,0:T(8,128)(2,1)}), bf16[8,96,768]{2,1,0:T(8,128)(2,1)S(1)}, u32[]{:S(2)}, u32[]{:S(2)}) async-start(bf16[8,96,768]{2,1,0:T(8,128)(2,1)} %leave_rows.1), calls=%async_computation.2 | async-start | bytes 2359296 | tf_op jit(solution)/shard_map/all_to_all | solution.py:516
  (17 other events, 21.6 us)

commit v3 on v2

--- a/solution.py
+++ b/solution.py
@@ -1,6 +1,7 @@
 import functools
 import jax
 import jax.numpy as jnp
+import numpy as np
 from jax import lax
 from jax.experimental import pallas as pl
 from jax.experimental.pallas import tpu as pltpu
@@ -8,7 +9,7 @@
 
 CAP = 2
 CODE = 16
-LIMIT = 60 << 20
+LIMIT = 63 << 20
 BF = jnp.bfloat16
 F32 = jnp.float32
 
@@ -69,7 +70,7 @@
     return jnp.where(code[2:3] > 0.5, place, -1)
 
 
-def land_body(groups, slots, arrived_ref, place_ref, *pair_refs):
+def land_body(groups, slots, arrived_ref, code_ref, place_ref, *pair_refs):
     part = pair_refs[0].shape[1]
     rows = 2 * part * len(pair_refs)
     total = jnp.zeros((rows, arrived_ref.shape[2]), F32)
@@ -82,15 +83,16 @@
         pair_refs[k // 2][k % 2] = total[k * part : (k + 1) * part].astype(BF)
 
 
-def land(arrived, rows, slots):
+def land(arrived, codes, rows, slots):
     groups, _, width = arrived.shape
     pair = jax.ShapeDtypeStruct((2, rows // STREAMS, width), BF)
     return pl.pallas_call(
         functools.partial(land_body, groups, slots),
+        in_specs=[pl.BlockSpec(memory_space=pltpu.VMEM), pl.BlockSpec(memory_space=pltpu.HBM)],
         out_shape=(jax.ShapeDtypeStruct((groups, slots), jnp.int32), pair, pair),
         compiler_params=params(LIMIT),
         name="land_rows",
-    )(arrived)
+    )(arrived, codes)
 
 
 def leave_body(groups, slots, terms, *refs):
@@ -180,13 +182,47 @@
     )(back, rank)
 
 
+def cut_body(halves, *refs):
+    n = len(halves)
+    buf, in_sem, out_sem = refs[2 * n :]
+    loads = [pltpu.make_async_copy(refs[i].at[h], buf.at[i], in_sem.at[i]) for i, h in enumerate(halves)]
+    stores = [pltpu.make_async_copy(buf.at[i], refs[n + i], out_sem.at[i]) for i in range(n)]
+    for load in loads:
+        load.start()
+    for load, store in zip(loads, stores):
+        load.wait()
+        store.start()
+    for store in stores:
+        store.wait()
+
+
+def cut(items):
+    n = len(items)
+    loose = pl.BlockSpec(memory_space=pltpu.HBM)
+    return pl.pallas_call(
+        functools.partial(cut_body, [h for _, h in items]),
+        in_specs=[loose] * n,
+        out_specs=[loose] * n,
+        out_shape=[jax.ShapeDtypeStruct(a.shape[1:], a.dtype) for a, _ in items],
+        scratch_shapes=[
+            pltpu.VMEM((n, *items[0][0].shape[1:]), items[0][0].dtype),
+            pltpu.SemaphoreType.DMA((n,)),
+            pltpu.SemaphoreType.DMA((n,)),
+        ],
+        compiler_params=params(LIMIT),
+        name="cut_halves",
+    )(*[a for a, _ in items])
+
+
 def work_body(units, n_in, n_out, *refs):
-    table_ref, meta_ref, code_ref, w_hbm, scale_ref = refs[:5]
+    table_ref, meta_ref, code_hbm, w_hbm, scale_hbm = refs[:5]
     x_refs = refs[5 : 5 + n_in]
     out_refs = refs[5 + n_in : 5 + n_in + n_out]
     signal_ref = refs[5 + n_in + n_out]
     scratch = refs[6 + n_in + n_out :]
-    x_buf, out_buf, signal_buf, w_ref, lane_scale_ref, ready_ref, in_sem, out_sem, signal_sem, w_sem = scratch
+    x_buf, out_buf, signal_buf, w_ref, code_ref, lane_scale_ref, state_ref, in_sem, out_sem, signal_sem, w_sem, code_sem = (
+        scratch
+    )
     total = len(units)
     count, lanes, width = w_ref.shape
     rows = x_buf.shape[1]
@@ -204,63 +240,72 @@
             cut = x_buf.at[u, pl.ds(h * part, part)]
             pltpu.make_async_copy(x_refs[array].at[index], cut, in_sem.at[u]).start()
 
-    def panel_copy(p):
-        return pltpu.make_async_copy(w_hbm.at[p], w_ref.at[p], w_sem.at[p])
-
-    fetch(0)
+    def panel_copies(p):
+        return (
+            pltpu.make_async_copy(w_hbm.at[p], w_ref.at[p], w_sem.at[p, 0]),
+            pltpu.make_async_copy(scale_hbm.at[p], lane_scale_ref.at[p], w_sem.at[p, 1]),
+        )
+
+    def ask(panel):
+        @pl.when(state_ref[panel] == 0)
+        def _():
+            state_ref[panel] = 1
+            for copy in panel_copies(panel):
+                copy.start()
+
+    def need(panel):
+        @pl.when(state_ref[panel] == 1)
+        def _():
+            state_ref[panel] = 2
+            for copy in panel_copies(panel):
+                copy.wait()
+
+    def slots_of(u):
+        batch = meta_ref[0, u]
+        first = table_ref[batch, 1]
+        second = table_ref[batch, 3]
+        use_first = jnp.maximum(first, 0)
+        use_second = jnp.where(second >= 0, second, use_first)
+        return batch, (first, second), (use_first, use_second)
+
+    code_cut = code_hbm.at[:, pl.ds(0, 2)]
+    code_copy = pltpu.make_async_copy(code_cut, code_ref, code_sem.at[0])
+    code_copy.start()
     for p in range(count):
-        panel_copy(p).start()
-        ready_ref[p] = 0
-    for u in range(1, total):
+        state_ref[p] = 0
+    for u in range(total):
         fetch(u)
-    columns = jnp.transpose(scale_ref[...].astype(F32))
-    for p in range(count):
-        lane_scale_ref[p] = jnp.broadcast_to(columns[:, p : p + 1], (lanes, 128))
-
-    def need(panel):
-        @pl.when(ready_ref[panel] == 0)
-        def _():
-            panel_copy(panel).wait()
-            ready_ref[panel] = 1
-
-    def unit(u, carry):
+        for panel in slots_of(u)[2]:
+            ask(panel)
+    code_copy.wait()
+
+    def ready(u):
         pltpu.make_async_copy(x_buf.at[u], x_buf.at[u], in_sem.at[u]).wait()
-        batch = meta_ref[0, u]
-        x = x_buf[u]
+        for panel in slots_of(u)[2]:
+            need(panel)
+
+    def signals(u):
+        batch, asked, use = slots_of(u)
         code = code_ref[batch, meta_ref[1, u]].astype(F32).astype(jnp.int32)
-
-        def one(c):
+        scores = dot(jnp.concatenate([w_ref[use[0]], w_ref[use[1]]], axis=0), x_buf[u], NT)
+        for c in range(CAP):
             slot = table_ref[batch, 2 * c]
-            panel = table_ref[batch, 2 * c + 1]
-            w = w_ref[panel]
-            scale = jnp.concatenate([lane_scale_ref[panel]] * (rows // 128), axis=1)
-            score = dot(w, x, NT) * scale
+            weight = jnp.where(asked[c] >= 0, 1.0, 0.0)
+            scale = jnp.concatenate([lane_scale_ref[use[c]].astype(F32)] * (rows // 128), axis=1)
+            score = scores[c * lanes : (c + 1) * lanes] * scale
             lane = iota((lanes, rows), 0)
             hit = lane == jnp.where(code[0:1] == slot, code[4:5], -1)
             for k in range(1, 4):
                 hit |= lane == jnp.where(code[k : k + 1] == slot, code[4 + k : 5 + k], -1)
-            signal = ((jax.nn.sigmoid(score) - jnp.where(hit, 1.0, 0.0)) * scale).astype(BF)
-            signal_buf[u, c] = signal
-            return dot(signal, w, TN)
-
-        first = table_ref[batch, 0] >= 0
-        second = table_ref[batch, 2] >= 0
-
-        @pl.when(jnp.logical_not(first))
-        def _():
-            out_buf[u] = jnp.zeros((rows, width), BF)
-
-        @pl.when(first & jnp.logical_not(second))
-        def _():
-            need(table_ref[batch, 1])
-            out_buf[u] = one(0).astype(BF)
-
-        @pl.when(second)
-        def _():
-            need(table_ref[batch, 1])
-            need(table_ref[batch, 3])
-            out_buf[u] = (one(0) + one(1)).astype(BF)
-
+            signal = (jax.nn.sigmoid(score) - jnp.where(hit, 1.0, 0.0)) * (scale * weight)
+            signal_buf[u, c] = signal.astype(BF)
+
+    def partial(u):
+        use = slots_of(u)[2]
+        total_grad = dot(signal_buf[u, 0], w_ref[use[0]], TN) + dot(signal_buf[u, 1], w_ref[use[1]], TN)
+        out_buf[u] = total_grad.astype(BF)
+
+    def send(u):
         for v in range(total):
 
             @pl.when(u == v)
@@ -268,28 +313,36 @@
                 for copy in store(v):
                     copy.start()
 
+    ready(0)
+    signals(0)
+
+    def step(u, carry):
+        ready(u)
+        partial(u - 1)
+        signals(u)
+        send(u - 1)
         return carry
 
-    lax.fori_loop(0, total, unit, 0)
-    for p in range(count):
-        need(p)
+    lax.fori_loop(1, total, step, 0)
+    partial(total - 1)
+    for copy in store(total - 1):
+        copy.start()
     for u in range(total):
         for copy in store(u):
             copy.wait()
 
 
-def work(table, batches, codes, panels, scales, arrays, units, out_blocks, name):
+def work(table, offsets, codes, panels, scales, arrays, units, out_blocks, name):
     count, lanes, width = panels.shape
-    part = codes.shape[3] // 2
+    part = arrays[0].shape[-2]
     rows = 2 * part
-    meta = jnp.stack([batches, jnp.array([u[2] for u in units], jnp.int32)])
+    meta = np.array([offsets, [u[2] for u in units]], np.int32)
     total = len(units)
-    whole = pl.BlockSpec(memory_space=pltpu.VMEM)
     scalar = pl.BlockSpec(memory_space=pltpu.SMEM)
     loose = pl.BlockSpec(memory_space=pltpu.HBM)
     outs = pl.pallas_call(
         functools.partial(work_body, units, len(arrays), len(out_blocks)),
-        in_specs=[scalar, scalar, whole, loose, whole] + [loose] * len(arrays),
+        in_specs=[scalar, scalar, loose, loose, loose] + [loose] * len(arrays),
         out_specs=[loose] * len(out_blocks) + [loose],
         out_shape=[jax.ShapeDtypeStruct((n, part, width), BF) for n in out_blocks]
         + [jax.ShapeDtypeStruct((total, CAP, lanes, rows), BF)],
@@ -298,12 +351,14 @@
             pltpu.VMEM((total, rows, width), BF),
             pltpu.VMEM((total, CAP, lanes, rows), BF),
             pltpu.VMEM(panels.shape, BF),
-            pltpu.VMEM((count, lanes, 128), F32),
+            pltpu.VMEM((codes.shape[0], 2, CODE, rows), BF),
+            pltpu.VMEM(scales.shape, BF),
             pltpu.SMEM((count,), jnp.int32),
             pltpu.SemaphoreType.DMA((total,)),
             pltpu.SemaphoreType.DMA((2 * total,)),
             pltpu.SemaphoreType.DMA((total,)),
-            pltpu.SemaphoreType.DMA((count,)),
+            pltpu.SemaphoreType.DMA((count, 2)),
+            pltpu.SemaphoreType.DMA((1,)),
         ],
         compiler_params=params(LIMIT),
         cost_estimate=pl.CostEstimate(
@@ -317,10 +372,10 @@
 
 
 def panel_body(parts, n_arrays, n_signals, *refs):
-    table_ref, batch_ref = refs[:2]
-    x_refs = refs[2 : 2 + n_arrays]
-    s_refs = refs[2 + n_arrays : 2 + n_arrays + n_signals]
-    grad_ref, x_all, s_all, total_ref, x_sem, s_sem = refs[2 + n_arrays + n_signals :]
+    table_ref = refs[0]
+    x_refs = refs[1 : 1 + n_arrays]
+    s_refs = refs[1 + n_arrays : 1 + n_arrays + n_signals]
+    grad_ref, x_all, s_all, total_ref, x_sem, s_sem = refs[1 + n_arrays + n_signals :]
     rows = x_all.shape[1] // STREAMS
     for rel, pieces in enumerate(parts):
         for pair, (sources, signal, unit) in enumerate(pieces):
@@ -334,12 +389,19 @@
     def batch(rel, carry):
         pltpu.make_async_copy(x_all.at[rel], x_all.at[rel], x_sem.at[rel]).wait()
         pltpu.make_async_copy(s_all.at[rel], s_all.at[rel], s_sem.at[rel]).wait()
-        for c in range(CAP):
-            panel = table_ref[batch_ref[rel], 2 * c + 1]
-
-            @pl.when(panel >= 0)
-            def _():
-                total_ref[panel] += dot(s_all[rel, c], x_all[rel], NN)
+        first = table_ref[rel, 1]
+        second = table_ref[rel, 3]
+        lanes = s_all.shape[2]
+
+        @pl.when((first >= 0) & (second < 0))
+        def _():
+            total_ref[first] += dot(s_all[rel, 0], x_all[rel], NN)
+
+        @pl.when(second >= 0)
+        def _():
+            both = dot(jnp.concatenate([s_all[rel, 0], s_all[rel, 1]], axis=0), x_all[rel], NN)
+            total_ref[first] += both[:lanes]
+            total_ref[second] += both[lanes:]
 
         return carry
 
@@ -347,14 +409,14 @@
     grad_ref[...] = total_ref[...].astype(BF)
 
 
-def panel_sum(table, batches, arrays, signals, parts, shape):
+def panel_sum(table, arrays, signals, parts, shape):
     count, lanes, width = shape
     rows = arrays[0].shape[2] * STREAMS
     scalar = pl.BlockSpec(memory_space=pltpu.SMEM)
     loose = pl.BlockSpec(memory_space=pltpu.HBM)
     return pl.pallas_call(
         functools.partial(panel_body, parts, len(arrays), len(signals)),
-        in_specs=[scalar, scalar] + [loose] * (len(arrays) + len(signals)),
+        in_specs=[scalar] + [loose] * (len(arrays) + len(signals)),
         out_specs=pl.BlockSpec(memory_space=pltpu.VMEM),
         out_shape=jax.ShapeDtypeStruct(shape, BF),
         scratch_shapes=[
@@ -371,7 +433,7 @@
             bytes_accessed=len(parts) * rows * (width + CAP * lanes) * 2 + count * lanes * width * 2,
         ),
         name="panel_grad",
-    )(table, batches, *arrays, *signals)
+    )(table, *arrays, *signals)
 
 
 ORDERS = ((1, 3, 4, 12), (3, 1, 12, 4), (4, 12, 1, 3), (12, 4, 3, 1))
@@ -392,15 +454,20 @@
     part = rows // STREAMS
     me = lax.axis_index("label").astype(jnp.int32)
 
-    marks = positives.T
-    code = jnp.concatenate([marks // lanes, marks % lanes], axis=0).astype(F32).astype(BF)
-    wanted_row = jnp.pad(shortlist.astype(F32).astype(BF), ((0, 0), (0, rows - shortlist.shape[1])))
-    code = jnp.concatenate([code, wanted_row, jnp.zeros((CODE - code.shape[0] - 1, rows), BF)], axis=0)
-    codes = lax.all_to_all(
-        jnp.broadcast_to(code, (owners, *code.shape)), "label", split_axis=0, concat_axis=0, tiled=True
-    )
-    wanted = codes[:, 8, : shortlist.shape[1]].astype(F32).astype(jnp.int32)
-    codes = jnp.transpose(codes.reshape(owners, CODE, STREAMS // 2, 2 * part), (0, 2, 1, 3))
+    outgoing, rank = pack(queries, cluster_dest.reshape(1, rows), groups, slots)
+
+    marks = jnp.transpose(positives.reshape(2, 2 * part, -1), (0, 2, 1))
+    code = jnp.concatenate([marks // lanes, marks % lanes], axis=1).astype(F32).astype(BF)
+    code = jnp.pad(code, ((0, 0), (0, CODE - code.shape[1]), (0, 0)))
+    listed = jnp.pad(shortlist.astype(F32).astype(BF), ((0, CODE - 1), (0, 2 * part - shortlist.shape[1])))
+    code = jnp.concatenate([code, listed[None]], axis=0)[None]
+    outgoing, codes = lax.optimization_barrier((outgoing, code))
+    arrived = lax.all_to_all(outgoing, "dp", split_axis=0, concat_axis=0, tiled=True)
+    for step in range(4):
+        codes = jnp.concatenate([codes, swap(codes, 1 << step, owners)], axis=0)
+    place, *own = land(arrived, codes, rows, slots)
+    wanted = codes[:, 2, 0, : shortlist.shape[1]].astype(F32).astype(jnp.int32)
+
     slot_ids = jnp.arange(wanted.shape[1], dtype=jnp.int32)[None, :]
     mine = wanted // count == me
     local = wanted % count
@@ -420,10 +487,6 @@
         axis=1,
     )
 
-    outgoing, rank = pack(queries, cluster_dest.reshape(1, rows), groups, slots)
-    arrived = lax.all_to_all(outgoing, "dp", split_axis=0, concat_axis=0, tiled=True)
-    place, *own = land(arrived, rows, slots)
-
     every = range(STREAMS)
     order = ORDERS
     arrays = []
@@ -432,9 +495,12 @@
         low, high = swap(by1[0], three, owners), swap(by3[1], one, owners)
         near = jnp.stack([pair, by1, jnp.stack([low, high]), by3], axis=1)
         arrays.append([near])
+
     for group, (one, three) in zip(arrays, RINGS[::-1]):
-        by1, by3 = swap(group[0], one, owners), swap(group[0], three, owners)
-        group += [by1, by3, swap(by1[0], three, owners), swap(by3[1], one, owners)]
+        group += [swap(group[0], one, owners), swap(group[0], three, owners)]
+    halves = cut([(group[1 + h], h) for group in arrays for h in (0, 1)])
+    for group, (one, three), (low, high) in zip(arrays, RINGS[::-1], (halves[:2], halves[2:])):
+        group += [swap(low, three, owners), swap(high, one, owners)]
 
     def rel(k, bits):
         out = 0
@@ -444,6 +510,7 @@
         return out
 
     where = {}
+    wide_scales = jnp.broadcast_to(scales[:, :, None], (count, lanes, 128))
 
     def bits_of(k, r):
         return next(b for b in range(owners) if rel(k, b) == r)
@@ -476,10 +543,9 @@
             (origin, tuple((keys.index((k, b & 1)), outs_of[k, b & 1].index(b)) for k, b in legs), pair)
             for origin, legs, pair in units
         ]
-        batches = jnp.array(ids, jnp.int32) ^ me
         blocks = [len(outs_of[key]) for key in keys]
         ins = [arrays[pair][a] for pair, a in used]
-        outs, signals = work(table, batches, codes, panels, scales, ins, units, blocks, name)
+        outs, signals = work(table, ids, codes, panels, wide_scales, ins, units, blocks, name)
         outs = dict(zip(keys, outs))
         for key in keys:
             for n, b in enumerate(outs_of[key]):
@@ -524,7 +590,6 @@
             parts[r].append((tuple((flat.index(a), i) for a, i in origin), signal, unit))
     panel_grad = panel_sum(
         table,
-        jnp.arange(owners, dtype=jnp.int32) ^ me,
         [arrays[pair][a] for pair, a in flat],
         signals,
         parts,

time: 260 us -> 245 us (0.942)
  local copies, waits for them, and re-layouts: 15.3 us -> 3.92 us
  starting transfers between devices: 70.4 us -> 81 us
  waiting for transfers between devices: 68.2 us -> 60.8 us
  Pallas kernels: 98.9 us -> 92 us
    all_to_all x1, waiting for transfers between devices: 18.4 us -> 0.01 us  [shards(): lax.all_to_all(outgoing, 'dp', split_axis=0, concat_axis=0, tiled=True)]
    ppermute x40 -> x44, starting transfers between devices: 41.8 us -> 53.8 us  [swap(): return lax.ppermute(array, 'label', [(i, i ^ mask) for i in range(owners)])]
    ppermute x40 -> x44, waiting for transfers between devices: 49.9 us -> 59.3 us  [swap(): return lax.ppermute(array, 'label', [(i, i ^ mask) for i in range(owners)])]
    squeeze x4 -> x0, local copies, waits for them, and re-layouts: 8.26 us -> none  [shards(): group += [by1, by3, swap(by1[0], three, owners), swap(by3[1], one, owners)]]
    all_to_all x1 -> x0, starting transfers between devices: 7.77 us -> none  [shards(): lax.all_to_all(jnp.broadcast_to(code, (owners, *code.shape)), 'label', sp...]
    pallas_call x4, Pallas kernels: 54.1 us -> 46.8 us  [work(): pl.pallas_call(functools.partial(work_body, units, len(arrays), len(out_b...]
    all_to_all x1, starting transfers between devices: 14.9 us -> 21.4 us  [shards(): lax.all_to_all(leaving, 'dp', split_axis=0, concat_axis=0, tiled=True)]
    unnamed x76 -> x32, local copies, waits for them, and re-layouts: 4.72 us -> 1.59 us
  transfers between devices with their start and end apart: 43 -> 46, of which waited for: 13 -> 21; matrix products, arithmetic and copies ran while one was open for 5% -> 3% of each run, Pallas kernels for 29% -> 27%
where the time goes in v3:
time: 245 us; the launch traced here: 244 us
  Pallas kernels  92 us (38%)
  starting transfers between devices  81 us (33%)
  waiting for transfers between devices  60.8 us (25%)
  other arithmetic  5.33 us (2%)
  local copies, waits for them, and re-layouts  3.92 us (2%)
    ppermute x44, waiting for transfers between devices, swap(): return lax.ppermute(array, 'label', [(i, i ^ mask) for i in range(owners)])  59.3 us
    ppermute x44, starting transfers between devices, swap(): return lax.ppermute(array, 'label', [(i, i ^ mask) for i in range(owners)])  53.8 us
    pallas_call x4, Pallas kernels, work(): pl.pallas_call(functools.partial(work_body, units, len(arrays), len(out_b...  46.8 us
    all_to_all x1, starting transfers between devices, shards(): lax.all_to_all(leaving, 'dp', split_axis=0, concat_axis=0, tiled=True)  21.4 us
    pallas_call x1, Pallas kernels, panel_sum(): pl.pallas_call(functools.partial(panel_body, parts, len(arrays), len(sign...  15.1 us
    pallas_call x3, Pallas kernels, merge(): pl.pallas_call(functools.partial(merge_body, [[[0] * len(t) for t in b] f...  10.9 us
    all_to_all x1, starting transfers between devices, shards(): lax.all_to_all(outgoing, 'dp', split_axis=0, concat_axis=0, tiled=True)  5.81 us
  transfers between devices with their start and end apart: 46, of which 21 were waited for; matrix products, arithmetic and copies ran while one was open for 3% of the time, Pallas kernels for 27%

profile of v3, /device:TPU:1, one launch (start us, length us, event | category | flops | bytes accessed | tf_op | source)
XLA Modules:
  0.0 244.0 jit_solution(12156165754004801051)
XLA Ops:
  2.0 3.7 %pack_rows.1 = (bf16[8,112,768]{2,1,0:T(8,128)(2,1)}, s32[1,512]{1,0:T(1,128)}) custom-call(bf16[512,768]{1,0:T(8,128)(2,1)} %x_ref.1, s32[1,512]{1,0:T(1,128)} %bitcast.76), custom_call_target="tpu_custom_call" | custom-call | tf_op jit(solution)/shard_map/pack_rows/pallas_call | solution.py:56
  5.7 5.8 %all-to-all-start = ((bf16[8,112,768]{2,1,0:T(8,128)(2,1)}), bf16[8,112,768]{2,1,0:T(8,128)(2,1)}, u32[]{:S(2)}, u32[]{:S(2)}) async-start(bf16[8,112,768]{2,1,0:T(8,128)(2,1)} %get-tuple-element.58), calls=%async_computation | async-start | bytes 2752512 | tf_op jit(solution)/shard_map/all_to_all | solution.py:465
  11.5 1.7 collective-permute-start
  13.2 1.2 collective-permute-done
  14.4 3.4 %collective-permute-start.1 = (bf16[2,3,16,256]{3,2,1,0:T(8,128)(2,1)S(1)}, bf16[2,3,16,256]{3,2,1,0:T(8,128)(2,1)S(1)}, u32[]{:S(2)}, u32[]{:S(2)}) collective-permute-start(bf16[2,3,16,256]{3,2,1,0:T(8,128)(2,1)S(1)} %pad_maximum_fusion.4), channel_id=1, source_target_pairs={{0,2},{1,3},{2,0},{3,1},{4,6},{5,7},{6,4},{7,5},{8,10},{9,11},{10,... | collective-permute-start | bytes 147464 | tf_op jit(solution)/shard_map/ppermute | solution.py:445
  17.8 1.5 collective-permute-done.1
  19.3 1.4 collective-permute-start.2
  20.7 2.6 %collective-permute-done.2 = bf16[4,3,16,256]{3,2,1,0:T(8,128)(2,1)S(1)} collective-permute-done((bf16[4,3,16,256]{3,2,1,0:T(8,128)(2,1)S(1)}, bf16[4,3,16,256]{3,2,1,0:T(8,128)(2,1)S(1)}, u32[]{:S(2)}, u32[]{:S(2)}) %collective-permute-start.2) | collective-permute-done | bytes 98336 | tf_op jit(solution)/shard_map/ppermute | solution.py:445
  23.3 3.0 %collective-permute-start.3 = (bf16[8,3,16,256]{3,2,1,0:T(8,128)(2,1)S(1)}, bf16[8,3,16,256]{3,2,1,0:T(8,128)(2,1)S(1)}, u32[]{:S(2)}, u32[]{:S(2)}) collective-permute-start(bf16[8,3,16,256]{3,2,1,0:T(8,128)(2,1)S(1)} %pad_maximum_fusion.2), channel_id=1, source_target_pairs={{0,8},{1,9},{2,10},{3,11},{4,12},{5,13},{6,14},{7,15},{8,0},{9,1},... | collective-permute-start | bytes 589832 | tf_op jit(solution)/shard_map/ppermute | solution.py:445
  26.3 4.1 %collective-permute-done.3 = bf16[8,3,16,256]{3,2,1,0:T(8,128)(2,1)S(1)} collective-permute-done((bf16[8,3,16,256]{3,2,1,0:T(8,128)(2,1)S(1)}, bf16[8,3,16,256]{3,2,1,0:T(8,128)(2,1)S(1)}, u32[]{:S(2)}, u32[]{:S(2)}) %collective-permute-start.3) | collective-permute-done | bytes 196640 | tf_op jit(solution)/shard_map/ppermute | solution.py:445
  31.1 3.9 %land_rows.1 = (s32[8,96]{1,0:T(8,128)}, bf16[2,128,768]{2,1,0:T(8,128)(2,1)}, bf16[2,128,768]{2,1,0:T(8,128)(2,1)}) custom-call(bf16[8,112,768]{2,1,0:T(8,128)(2,1)} %all-to-all-done.arrived_ref, bf16[16,3,16,256]{3,2,1,0:T(8,128)(2,1)} %copy-done.2), custom_call_target="tpu_custom_call" | custom-call | tf_op jit(solution)/shard_map/land_rows/pallas_call | solution.py:89
  35.1 3.4 %collective-permute-start.6 = (bf16[2,128,768]{2,1,0:T(8,128)(2,1)}, bf16[2,128,768]{2,1,0:T(8,128)(2,1)S(1)}, u32[]{:S(2)}, u32[]{:S(2)}) collective-permute-start(bf16[2,128,768]{2,1,0:T(8,128)(2,1)} %get-tuple-element.61), channel_id=1, source_target_pairs={{0,3},{1,2},{2,1},{3,0},{4,7},{5,6},{6,5},{7,4},{8,11},{9,10},{10,... | collective-permute-start | bytes 1179656 | tf_op jit(solution)/shard_map/ppermute | solution.py:445
  38.5 2.3 collective-permute-start.10
  40.8 4.4 %collective-permute-done.6 = bf16[2,128,768]{2,1,0:T(8,128)(2,1)S(1)} collective-permute-done((bf16[2,128,768]{2,1,0:T(8,128)(2,1)}, bf16[2,128,768]{2,1,0:T(8,128)(2,1)S(1)}, u32[]{:S(2)}, u32[]{:S(2)}) %collective-permute-start.6) | collective-permute-done | bytes 393248 | tf_op jit(solution)/shard_map/ppermute | solution.py:445
  46.0 1.7 collective-permute-start.5
  48.2 2.0 collective-permute-start.9
  50.2 1.7 collective-permute-done.7
  52.0 1.4 pad_maximum_fusion.refs_5_.refs_1_
  54.9 1.3 pad_maximum_fusion.1.refs_6_
  56.2 0.8 collective-permute-start.13
  57.0 1.8 collective-permute-start.14
  58.8 0.8 fusion.5
  60.6 1.6 broadcast_in_dim.44.refs_4_
  62.2 9.8 %work_near.1 = (bf16[1,128,768]{2,1,0:T(8,128)(2,1)}, bf16[2,128,768]{2,1,0:T(8,128)(2,1)}, bf16[1,128,768]{2,1,0:T(8,128)(2,1)}, bf16[2,128,768]{2,1,0:T(8,128)...) custom-call(s32[16,4]{1,0:T(8,128)} %copy.27.refs_0_, ...), custom_call_target="tpu_custom_call" | custom-call | flops 3623878656 | bytes 11796480 | tf_op jit(solution)/shard_map/work_near/pallas_call | solution.py:343
  72.7 12.2 %collective-permute-done.12.refs_0_.refs_7_.refs_5_.refs_2_ = bf16[2,4,128,768]{3,2,1,0:T(8,128)(2,1)} collective-permute-done((bf16[2,4,128,768]{3,2,1,0:T(8,128)(2,1)}, bf16[2,4,128,768]{3,2,1,0:T(8,128)(2,1)}, u32[]{:S(2)}, u32[]{:S(2)}) %collective-permute-start.12) | collective-permute-done | bytes 1572896 | tf_op jit(solution)/shard_map/ppermute | solution.py:445
  84.9 5.0 %collective-permute-start.23 = (bf16[2,128,768]{2,1,0:T(8,128)(2,1)}, bf16[2,128,768]{2,1,0:T(8,128)(2,1)S(1)}, u32[]{:S(2)}, u32[]{:S(2)}) collective-permute-start(bf16[2,128,768]{2,1,0:T(8,128)(2,1)} %get-tuple-element.75), channel_id=1, source_target_pairs={{0,3},{1,2},{2,1},{3,0},{4,7},{5,6},{6,5},{7,4},{8,11},{9,10},{10,... | collective-permute-start | bytes 1179656 | tf_op jit(solution)/shard_map/ppermute | solution.py:445
  89.9 2.9 %cut_halves.1 = (bf16[4,128,768]{2,1,0:T(8,128)(2,1)}, bf16[4,128,768]{2,1,0:T(8,128)(2,1)}, bf16[4,128,768]{2,1,0:T(8,128)(2,1)}, bf16[4,128,768]{2,1,0:T(8,128)(2,1)}) custom-call(bf16[2,4,128,768]{3,2,1,0:T(8,128)(2,1)} %collective-permute-done.12.refs_0_.refs_7_.refs_5_.refs_2_, ...), custom_call_target="tpu_custom_call" | custom-call | tf_op jit(solution)/shard_map/cut_halves/pallas_call | solution.py:202
  92.9 1.0 collective-permute-start.16
  94.0 1.3 collective-permute-start.26
  95.3 4.6 %collective-permute-done.23.refs_9_.refs_7_ = bf16[2,128,768]{2,1,0:T(8,128)(2,1)S(1)} collective-permute-done((bf16[2,128,768]{2,1,0:T(8,128)(2,1)}, bf16[2,128,768]{2,1,0:T(8,128)(2,1)S(1)}, u32[]{:S(2)}, u32[]{:S(2)}) %collective-permute-start.23) | collective-permute-done | bytes 393248 | tf_op jit(solution)/shard_map/ppermute | solution.py:445
  100.2 15.7 %work_far.1 = (bf16[2,128,768]{2,1,0:T(8,128)(2,1)}, bf16[4,128,768]{2,1,0:T(8,128)(2,1)}, bf16[2,128,768]{2,1,0:T(8,128)(2,1)}, bf16[4,128,768]{2,1,0:T(8,128)(...) custom-call(s32[16,4]{1,0:T(8,128)} %copy.27.refs_0_, ...), custom_call_target="tpu_custom_call" | custom-call | flops 7247757312 | bytes 17301504 | tf_op jit(solution)/shard_map/work_far/pallas_call | solution.py:343
  116.0 1.5 collective-permute-start.21
  117.5 2.2 collective-permute-start.24
  119.7 1.2 collective-permute-start.29
  120.9 1.5 collective-permute-start.30
  122.5 9.5 %work_last.1 = (bf16[1,128,768]{2,1,0:T(8,128)(2,1)}, bf16[2,128,768]{2,1,0:T(8,128)(2,1)}, bf16[1,128,768]{2,1,0:T(8,128)(2,1)}, bf16[2,128,768]{2,1,0:T(8,128)...) custom-call(s32[16,4]{1,0:T(8,128)} %copy.27.refs_0_, ...), custom_call_target="tpu_custom_call" | custom-call | flops 3623878656 | bytes 11796480 | tf_op jit(solution)/shard_map/work_last/pallas_call | solution.py:343
  132.9 1.7 collective-permute-start.31
  134.6 4.5 %collective-permute-done.30.refs_27_.refs_29_.refs_19_.refs_13_ = bf16[4,128,768]{2,1,0:T(8,128)(2,1)} collective-permute-done((bf16[4,128,768]{2,1,0:T(8,128)(2,1)}, bf16[4,128,768]{2,1,0:T(8,128)(2,1)}, u32[]{:S(2)}, u32[]{:S(2)}) %collective-permute-start.30) | collective-permute-done | bytes 786464 | tf_op jit(solution)/shard_map/ppermute | solution.py:445
  139.1 4.5 %collective-permute-done.22.refs_7_.refs_4_ = bf16[2,128,768]{2,1,0:T(8,128)(2,1)} collective-permute-done((bf16[2,128,768]{2,1,0:T(8,128)(2,1)}, bf16[2,128,768]{2,1,0:T(8,128)(2,1)}, u32[]{:S(2)}, u32[]{:S(2)}) %collective-permute-start.22) | collective-permute-done | bytes 393248 | tf_op jit(solution)/shard_map/ppermute | solution.py:445
  143.6 1.3 collective-permute-done.25.refs_15_.refs_10_
  144.9 2.6 %collective-permute-done.31.refs_31_.refs_22_ = bf16[2,128,768]{2,1,0:T(8,128)(2,1)} collective-permute-done((bf16[2,128,768]{2,1,0:T(8,128)(2,1)}, bf16[2,128,768]{2,1,0:T(8,128)(2,1)}, u32[]{:S(2)}, u32[]{:S(2)}) %collective-permute-start.31) | collective-permute-done | bytes 393248 | tf_op jit(solution)/shard_map/ppermute | solution.py:445
  147.5 4.4 %merge_1.1 = (bf16[4,128,768]{2,1,0:T(8,128)(2,1)}, bf16[4,128,768]{2,1,0:T(8,128)(2,1)}, bf16[4,128,768]{2,1,0:T(8,128)(2,1)}, bf16[4,128,768]{2,1,0:T(8,128)(2,1)}) custom-call(bf16[1,128,768]{2,1,0:T(8,128)(2,1)} %get-tuple-element.69.refs_0_, bf16[2,128,768]{2,1,0:T(8,128)(2,1)} %copy-done.3, bf16[2,128,768]{2,1,0:T(8,128)(2,1)} %get-tuple-element.70.refs_2_.refs_4_, ...), custom_call_target="tpu_custom_call" | custom-call | bytes 9437184 | tf_op jit(solution)/shard_map/merge_1/pallas_call | solution.py:152
  152.4 0.9 collective-permute-start.34
  153.4 11.7 %work_kept.1 = (bf16[4,128,768]{2,1,0:T(8,128)(2,1)}, bf16[4,128,768]{2,1,0:T(8,128)(2,1)}, bf16[4,128,768]{2,1,0:T(8,128)(2,1)}, bf16[4,128,768]{2,1,0:T(8,128)(2,1)}, bf16[8,2,256,256]{3,2,1,0:T(8,128)(2,1)}) custom-call(s32[16,4]{1,0:T(8,128)} %copy.27.refs_0_, s32[2,8]{1,0:T(2,128)} %constant.79.clone.refs_1_, bf16[16,3,16,256]{3,2,1,0:T(8,128)(2,1)} %copy-done.2, ...), custom_call_target="tpu_custom_call" | custom-call | flops 4831838208 | bytes 13631488 | tf_op jit(solution)/shard_map/work_kept/pallas_call | solution.py:343
  165.1 0.7 collective-permute-done.34.refs_14_.refs_17_.refs_10_.refs_13_
  166.0 3.6 %merge_2.1 = (bf16[2,128,768]{2,1,0:T(8,128)(2,1)}, bf16[2,128,768]{2,1,0:T(8,128)(2,1)}, bf16[2,128,768]{2,1,0:T(8,128)(2,1)}, bf16[2,128,768]{2,1,0:T(8,128)(2,1)}) custom-call(bf16[4,128,768]{2,1,0:T(8,128)(2,1)} %get-tuple-element.67.refs_0_.refs_3_.refs_1_, bf16[4,128,768]{2,1,0:T(8,128)(2,1)} %copy-done, bf16[4,128,768]{2,1,0:T(8,128)(2,1)} %copy-done.1, ...), custom_call_target="tpu_custom_call" | custom-call | bytes 6291456 | tf_op jit(solution)/shard_map/merge_2/pallas_call | solution.py:152
  169.6 1.4 collective-permute-start.36
  171.0 1.8 collective-permute-start.37
  172.8 1.2 collective-permute-start.38
  174.0 2.5 %collective-permute-start.39 = (bf16[2,128,768]{2,1,0:T(8,128)(2,1)}, bf16[2,128,768]{2,1,0:T(8,128)(2,1)}, u32[]{:S(2)}, u32[]{:S(2)}) collective-permute-start(bf16[2,128,768]{2,1,0:T(8,128)(2,1)} %get-tuple-element.102), channel_id=1, source_target_pairs={{0,3},{1,2},{2,1},{3,0},{4,7},{5,6},{6,5},{7,4},{8,11},{9,10},{10,... | collective-permute-start | bytes 1179656 | tf_op jit(solution)/shard_map/ppermute | solution.py:445
  176.4 4.8 %collective-permute-done.36.refs_3_.refs_4_ = bf16[2,128,768]{2,1,0:T(8,128)(2,1)S(1)} collective-permute-done((bf16[2,128,768]{2,1,0:T(8,128)(2,1)}, bf16[2,128,768]{2,1,0:T(8,128)(2,1)S(1)}, u32[]{:S(2)}, u32[]{:S(2)}) %collective-permute-start.36) | collective-permute-done | bytes 393248 | tf_op jit(solution)/shard_map/ppermute | solution.py:445
  181.2 0.9 collective-permute-done.39.refs_15_.refs_19_
  182.1 2.9 %merge_3.1 = (bf16[1,128,768]{2,1,0:T(8,128)(2,1)}, bf16[1,128,768]{2,1,0:T(8,128)(2,1)}, bf16[1,128,768]{2,1,0:T(8,128)(2,1)}, bf16[1,128,768]{2,1,0:T(8,128)(2,1)}) custom-call(bf16[4,128,768]{2,1,0:T(8,128)(2,1)} %get-tuple-element.67.refs_0_.refs_3_.refs_1_, bf16[4,128,768]{2,1,0:T(8,128)(2,1)} %copy-done, bf16[4,128,768]{2,1,0:T(8,128)(2,1)} %copy-done.1, ...), custom_call_target="tpu_custom_call" | custom-call | bytes 3932160 | tf_op jit(solution)/shard_map/merge_3/pallas_call | solution.py:152
  185.0 1.7 collective-permute-start.40
  186.7 2.8 %collective-permute-start.42 = (bf16[1,128,768]{2,1,0:T(8,128)(2,1)}, bf16[1,128,768]{2,1,0:T(8,128)(2,1)S(1)}, u32[]{:S(2)}, u32[]{:S(2)}) collective-permute-start(bf16[1,128,768]{2,1,0:T(8,128)(2,1)} %get-tuple-element.105), channel_id=1, source_target_pairs={{0,3},{1,2},{2,1},{3,0},{4,7},{5,6},{6,5},{7,4},{8,11},{9,10},{10,... | collective-permute-start | bytes 589832 | tf_op jit(solution)/shard_map/ppermute | solution.py:445
  189.5 1.1 collective-permute-start.43
  190.6 0.8 collective-permute-done.40.refs_5_
  191.4 2.4 collective-permute-done.41.refs_10_
  193.8 2.9 %collective-permute-done.43.refs_20_ = bf16[1,128,768]{2,1,0:T(8,128)(2,1)S(1)} collective-permute-done((bf16[1,128,768]{2,1,0:T(8,128)(2,1)}, bf16[1,128,768]{2,1,0:T(8,128)(2,1)S(1)}, u32[]{:S(2)}, u32[]{:S(2)}) %collective-permute-start.43) | collective-permute-done | bytes 196640 | tf_op jit(solution)/shard_map/ppermute | solution.py:445
  197.4 4.6 %leave_rows.1 = bf16[8,96,768]{2,1,0:T(8,128)(2,1)} custom-call(s32[8,96]{1,0:T(8,128)} %get-tuple-element.60.refs_0_, bf16[4,128,768]{2,1,0:T(8,128)(2,1)} %get-tuple-element.67.refs_0_.refs_3_.refs_1_, bf16[2,128,768]{2,1,0:T(8,128)(2,1)} %copy-done.3, bf16[4,128,768]{2,1,0:T(8,128)(2,1)} %copy-done.1, bf16[2,128,768]{2,1,0:T(8,128)(2,1)} %copy-done.5, ...), custom_call_target="tpu_custom_call" | custom-call | tf_op jit(solution)/shard_map/leave_rows/pallas_call | solution.py:122
  202.0 21.4 %all-to-all-start.1 = ((bf16[8,96,768]{2,1,0:T(8,128)(2,1)}), bf16[8,96,768]{2,1,0:T(8,128)(2,1)}, u32[]{:S(2)}, u32[]{:S(2)}) async-start(bf16[8,96,768]{2,1,0:T(8,128)(2,1)} %leave_rows.1), calls=%async_computation.1 | async-start | bytes 2359296 | tf_op jit(solution)/shard_map/all_to_all | solution.py:582
  223.4 15.1 %panel_grad.1 = bf16[16,256,768]{2,1,0:T(8,128)(2,1)} custom-call(s32[16,4]{1,0:T(8,128)} %copy.27.refs_0_, bf16[2,4,128,768]{3,2,1,0:T(8,128)(2,1)} %pad_maximum_fusion.refs_5_.refs_1_, bf16[2,4,128,768]{3,2,1,0:T(8,128)(2,1)} %collective-permute-done.12.refs_0_.refs_7_.refs_5_.refs_2_, ...), custom_call_target="tpu_custom_call" | custom-call | flops 6442450944 | bytes 27262976 | tf_op jit(solution)/shard_map/panel_grad/pallas_call | solution.py:417
  238.5 1.5 all-to-all-done.1.back_ref
  240.0 4.0 %home_rows.1 = bf16[512,768]{1,0:T(8,128)(2,1)} custom-call(bf16[8,96,768]{2,1,0:T(8,128)(2,1)} %all-to-all-done.1.back_ref, s32[1,512]{1,0:T(1,128)} %get-tuple-element.107.rank_ref), custom_call_target="tpu_custom_call" | custom-call | tf_op jit(solution)/shard_map/home_rows/pallas_call | solution.py:177
  (97 shorter events, 9.4 us)
Async XLA Ops:
  5.7 24.7 %all-to-all-start = ((bf16[8,112,768]{2,1,0:T(8,128)(2,1)}), bf16[8,112,768]{2,1,0:T(8,128)(2,1)}, u32[]{:S(2)}, u32[]{:S(2)}) async-start(bf16[8,112,768]{2,1,0:T(8,128)(2,1)} %get-tuple-element.58), calls=%async_computation | async-start | bytes 2752512 | tf_op jit(solution)/shard_map/all_to_all | solution.py:465
  11.5 2.9 %collective-permute-start = (bf16[1,3,16,256]{3,2,1,0:T(8,128)(2,1)S(1)}, bf16[1,3,16,256]{3,2,1,0:T(8,128)(2,1)S(1)}, u32[]{:S(2)}, u32[]{:S(2)}) collective-permute-start(bf16[1,3,16,256]{3,2,1,0:T(8,128)(2,1)S(1)} %fusion.2), channel_id=1, source_target_pairs={{0,1},{1,0},{2,3},{3,2},{4,5},{5,4},{6,7},{7,6},{8,9},{9,8},{10,11... | collective-permute-start | bytes 73736 | tf_op jit(solution)/shard_map/ppermute | solution.py:445
  14.4 4.9 %collective-permute-start.1 = (bf16[2,3,16,256]{3,2,1,0:T(8,128)(2,1)S(1)}, bf16[2,3,16,256]{3,2,1,0:T(8,128)(2,1)S(1)}, u32[]{:S(2)}, u32[]{:S(2)}) collective-permute-start(bf16[2,3,16,256]{3,2,1,0:T(8,128)(2,1)S(1)} %pad_maximum_fusion.4), channel_id=1, source_target_pairs={{0,2},{1,3},{2,0},{3,1},{4,6},{5,7},{6,4},{7,5},{8,10},{9,11},{10,... | collective-permute-start | bytes 147464 | tf_op jit(solution)/shard_map/ppermute | solution.py:445
  19.3 3.9 %collective-permute-start.2 = (bf16[4,3,16,256]{3,2,1,0:T(8,128)(2,1)S(1)}, bf16[4,3,16,256]{3,2,1,0:T(8,128)(2,1)S(1)}, u32[]{:S(2)}, u32[]{:S(2)}) collective-permute-start(bf16[4,3,16,256]{3,2,1,0:T(8,128)(2,1)S(1)} %pad_maximum_fusion.3), channel_id=1, source_target_pairs={{0,4},{1,5},{2,6},{3,7},{4,0},{5,1},{6,2},{7,3},{8,12},{9,13},{10,... | collective-permute-start | bytes 294920 | tf_op jit(solution)/shard_map/ppermute | solution.py:445
  23.3 7.1 %collective-permute-start.3 = (bf16[8,3,16,256]{3,2,1,0:T(8,128)(2,1)S(1)}, bf16[8,3,16,256]{3,2,1,0:T(8,128)(2,1)S(1)}, u32[]{:S(2)}, u32[]{:S(2)}) collective-permute-start(bf16[8,3,16,256]{3,2,1,0:T(8,128)(2,1)S(1)} %pad_maximum_fusion.2), channel_id=1, source_target_pairs={{0,8},{1,9},{2,10},{3,11},{4,12},{5,13},{6,14},{7,15},{8,0},{9,1},... | collective-permute-start | bytes 589832 | tf_op jit(solution)/shard_map/ppermute | solution.py:445
  30.4 0.8 copy-start.2
  35.1 16.9 %copy-start.8 = (bf16[2,128,768]{2,1,0:T(8,128)(2,1)S(1)}, bf16[2,128,768]{2,1,0:T(8,128)(2,1)}, u32[]{:S(2)}) copy-start(bf16[2,128,768]{2,1,0:T(8,128)(2,1)} %get-tuple-element.61) | copy-start | bytes 1179652
  35.1 10.1 %collective-permute-start.6 = (bf16[2,128,768]{2,1,0:T(8,128)(2,1)}, bf16[2,128,768]{2,1,0:T(8,128)(2,1)S(1)}, u32[]{:S(2)}, u32[]{:S(2)}) collective-permute-start(bf16[2,128,768]{2,1,0:T(8,128)(2,1)} %get-tuple-element.61), channel_id=1, source_target_pairs={{0,3},{1,2},{2,1},{3,0},{4,7},{5,6},{6,5},{7,4},{8,11},{9,10},{10,... | collective-permute-start | bytes 1179656 | tf_op jit(solution)/shard_map/ppermute | solution.py:445
  38.5 7.5 %collective-permute-start.4 = (bf16[2,128,768]{2,1,0:T(8,128)(2,1)}, bf16[2,128,768]{2,1,0:T(8,128)(2,1)S(1)}, u32[]{:S(2)}, u32[]{:S(2)}) collective-permute-start(bf16[2,128,768]{2,1,0:T(8,128)(2,1)} %get-tuple-element.61), channel_id=1, source_target_pairs={{0,1},{1,0},{2,3},{3,2},{4,5},{5,4},{6,7},{7,6},{8,9},{9,8},{10,11... | collective-permute-start | bytes 1179656 | tf_op jit(solution)/shard_map/ppermute | solution.py:445
  38.5 9.2 %collective-permute-start.10 = (bf16[2,128,768]{2,1,0:T(8,128)(2,1)}, bf16[2,128,768]{2,1,0:T(8,128)(2,1)S(1)}, u32[]{:S(2)}, u32[]{:S(2)}) collective-permute-start(bf16[2,128,768]{2,1,0:T(8,128)(2,1)} %get-tuple-element.62), channel_id=1, source_target_pairs={{0,12},{1,13},{2,14},{3,15},{4,8},{5,9},{6,10},{7,11},{8,4},{9,5},... | collective-permute-start | bytes 1179656 | tf_op jit(solution)/shard_map/ppermute | solution.py:445
  40.8 7.4 %collective-permute-start.8 = (bf16[2,128,768]{2,1,0:T(8,128)(2,1)}, bf16[2,128,768]{2,1,0:T(8,128)(2,1)S(1)}, u32[]{:S(2)}, u32[]{:S(2)}) collective-permute-start(bf16[2,128,768]{2,1,0:T(8,128)(2,1)} %get-tuple-element.62), channel_id=1, source_target_pairs={{0,4},{1,5},{2,6},{3,7},{4,0},{5,1},{6,2},{7,3},{8,12},{9,13},{10,... | collective-permute-start | bytes 1179656 | tf_op jit(solution)/shard_map/ppermute | solution.py:445
  45.2 6.7 %collective-permute-start.7 = (bf16[128,768]{1,0:T(8,128)(2,1)S(1)}, bf16[128,768]{1,0:T(8,128)(2,1)S(1)}, u32[]{:S(2)}, u32[]{:S(2)}) collective-permute-start(bf16[128,768]{1,0:T(8,128)(2,1)S(1)} %slice_bitcast_fusion.2), channel_id=1, source_target_pairs={{0,1},{1,0},{2,3},{3,2},{4,5},{5,4},{6,7},{7,6},{8,9},{9,8},{10,11... | collective-permute-start | bytes 589832 | tf_op jit(solution)/shard_map/ppermute | solution.py:445
  46.0 5.9 %collective-permute-start.5 = (bf16[128,768]{1,0:T(8,128)(2,1)S(1)}, bf16[128,768]{1,0:T(8,128)(2,1)S(1)}, u32[]{:S(2)}, u32[]{:S(2)}) collective-permute-start(bf16[128,768]{1,0:T(8,128)(2,1)S(1)} %slice_bitcast_fusion.3), channel_id=1, source_target_pairs={{0,3},{1,2},{2,1},{3,0},{4,7},{5,6},{6,5},{7,4},{8,11},{9,10},{10,... | collective-permute-start | bytes 589832 | tf_op jit(solution)/shard_map/ppermute | solution.py:445
  47.7 7.1 %collective-permute-start.11 = (bf16[128,768]{1,0:T(8,128)(2,1)S(1)}, bf16[128,768]{1,0:T(8,128)(2,1)S(1)}, u32[]{:S(2)}, u32[]{:S(2)}) collective-permute-start(bf16[128,768]{1,0:T(8,128)(2,1)S(1)} %slice_bitcast_fusion), channel_id=1, source_target_pairs={{0,4},{1,5},{2,6},{3,7},{4,0},{5,1},{6,2},{7,3},{8,12},{9,13},{10,... | collective-permute-start | bytes 589832 | tf_op jit(solution)/shard_map/ppermute | solution.py:445
  48.2 6.6 %collective-permute-start.9 = (bf16[128,768]{1,0:T(8,128)(2,1)S(1)}, bf16[128,768]{1,0:T(8,128)(2,1)S(1)}, u32[]{:S(2)}, u32[]{:S(2)}) collective-permute-start(bf16[128,768]{1,0:T(8,128)(2,1)S(1)} %slice_bitcast_fusion.1), channel_id=1, source_target_pairs={{0,12},{1,13},{2,14},{3,15},{4,8},{5,9},{6,10},{7,11},{8,4},{9,5},... | collective-permute-start | bytes 589832 | tf_op jit(solution)/shard_map/ppermute | solution.py:445
  52.0 2.9 %copy-start.7 = (bf16[2,128,768]{2,1,0:T(8,128)(2,1)S(1)}, bf16[2,128,768]{2,1,0:T(8,128)(2,1)}, u32[]{:S(2)}) copy-start(bf16[2,128,768]{2,1,0:T(8,128)(2,1)} %get-tuple-element.62) | copy-start | bytes 1179652
  53.4 31.5 %collective-permute-start.12 = (bf16[2,4,128,768]{3,2,1,0:T(8,128)(2,1)}, bf16[2,4,128,768]{3,2,1,0:T(8,128)(2,1)}, u32[]{:S(2)}, u32[]{:S(2)}) collective-permute-start(bf16[2,4,128,768]{3,2,1,0:T(8,128)(2,1)} %pad_maximum_fusion.refs_5_.refs_1_), channel_id=1, source_target_pairs={{0,4},{1,5},{2,6},{3,7},{4,0},{5,1},{6,2},{7,3},{8,12},{9,13},{10,... | collective-permute-start | bytes 4718600 | tf_op jit(solution)/shard_map/ppermute | solution.py:445
  54.9 5.7 %copy-start.13 = (bf16[16,256]{1,0:T(8,128)(2,1)S(1)}, bf16[16,256]{1,0:T(8,128)(2,1)}, u32[]{:S(2)}) copy-start(bf16[16,256]{1,0:T(8,128)(2,1)} %param.13) | copy-start | bytes 24580
  56.2 33.7 %collective-permute-start.13 = (bf16[2,4,128,768]{3,2,1,0:T(8,128)(2,1)}, bf16[2,4,128,768]{3,2,1,0:T(8,128)(2,1)}, u32[]{:S(2)}, u32[]{:S(2)}) collective-permute-start(bf16[2,4,128,768]{3,2,1,0:T(8,128)(2,1)} %pad_maximum_fusion.1.refs_6_), channel_id=1, source_target_pairs={{0,1},{1,0},{2,3},{3,2},{4,5},{5,4},{6,7},{7,6},{8,9},{9,8},{10,11... | collective-permute-start | bytes 4718600 | tf_op jit(solution)/shard_map/ppermute | solution.py:445
  57.0 32.9 %collective-permute-start.14 = (bf16[2,4,128,768]{3,2,1,0:T(8,128)(2,1)}, bf16[2,4,128,768]{3,2,1,0:T(8,128)(2,1)}, u32[]{:S(2)}, u32[]{:S(2)}) collective-permute-start(bf16[2,4,128,768]{3,2,1,0:T(8,128)(2,1)} %pad_maximum_fusion.refs_5_.refs_1_), channel_id=1, source_target_pairs={{0,12},{1,13},{2,14},{3,15},{4,8},{5,9},{6,10},{7,11},{8,4},{9,5},... | collective-permute-start | bytes 4718600 | tf_op jit(solution)/shard_map/ppermute | solution.py:445
  58.8 31.1 %collective-permute-start.15 = (bf16[2,4,128,768]{3,2,1,0:T(8,128)(2,1)}, bf16[2,4,128,768]{3,2,1,0:T(8,128)(2,1)}, u32[]{:S(2)}, u32[]{:S(2)}) collective-permute-start(bf16[2,4,128,768]{3,2,1,0:T(8,128)(2,1)} %pad_maximum_fusion.1.refs_6_), channel_id=1, source_target_pairs={{0,3},{1,2},{2,1},{3,0},{4,7},{5,6},{6,5},{7,4},{8,11},{9,10},{10,... | collective-permute-start | bytes 4718600 | tf_op jit(solution)/shard_map/ppermute | solution.py:445
  72.0 23.3 %collective-permute-start.20 = (bf16[2,128,768]{2,1,0:T(8,128)(2,1)}, bf16[2,128,768]{2,1,0:T(8,128)(2,1)S(1)}, u32[]{:S(2)}, u32[]{:S(2)}) collective-permute-start(bf16[2,128,768]{2,1,0:T(8,128)(2,1)} %get-tuple-element.68), channel_id=1, source_target_pairs={{0,1},{1,0},{2,3},{3,2},{4,5},{5,4},{6,7},{7,6},{8,9},{9,8},{10,11... | collective-permute-start | bytes 1179656 | tf_op jit(solution)/shard_map/ppermute | solution.py:445
  84.9 15.0 %collective-permute-start.23 = (bf16[2,128,768]{2,1,0:T(8,128)(2,1)}, bf16[2,128,768]{2,1,0:T(8,128)(2,1)S(1)}, u32[]{:S(2)}, u32[]{:S(2)}) collective-permute-start(bf16[2,128,768]{2,1,0:T(8,128)(2,1)} %get-tuple-element.75), channel_id=1, source_target_pairs={{0,3},{1,2},{2,1},{3,0},{4,7},{5,6},{6,5},{7,4},{8,11},{9,10},{10,... | collective-permute-start | bytes 1179656 | tf_op jit(solution)/shard_map/ppermute | solution.py:445
  92.9 24.7 %collective-permute-start.16 = (bf16[4,128,768]{2,1,0:T(8,128)(2,1)}, bf16[4,128,768]{2,1,0:T(8,128)(2,1)}, u32[]{:S(2)}, u32[]{:S(2)}) collective-permute-start(bf16[4,128,768]{2,1,0:T(8,128)(2,1)} %get-tuple-element.63), channel_id=1, source_target_pairs={{0,12},{1,13},{2,14},{3,15},{4,8},{5,9},{6,10},{7,11},{8,4},{9,5},... | collective-permute-start | bytes 2359304 | tf_op jit(solution)/shard_map/ppermute | solution.py:445
  93.8 25.9 %collective-permute-start.17 = (bf16[4,128,768]{2,1,0:T(8,128)(2,1)}, bf16[4,128,768]{2,1,0:T(8,128)(2,1)}, u32[]{:S(2)}, u32[]{:S(2)}) collective-permute-start(bf16[4,128,768]{2,1,0:T(8,128)(2,1)} %get-tuple-element.64), channel_id=1, source_target_pairs={{0,4},{1,5},{2,6},{3,7},{4,0},{5,1},{6,2},{7,3},{8,12},{9,13},{10,... | collective-permute-start | bytes 2359304 | tf_op jit(solution)/shard_map/ppermute | solution.py:445
  94.0 22.0 %collective-permute-start.26 = (bf16[2,128,768]{2,1,0:T(8,128)(2,1)}, bf16[2,128,768]{2,1,0:T(8,128)(2,1)}, u32[]{:S(2)}, u32[]{:S(2)}) collective-permute-start(bf16[2,128,768]{2,1,0:T(8,128)(2,1)} %get-tuple-element.81), channel_id=1, source_target_pairs={{0,4},{1,5},{2,6},{3,7},{4,0},{5,1},{6,2},{7,3},{8,12},{9,13},{10,... | collective-permute-start | bytes 1179656 | tf_op jit(solution)/shard_map/ppermute | solution.py:445
  95.3 20.7 %copy-start.3 = (bf16[2,128,768]{2,1,0:T(8,128)(2,1)}, bf16[2,128,768]{2,1,0:T(8,128)(2,1)S(1)}, u32[]{:S(2)}) copy-start(bf16[2,128,768]{2,1,0:T(8,128)(2,1)S(1)} %collective-permute-done.20.refs_1_.refs_2_) | copy-start | bytes 1179652
  95.3 24.4 %collective-permute-start.18 = (bf16[4,128,768]{2,1,0:T(8,128)(2,1)}, bf16[4,128,768]{2,1,0:T(8,128)(2,1)}, u32[]{:S(2)}, u32[]{:S(2)}) collective-permute-start(bf16[4,128,768]{2,1,0:T(8,128)(2,1)} %get-tuple-element.65), channel_id=1, source_target_pairs={{0,3},{1,2},{2,1},{3,0},{4,7},{5,6},{6,5},{7,4},{8,11},{9,10},{10,... | collective-permute-start | bytes 2359304 | tf_op jit(solution)/shard_map/ppermute | solution.py:445
  99.9 16.0 %copy-start.4 = (bf16[2,128,768]{2,1,0:T(8,128)(2,1)}, bf16[2,128,768]{2,1,0:T(8,128)(2,1)S(1)}, u32[]{:S(2)}) copy-start(bf16[2,128,768]{2,1,0:T(8,128)(2,1)S(1)} %collective-permute-done.23.refs_9_.refs_7_) | copy-start | bytes 1179652
  99.9 21.0 %collective-permute-start.19 = (bf16[4,128,768]{2,1,0:T(8,128)(2,1)}, bf16[4,128,768]{2,1,0:T(8,128)(2,1)}, u32[]{:S(2)}, u32[]{:S(2)}) collective-permute-start(bf16[4,128,768]{2,1,0:T(8,128)(2,1)} %get-tuple-element.66), channel_id=1, source_target_pairs={{0,1},{1,0},{2,3},{3,2},{4,5},{5,4},{6,7},{7,6},{8,9},{9,8},{10,11... | collective-permute-start | bytes 2359304 | tf_op jit(solution)/shard_map/ppermute | solution.py:445
  116.0 16.1 %collective-permute-start.21 = (bf16[4,128,768]{2,1,0:T(8,128)(2,1)}, bf16[4,128,768]{2,1,0:T(8,128)(2,1)S(1)}, u32[]{:S(2)}, u32[]{:S(2)}) collective-permute-start(bf16[4,128,768]{2,1,0:T(8,128)(2,1)} %get-tuple-element.71), channel_id=1, source_target_pairs={{0,1},{1,0},{2,3},{3,2},{4,5},{5,4},{6,7},{7,6},{8,9},{9,8},{10,11... | collective-permute-start | bytes 2359304 | tf_op jit(solution)/shard_map/ppermute | solution.py:445
  117.5 15.0 %collective-permute-start.24 = (bf16[4,128,768]{2,1,0:T(8,128)(2,1)}, bf16[4,128,768]{2,1,0:T(8,128)(2,1)}, u32[]{:S(2)}, u32[]{:S(2)}) collective-permute-start(bf16[4,128,768]{2,1,0:T(8,128)(2,1)} %get-tuple-element.77), channel_id=1, source_target_pairs={{0,3},{1,2},{2,1},{3,0},{4,7},{5,6},{6,5},{7,4},{8,11},{9,10},{10,... | collective-permute-start | bytes 2359304 | tf_op jit(solution)/shard_map/ppermute | solution.py:445
  119.7 13.2 %collective-permute-start.27 = (bf16[4,128,768]{2,1,0:T(8,128)(2,1)}, bf16[4,128,768]{2,1,0:T(8,128)(2,1)}, u32[]{:S(2)}, u32[]{:S(2)}) collective-permute-start(bf16[4,128,768]{2,1,0:T(8,128)(2,1)} %get-tuple-element.83), channel_id=1, source_target_pairs={{0,4},{1,5},{2,6},{3,7},{4,0},{5,1},{6,2},{7,3},{8,12},{9,13},{10,... | collective-permute-start | bytes 2359304 | tf_op jit(solution)/shard_map/ppermute | solution.py:445
  119.7 12.3 %collective-permute-start.29 = (bf16[2,128,768]{2,1,0:T(8,128)(2,1)}, bf16[2,128,768]{2,1,0:T(8,128)(2,1)}, u32[]{:S(2)}, u32[]{:S(2)}) collective-permute-start(bf16[2,128,768]{2,1,0:T(8,128)(2,1)} %get-tuple-element.87), channel_id=1, source_target_pairs={{0,12},{1,13},{2,14},{3,15},{4,8},{5,9},{6,10},{7,11},{8,4},{9,5},... | collective-permute-start | bytes 1179656 | tf_op jit(solution)/shard_map/ppermute | solution.py:445
  120.9 18.2 %collective-permute-start.30 = (bf16[4,128,768]{2,1,0:T(8,128)(2,1)}, bf16[4,128,768]{2,1,0:T(8,128)(2,1)}, u32[]{:S(2)}, u32[]{:S(2)}) collective-permute-start(bf16[4,128,768]{2,1,0:T(8,128)(2,1)} %get-tuple-element.89), channel_id=1, source_target_pairs={{0,12},{1,13},{2,14},{3,15},{4,8},{5,9},{6,10},{7,11},{8,4},{9,5},... | collective-permute-start | bytes 2359304 | tf_op jit(solution)/shard_map/ppermute | solution.py:445
  132.0 11.6 %collective-permute-start.22 = (bf16[2,128,768]{2,1,0:T(8,128)(2,1)}, bf16[2,128,768]{2,1,0:T(8,128)(2,1)}, u32[]{:S(2)}, u32[]{:S(2)}) collective-permute-start(bf16[2,128,768]{2,1,0:T(8,128)(2,1)} %get-tuple-element.73), channel_id=1, source_target_pairs={{0,1},{1,0},{2,3},{3,2},{4,5},{5,4},{6,7},{7,6},{8,9},{9,8},{10,11... | collective-permute-start | bytes 1179656 | tf_op jit(solution)/shard_map/ppermute | solution.py:445
  132.1 15.4 %copy-start = (bf16[4,128,768]{2,1,0:T(8,128)(2,1)}, bf16[4,128,768]{2,1,0:T(8,128)(2,1)S(1)}, u32[]{:S(2)}) copy-start(bf16[4,128,768]{2,1,0:T(8,128)(2,1)S(1)} %collective-permute-done.21.refs_3_.refs_5_.refs_1_) | copy-start | bytes 2359300
  132.1 12.8 %collective-permute-start.25 = (bf16[2,128,768]{2,1,0:T(8,128)(2,1)}, bf16[2,128,768]{2,1,0:T(8,128)(2,1)}, u32[]{:S(2)}, u32[]{:S(2)}) collective-permute-start(bf16[2,128,768]{2,1,0:T(8,128)(2,1)} %get-tuple-element.79), channel_id=1, source_target_pairs={{0,3},{1,2},{2,1},{3,0},{4,7},{5,6},{6,5},{7,4},{8,11},{9,10},{10,... | collective-permute-start | bytes 1179656 | tf_op jit(solution)/shard_map/ppermute | solution.py:445
  132.5 12.4 %collective-permute-start.28 = (bf16[2,128,768]{2,1,0:T(8,128)(2,1)}, bf16[2,128,768]{2,1,0:T(8,128)(2,1)}, u32[]{:S(2)}, u32[]{:S(2)}) collective-permute-start(bf16[2,128,768]{2,1,0:T(8,128)(2,1)} %get-tuple-element.85), channel_id=1, source_target_pairs={{0,4},{1,5},{2,6},{3,7},{4,0},{5,1},{6,2},{7,3},{8,12},{9,13},{10,... | collective-permute-start | bytes 1179656 | tf_op jit(solution)/shard_map/ppermute | solution.py:445
  132.9 14.7 %collective-permute-start.31 = (bf16[2,128,768]{2,1,0:T(8,128)(2,1)}, bf16[2,128,768]{2,1,0:T(8,128)(2,1)}, u32[]{:S(2)}, u32[]{:S(2)}) collective-permute-start(bf16[2,128,768]{2,1,0:T(8,128)(2,1)} %get-tuple-element.91), channel_id=1, source_target_pairs={{0,12},{1,13},{2,14},{3,15},{4,8},{5,9},{6,10},{7,11},{8,4},{9,5},... | collective-permute-start | bytes 1179656 | tf_op jit(solution)/shard_map/ppermute | solution.py:445
  152.0 13.1 %collective-permute-start.32 = (bf16[4,128,768]{2,1,0:T(8,128)(2,1)}, bf16[4,128,768]{2,1,0:T(8,128)(2,1)S(1)}, u32[]{:S(2)}, u32[]{:S(2)}) collective-permute-start(bf16[4,128,768]{2,1,0:T(8,128)(2,1)} %get-tuple-element.92), channel_id=1, source_target_pairs={{0,3},{1,2},{2,1},{3,0},{4,7},{5,6},{6,5},{7,4},{8,11},{9,10},{10,... | collective-permute-start | bytes 2359304 | tf_op jit(solution)/shard_map/ppermute | solution.py:445
  152.3 12.8 %collective-permute-start.33 = (bf16[4,128,768]{2,1,0:T(8,128)(2,1)}, bf16[4,128,768]{2,1,0:T(8,128)(2,1)}, u32[]{:S(2)}, u32[]{:S(2)}) collective-permute-start(bf16[4,128,768]{2,1,0:T(8,128)(2,1)} %get-tuple-element.94), channel_id=1, source_target_pairs={{0,1},{1,0},{2,3},{3,2},{4,5},{5,4},{6,7},{7,6},{8,9},{9,8},{10,11... | collective-permute-start | bytes 2359304 | tf_op jit(solution)/shard_map/ppermute | solution.py:445
  152.4 13.4 %collective-permute-start.34 = (bf16[4,128,768]{2,1,0:T(8,128)(2,1)}, bf16[4,128,768]{2,1,0:T(8,128)(2,1)}, u32[]{:S(2)}, u32[]{:S(2)}) collective-permute-start(bf16[4,128,768]{2,1,0:T(8,128)(2,1)} %get-tuple-element.96), channel_id=1, source_target_pairs={{0,12},{1,13},{2,14},{3,15},{4,8},{5,9},{6,10},{7,11},{8,4},{9,5},... | collective-permute-start | bytes 2359304 | tf_op jit(solution)/shard_map/ppermute | solution.py:445
  153.3 12.5 %collective-permute-start.35 = (bf16[4,128,768]{2,1,0:T(8,128)(2,1)}, bf16[4,128,768]{2,1,0:T(8,128)(2,1)}, u32[]{:S(2)}, u32[]{:S(2)}) collective-permute-start(bf16[4,128,768]{2,1,0:T(8,128)(2,1)} %get-tuple-element.98), channel_id=1, source_target_pairs={{0,4},{1,5},{2,6},{3,7},{4,0},{5,1},{6,2},{7,3},{8,12},{9,13},{10,... | collective-permute-start | bytes 2359304 | tf_op jit(solution)/shard_map/ppermute | solution.py:445
  165.1 0.9 copy-start.1
  169.6 11.6 %collective-permute-start.36 = (bf16[2,128,768]{2,1,0:T(8,128)(2,1)}, bf16[2,128,768]{2,1,0:T(8,128)(2,1)S(1)}, u32[]{:S(2)}, u32[]{:S(2)}) collective-permute-start(bf16[2,128,768]{2,1,0:T(8,128)(2,1)} %get-tuple-element.99), channel_id=1, source_target_pairs={{0,4},{1,5},{2,6},{3,7},{4,0},{5,1},{6,2},{7,3},{8,12},{9,13},{10,... | collective-permute-start | bytes 1179656 | tf_op jit(solution)/shard_map/ppermute | solution.py:445
  171.0 10.2 %collective-permute-start.37 = (bf16[2,128,768]{2,1,0:T(8,128)(2,1)}, bf16[2,128,768]{2,1,0:T(8,128)(2,1)S(1)}, u32[]{:S(2)}, u32[]{:S(2)}) collective-permute-start(bf16[2,128,768]{2,1,0:T(8,128)(2,1)} %get-tuple-element.100), channel_id=1, source_target_pairs={{0,12},{1,13},{2,14},{3,15},{4,8},{5,9},{6,10},{7,11},{8,4},{9,5},... | collective-permute-start | bytes 1179656 | tf_op jit(solution)/shard_map/ppermute | solution.py:445
  172.8 8.4 %collective-permute-start.38 = (bf16[2,128,768]{2,1,0:T(8,128)(2,1)}, bf16[2,128,768]{2,1,0:T(8,128)(2,1)}, u32[]{:S(2)}, u32[]{:S(2)}) collective-permute-start(bf16[2,128,768]{2,1,0:T(8,128)(2,1)} %get-tuple-element.101), channel_id=1, source_target_pairs={{0,1},{1,0},{2,3},{3,2},{4,5},{5,4},{6,7},{7,6},{8,9},{9,8},{10,11... | collective-permute-start | bytes 1179656 | tf_op jit(solution)/shard_map/ppermute | solution.py:445
  174.0 8.2 %collective-permute-start.39 = (bf16[2,128,768]{2,1,0:T(8,128)(2,1)}, bf16[2,128,768]{2,1,0:T(8,128)(2,1)}, u32[]{:S(2)}, u32[]{:S(2)}) collective-permute-start(bf16[2,128,768]{2,1,0:T(8,128)(2,1)} %get-tuple-element.102), channel_id=1, source_target_pairs={{0,3},{1,2},{2,1},{3,0},{4,7},{5,6},{6,5},{7,4},{8,11},{9,10},{10,... | collective-permute-start | bytes 1179656 | tf_op jit(solution)/shard_map/ppermute | solution.py:445
  181.2 0.9 copy-start.5
  181.2 0.9 copy-start.6
  185.0 6.4 %collective-permute-start.40 = (bf16[1,128,768]{2,1,0:T(8,128)(2,1)}, bf16[1,128,768]{2,1,0:T(8,128)(2,1)S(1)}, u32[]{:S(2)}, u32[]{:S(2)}) collective-permute-start(bf16[1,128,768]{2,1,0:T(8,128)(2,1)} %get-tuple-element.103), channel_id=1, source_target_pairs={{0,12},{1,13},{2,14},{3,15},{4,8},{5,9},{6,10},{7,11},{8,4},{9,5},... | collective-permute-start | bytes 589832 | tf_op jit(solution)/shard_map/ppermute | solution.py:445
  186.7 7.2 %collective-permute-start.41 = (bf16[1,128,768]{2,1,0:T(8,128)(2,1)}, bf16[1,128,768]{2,1,0:T(8,128)(2,1)S(1)}, u32[]{:S(2)}, u32[]{:S(2)}) collective-permute-start(bf16[1,128,768]{2,1,0:T(8,128)(2,1)} %get-tuple-element.104), channel_id=1, source_target_pairs={{0,4},{1,5},{2,6},{3,7},{4,0},{5,1},{6,2},{7,3},{8,12},{9,13},{10,... | collective-permute-start | bytes 589832 | tf_op jit(solution)/shard_map/ppermute | solution.py:445
  186.7 7.2 %collective-permute-start.42 = (bf16[1,128,768]{2,1,0:T(8,128)(2,1)}, bf16[1,128,768]{2,1,0:T(8,128)(2,1)S(1)}, u32[]{:S(2)}, u32[]{:S(2)}) collective-permute-start(bf16[1,128,768]{2,1,0:T(8,128)(2,1)} %get-tuple-element.105), channel_id=1, source_target_pairs={{0,3},{1,2},{2,1},{3,0},{4,7},{5,6},{6,5},{7,4},{8,11},{9,10},{10,... | collective-permute-start | bytes 589832 | tf_op jit(solution)/shard_map/ppermute | solution.py:445
  189.5 7.2 %collective-permute-start.43 = (bf16[1,128,768]{2,1,0:T(8,128)(2,1)}, bf16[1,128,768]{2,1,0:T(8,128)(2,1)S(1)}, u32[]{:S(2)}, u32[]{:S(2)}) collective-permute-start(bf16[1,128,768]{2,1,0:T(8,128)(2,1)} %get-tuple-element.106), channel_id=1, source_target_pairs={{0,1},{1,0},{2,3},{3,2},{4,5},{5,4},{6,7},{7,6},{8,9},{9,8},{10,11... | collective-permute-start | bytes 589832 | tf_op jit(solution)/shard_map/ppermute | solution.py:445
  191.4 5.3 %copy-start.9 = (bf16[1,128,768]{2,1,0:T(8,128)(2,1)}, bf16[1,128,768]{2,1,0:T(8,128)(2,1)S(1)}, u32[]{:S(2)}) copy-start(bf16[1,128,768]{2,1,0:T(8,128)(2,1)S(1)} %collective-permute-done.40.refs_5_) | copy-start | bytes 589828
  193.8 2.9 %copy-start.10 = (bf16[1,128,768]{2,1,0:T(8,128)(2,1)}, bf16[1,128,768]{2,1,0:T(8,128)(2,1)S(1)}, u32[]{:S(2)}) copy-start(bf16[1,128,768]{2,1,0:T(8,128)(2,1)S(1)} %collective-permute-done.41.refs_10_) | copy-start | bytes 589828
  193.8 2.9 %copy-start.11 = (bf16[1,128,768]{2,1,0:T(8,128)(2,1)}, bf16[1,128,768]{2,1,0:T(8,128)(2,1)S(1)}, u32[]{:S(2)}) copy-start(bf16[1,128,768]{2,1,0:T(8,128)(2,1)S(1)} %collective-permute-done.42.refs_15_) | copy-start | bytes 589828
  196.7 0.7 copy-start.12
  202.0 38.0 %all-to-all-start.1 = ((bf16[8,96,768]{2,1,0:T(8,128)(2,1)}), bf16[8,96,768]{2,1,0:T(8,128)(2,1)}, u32[]{:S(2)}, u32[]{:S(2)}) async-start(bf16[8,96,768]{2,1,0:T(8,128)(2,1)} %leave_rows.1), calls=%async_computation.1 | async-start | bytes 2359296 | tf_op jit(solution)/shard_map/all_to_all | solution.py:582

commit v4 on v3

--- a/solution.py
+++ b/solution.py
@@ -64,21 +64,17 @@
     )(x, dest)
 
 
-def places(coded, slots):
-    code = coded[:, :slots].astype(F32)
-    place = (code[0:1] * 16.0 + code[1:2]).astype(jnp.int32)
-    return jnp.where(code[2:3] > 0.5, place, -1)
-
-
-def land_body(groups, slots, arrived_ref, code_ref, place_ref, *pair_refs):
+def land_body(groups, slots, arrived_ref, code_ref, put_ref, *pair_refs):
     part = pair_refs[0].shape[1]
     rows = 2 * part * len(pair_refs)
-    total = jnp.zeros((rows, arrived_ref.shape[2]), F32)
+    width = arrived_ref.shape[2]
     for s in range(groups):
-        place = places(arrived_ref[s, slots:, :], slots)
-        place_ref[s : s + 1, :] = place
-        put = jnp.where(iota((rows, slots), 0) == place, 1.0, 0.0).astype(BF)
-        total += dot(put, arrived_ref[s, :slots, :], NN)
+        code = jnp.transpose(arrived_ref[s, slots:, :128].astype(F32))[:slots]
+        place = jnp.where(code[:, 2:3] > 0.5, code[:, 0:1] * 16.0 + code[:, 1:2], -1.0).astype(jnp.int32)
+        put = jnp.where(iota((slots, rows), 1) == place, 1.0, 0.0).astype(BF)
+        put_ref[s * slots : (s + 1) * slots, :] = put
+    sent = arrived_ref[:, :slots, :].reshape(groups * slots, width)
+    total = dot(put_ref[...], sent, TN)
     for k in range(2 * len(pair_refs)):
         pair_refs[k // 2][k % 2] = total[k * part : (k + 1) * part].astype(BF)
 
@@ -89,14 +85,14 @@
     return pl.pallas_call(
         functools.partial(land_body, groups, slots),
         in_specs=[pl.BlockSpec(memory_space=pltpu.VMEM), pl.BlockSpec(memory_space=pltpu.HBM)],
-        out_shape=(jax.ShapeDtypeStruct((groups, slots), jnp.int32), pair, pair),
+        out_shape=(jax.ShapeDtypeStruct((groups * slots, rows), BF), pair, pair),
         compiler_params=params(LIMIT),
         name="land_rows",
     )(arrived, codes)
 
 
 def leave_body(groups, slots, terms, *refs):
-    place_ref, out_ref = refs[0], refs[-1]
+    put_ref, out_ref = refs[0], refs[-1]
     streams = []
     for k in range(STREAMS):
         total = refs[1 + k * terms][0].astype(F32)
@@ -104,10 +100,7 @@
             total += ref[0].astype(F32)
         streams.append(total.astype(BF))
     grad = jnp.concatenate(streams, axis=0)
-    rows = grad.shape[0]
-    for s in range(groups):
-        put = jnp.where(iota((rows, slots), 0) == place_ref[s : s + 1, :], 1.0, 0.0).astype(BF)
-        out_ref[s] = dot(put, grad, TN).astype(BF)
+    out_ref[...] = dot(put_ref[...], grad, NN).astype(BF).reshape(groups, slots, grad.shape[1])
 
 
 def one_block(array, index, part):
@@ -115,20 +108,20 @@
     return pl.BlockSpec((1, part, width), lambda i: (index, i, 0))
 
 
-def leave(place, terms):
-    groups, slots = place.shape
+def leave(put, terms, groups):
+    slots = put.shape[0] // groups
     flat = [term for stream in terms for term in stream]
     width = flat[0][0].shape[2]
     return pl.pallas_call(
         functools.partial(leave_body, groups, slots, len(terms[0])),
         grid=(1,),
-        in_specs=[pl.BlockSpec((groups, slots), lambda i: (0, 0))]
+        in_specs=[pl.BlockSpec(put.shape, lambda i: (0, 0))]
         + [one_block(a, index, a.shape[1]) for a, index in flat],
         out_specs=pl.BlockSpec((groups, slots, width), lambda i: (0, 0, 0)),
         out_shape=jax.ShapeDtypeStruct((groups, slots, width), BF),
         compiler_params=params(LIMIT),
         name="leave_rows",
-    )(place, *[a for a, _ in flat])
+    )(put, *[a for a, _ in flat])
 
 
 def merge_body(sums, *refs):
@@ -164,12 +157,9 @@
 
 
 def home_body(groups, slots, back_ref, rank_ref, out_ref):
-    rows = out_ref.shape[0]
-    total = jnp.zeros(out_ref.shape, F32)
-    for t in range(groups):
-        pick = jnp.where(iota((slots, rows), 0) + t * slots == rank_ref[...], 1.0, 0.0).astype(BF)
-        total += dot(pick, back_ref[t], TN)
-    out_ref[...] = total.astype(BF)
+    rows, width = out_ref.shape
+    pick = jnp.where(iota((groups * slots, rows), 0) == rank_ref[...], 1.0, 0.0).astype(BF)
+    out_ref[...] = dot(pick, back_ref[...].reshape(groups * slots, width), TN).astype(BF)
 
 
 def home(back, rank):
@@ -268,7 +258,7 @@
         use_second = jnp.where(second >= 0, second, use_first)
         return batch, (first, second), (use_first, use_second)
 
-    code_cut = code_hbm.at[:, pl.ds(0, 2)]
+    code_cut = code_hbm.at[:, 0]
     code_copy = pltpu.make_async_copy(code_cut, code_ref, code_sem.at[0])
     code_copy.start()
     for p in range(count):
@@ -286,7 +276,8 @@
 
     def signals(u):
         batch, asked, use = slots_of(u)
-        code = code_ref[batch, meta_ref[1, u]].astype(F32).astype(jnp.int32)
+        code = code_ref[batch].astype(F32).astype(jnp.int32)
+        code = jnp.where(meta_ref[1, u] == 0, code[: CODE // 2], code[CODE // 2 :])
         scores = dot(jnp.concatenate([w_ref[use[0]], w_ref[use[1]]], axis=0), x_buf[u], NT)
         for c in range(CAP):
             slot = table_ref[batch, 2 * c]
@@ -351,7 +342,7 @@
             pltpu.VMEM((total, rows, width), BF),
             pltpu.VMEM((total, CAP, lanes, rows), BF),
             pltpu.VMEM(panels.shape, BF),
-            pltpu.VMEM((codes.shape[0], 2, CODE, rows), BF),
+            pltpu.VMEM((codes.shape[0], CODE, rows), BF),
             pltpu.VMEM(scales.shape, BF),
             pltpu.SMEM((count,), jnp.int32),
             pltpu.SemaphoreType.DMA((total,)),
@@ -439,6 +430,9 @@
 ORDERS = ((1, 3, 4, 12), (3, 1, 12, 4), (4, 12, 1, 3), (12, 4, 3, 1))
 STREAMS = len(ORDERS)
 RINGS = ((1, 3), (4, 12))
+SPREAD = [0]
+for mask in ORDERS[0]:
+    SPREAD += [r ^ mask for r in SPREAD]
 
 
 def swap(array, mask, owners):
@@ -452,21 +446,22 @@
     owners = lax.axis_size("label")
     slots = 3 * rows // (2 * groups)
     part = rows // STREAMS
+    every = range(STREAMS)
+    order = ORDERS
     me = lax.axis_index("label").astype(jnp.int32)
 
     outgoing, rank = pack(queries, cluster_dest.reshape(1, rows), groups, slots)
 
     marks = jnp.transpose(positives.reshape(2, 2 * part, -1), (0, 2, 1))
-    code = jnp.concatenate([marks // lanes, marks % lanes], axis=1).astype(F32).astype(BF)
-    code = jnp.pad(code, ((0, 0), (0, CODE - code.shape[1]), (0, 0)))
-    listed = jnp.pad(shortlist.astype(F32).astype(BF), ((0, CODE - 1), (0, 2 * part - shortlist.shape[1])))
-    code = jnp.concatenate([code, listed[None]], axis=0)[None]
+    code = jnp.concatenate([marks // lanes, marks % lanes], axis=1).reshape(CODE, 2 * part)
+    listed = jnp.pad(shortlist, ((0, CODE - 1), (0, 2 * part - shortlist.shape[1])))
+    code = jnp.stack([code, listed]).astype(F32).astype(BF)[None]
     outgoing, codes = lax.optimization_barrier((outgoing, code))
     arrived = lax.all_to_all(outgoing, "dp", split_axis=0, concat_axis=0, tiled=True)
-    for step in range(4):
-        codes = jnp.concatenate([codes, swap(codes, 1 << step, owners)], axis=0)
-    place, *own = land(arrived, codes, rows, slots)
-    wanted = codes[:, 2, 0, : shortlist.shape[1]].astype(F32).astype(jnp.int32)
+    for mask in order[0]:
+        codes = jnp.concatenate([codes, swap(codes, mask, owners)], axis=0)
+    put, *own = land(arrived, codes, rows, slots)
+    wanted = codes[:, 1, 0, : shortlist.shape[1]].astype(F32).astype(jnp.int32)
 
     slot_ids = jnp.arange(wanted.shape[1], dtype=jnp.int32)[None, :]
     mine = wanted // count == me
@@ -487,8 +482,6 @@
         axis=1,
     )
 
-    every = range(STREAMS)
-    order = ORDERS
     arrays = []
     for pair, (one, three) in zip(own, RINGS):
         by1, by3 = swap(pair, one, owners), swap(pair, three, owners)
@@ -535,7 +528,7 @@
                 outs_of.setdefault((k, b & 1), []).append(b)
             where[pair, r] = (origin, index, len(units))
             units.append((tuple((source(a), i) for a, i in origin), legs, pair))
-            ids.append(r)
+            ids.append(SPREAD.index(r))
         keys = sorted(outs_of)
         for key in keys:
             outs_of[key].sort(key=lambda b: (b >> 1 & 1, b))
@@ -576,18 +569,17 @@
         sent = [b for b in range(owners) if b & bit and not b & (bit - 1)]
         sums = merge([[terms(k, b) for b in sent] for k in every], f"merge_{step}")
         for k in every:
-            got = swap(sums[k], order[k][step], owners)
-            later[k].append((got, [b ^ bit for b in sent]))
-    leaving = leave(place, [terms(k, 0) for k in every])
+            later[k].append((swap(sums[k], order[k][step], owners), [b ^ bit for b in sent]))
+    leaving = leave(put, [terms(k, 0) for k in every], groups)
     returned = lax.all_to_all(leaving, "dp", split_axis=0, concat_axis=0, tiled=True)
 
     flat = [(pair, a) for pair in (0, 1) for a in range(5)]
     parts = []
-    for r in range(owners):
+    for r in SPREAD:
         parts.append([])
         for pair in (0, 1):
             origin, signal, unit = where[pair, r]
-            parts[r].append((tuple((flat.index(a), i) for a, i in origin), signal, unit))
+            parts[-1].append((tuple((flat.index(a), i) for a, i in origin), signal, unit))
     panel_grad = panel_sum(
         table,
         [arrays[pair][a] for pair, a in flat],

time: 245 us -> 244 us (level)
  starting transfers between devices: 81 us -> 83.8 us
  Pallas kernels: 92 us -> 89.5 us
    ppermute x44, waiting for transfers between devices: 59.3 us -> 56.4 us  [swap(): return lax.ppermute(array, 'label', [(i, i ^ mask) for i in range(owners)])]
  transfers between devices with their start and end apart: 46 -> 46, of which waited for: 21 -> 25; matrix products, arithmetic and copies ran while one was open for 3% -> 3% of each run, Pallas kernels for 27% -> 26%
where the time goes in v4:
time: 244 us; the launch traced here: 243 us
  Pallas kernels  89.5 us (37%)
  starting transfers between devices  83.8 us (34%)
  waiting for transfers between devices  59.4 us (24%)
  local copies, waits for them, and re-layouts  4.82 us (2%)
  other arithmetic  4.64 us (2%)
    ppermute x44, waiting for transfers between devices, swap(): return lax.ppermute(array, 'label', [(i, i ^ mask) for i in range(owners)])  56.4 us
    ppermute x44, starting transfers between devices, swap(): return lax.ppermute(array, 'label', [(i, i ^ mask) for i in range(owners)])  56.2 us
    pallas_call x4, Pallas kernels, work(): pl.pallas_call(functools.partial(work_body, units, len(arrays), len(out_b...  45.6 us
    all_to_all x1, starting transfers between devices, shards(): lax.all_to_all(leaving, 'dp', split_axis=0, concat_axis=0, tiled=True)  21.8 us
    pallas_call x1, Pallas kernels, panel_sum(): pl.pallas_call(functools.partial(panel_body, parts, len(arrays), len(sign...  15.5 us
    pallas_call x3, Pallas kernels, merge(): pl.pallas_call(functools.partial(merge_body, [[[0] * len(t) for t in b] f...  10.9 us
    all_to_all x1, starting transfers between devices, shards(): lax.all_to_all(outgoing, 'dp', split_axis=0, concat_axis=0, tiled=True)  5.81 us
  transfers between devices with their start and end apart: 46, of which 25 were waited for; matrix products, arithmetic and copies ran while one was open for 3% of the time, Pallas kernels for 26%

profile of v4, /device:TPU:1, one launch (start us, length us, event | category | flops | bytes accessed | tf_op | source)
XLA Modules:
  0.0 243.1 jit_solution(7113259300904344716)
XLA Ops:
  2.0 3.7 %pack_rows.1 = (bf16[8,112,768]{2,1,0:T(8,128)(2,1)}, s32[1,512]{1,0:T(1,128)}) custom-call(bf16[512,768]{1,0:T(8,128)(2,1)} %x_ref.1, s32[1,512]{1,0:T(1,128)} %bitcast.76), custom_call_target="tpu_custom_call" | custom-call | tf_op jit(solution)/shard_map/pack_rows/pallas_call | solution.py:56
  5.7 5.8 %all-to-all-start = ((bf16[8,112,768]{2,1,0:T(8,128)(2,1)}), bf16[8,112,768]{2,1,0:T(8,128)(2,1)}, u32[]{:S(2)}, u32[]{:S(2)}) async-start(bf16[8,112,768]{2,1,0:T(8,128)(2,1)} %get-tuple-element.58), calls=%async_computation | async-start | bytes 2752512 | tf_op jit(solution)/shard_map/all_to_all | solution.py:460
  11.5 1.6 collective-permute-start
  13.2 1.1 collective-permute-done
  14.3 3.6 %collective-permute-start.1 = (bf16[2,2,16,256]{3,2,1,0:T(8,128)(2,1)S(1)}, bf16[2,2,16,256]{3,2,1,0:T(8,128)(2,1)S(1)}, u32[]{:S(2)}, u32[]{:S(2)}) collective-permute-start(bf16[2,2,16,256]{3,2,1,0:T(8,128)(2,1)S(1)} %pad_maximum_fusion.4), channel_id=1, source_target_pairs={{0,3},{1,2},{2,1},{3,0},{4,7},{5,6},{6,5},{7,4},{8,11},{9,10},{10,... | collective-permute-start | bytes 98312 | tf_op jit(solution)/shard_map/ppermute | solution.py:439
  17.9 1.3 collective-permute-done.1
  19.2 1.4 collective-permute-start.2
  20.6 2.2 collective-permute-done.2
  22.8 2.8 %collective-permute-start.3 = (bf16[8,2,16,256]{3,2,1,0:T(8,128)(2,1)S(1)}, bf16[8,2,16,256]{3,2,1,0:T(8,128)(2,1)S(1)}, u32[]{:S(2)}, u32[]{:S(2)}) collective-permute-start(bf16[8,2,16,256]{3,2,1,0:T(8,128)(2,1)S(1)} %pad_maximum_fusion.2), channel_id=1, source_target_pairs={{0,12},{1,13},{2,14},{3,15},{4,8},{5,9},{6,10},{7,11},{8,4},{9,5},... | collective-permute-start | bytes 393224 | tf_op jit(solution)/shard_map/ppermute | solution.py:439
  25.6 2.7 %collective-permute-done.3 = bf16[8,2,16,256]{3,2,1,0:T(8,128)(2,1)S(1)} collective-permute-done((bf16[8,2,16,256]{3,2,1,0:T(8,128)(2,1)S(1)}, bf16[8,2,16,256]{3,2,1,0:T(8,128)(2,1)S(1)}, u32[]{:S(2)}, u32[]{:S(2)}) %collective-permute-start.3) | collective-permute-done | bytes 131104 | tf_op jit(solution)/shard_map/ppermute | solution.py:439
  28.4 1.8 all-to-all-done.arrived_ref
  30.2 3.6 %land_rows.1 = (bf16[768,512]{1,0:T(8,128)(2,1)}, bf16[2,128,768]{2,1,0:T(8,128)(2,1)}, bf16[2,128,768]{2,1,0:T(8,128)(2,1)}) custom-call(bf16[8,112,768]{2,1,0:T(8,128)(2,1)} %all-to-all-done.arrived_ref, bf16[16,2,16,256]{3,2,1,0:T(8,128)(2,1)} %copy-done.6), custom_call_target="tpu_custom_call" | custom-call | tf_op jit(solution)/shard_map/land_rows/pallas_call | solution.py:85
  33.8 3.8 %collective-permute-start.6 = (bf16[2,128,768]{2,1,0:T(8,128)(2,1)}, bf16[2,128,768]{2,1,0:T(8,128)(2,1)S(1)}, u32[]{:S(2)}, u32[]{:S(2)}) collective-permute-start(bf16[2,128,768]{2,1,0:T(8,128)(2,1)} %get-tuple-element.61), channel_id=1, source_target_pairs={{0,3},{1,2},{2,1},{3,0},{4,7},{5,6},{6,5},{7,4},{8,11},{9,10},{10,... | collective-permute-start | bytes 1179656 | tf_op jit(solution)/shard_map/ppermute | solution.py:439
  37.6 2.7 %collective-permute-start.10 = (bf16[2,128,768]{2,1,0:T(8,128)(2,1)}, bf16[2,128,768]{2,1,0:T(8,128)(2,1)S(1)}, u32[]{:S(2)}, u32[]{:S(2)}) collective-permute-start(bf16[2,128,768]{2,1,0:T(8,128)(2,1)} %get-tuple-element.62), channel_id=1, source_target_pairs={{0,12},{1,13},{2,14},{3,15},{4,8},{5,9},{6,10},{7,11},{8,4},{9,5},... | collective-permute-start | bytes 1179656 | tf_op jit(solution)/shard_map/ppermute | solution.py:439
  40.3 5.4 %collective-permute-done.6 = bf16[2,128,768]{2,1,0:T(8,128)(2,1)S(1)} collective-permute-done((bf16[2,128,768]{2,1,0:T(8,128)(2,1)}, bf16[2,128,768]{2,1,0:T(8,128)(2,1)S(1)}, u32[]{:S(2)}, u32[]{:S(2)}) %collective-permute-start.6) | collective-permute-done | bytes 393248 | tf_op jit(solution)/shard_map/ppermute | solution.py:439
  46.6 1.7 collective-permute-start.5
  48.3 2.1 collective-permute-start.11
  50.4 2.0 collective-permute-start.9
  52.4 1.3 pad_maximum_fusion.refs_5_.refs_1_
  53.8 2.0 collective-permute-start.12
  56.3 1.4 pad_maximum_fusion.1.refs_6_
  58.5 1.9 collective-permute-start.14
  63.1 1.6 broadcast_in_dim.37.refs_4_
  64.7 9.4 %work_near.1 = (bf16[1,128,768]{2,1,0:T(8,128)(2,1)}, bf16[2,128,768]{2,1,0:T(8,128)(2,1)}, bf16[1,128,768]{2,1,0:T(8,128)(2,1)}, bf16[2,128,768]{2,1,0:T(8,128)...) custom-call(s32[16,4]{1,0:T(8,128)} %copy.29.refs_0_, ...), custom_call_target="tpu_custom_call" | custom-call | flops 3623878656 | bytes 11796480 | tf_op jit(solution)/shard_map/work_near/pallas_call | solution.py:334
  75.1 11.7 %collective-permute-done.12.refs_0_.refs_7_.refs_5_.refs_2_ = bf16[2,4,128,768]{3,2,1,0:T(8,128)(2,1)} collective-permute-done((bf16[2,4,128,768]{3,2,1,0:T(8,128)(2,1)}, bf16[2,4,128,768]{3,2,1,0:T(8,128)(2,1)}, u32[]{:S(2)}, u32[]{:S(2)}) %collective-permute-start.12) | collective-permute-done | bytes 1572896 | tf_op jit(solution)/shard_map/ppermute | solution.py:439
  86.8 2.3 collective-permute-start.23
  89.1 1.4 collective-permute-done.13.refs_2_.refs_8_.refs_6_.refs_7_
  90.4 1.1 collective-permute-done.14.refs_1_.refs_9_.refs_7_.refs_3_
  91.6 1.9 collective-permute-done.15.refs_3_.refs_10_.refs_8_
  93.5 2.8 %cut_halves.1 = (bf16[4,128,768]{2,1,0:T(8,128)(2,1)}, bf16[4,128,768]{2,1,0:T(8,128)(2,1)}, bf16[4,128,768]{2,1,0:T(8,128)(2,1)}, bf16[4,128,768]{2,1,0:T(8,128)(2,1)}) custom-call(bf16[2,4,128,768]{3,2,1,0:T(8,128)(2,1)} %collective-permute-done.12.refs_0_.refs_7_.refs_5_.refs_2_, ...), custom_call_target="tpu_custom_call" | custom-call | tf_op jit(solution)/shard_map/cut_halves/pallas_call | solution.py:192
  96.9 1.5 collective-permute-start.26
  98.9 1.2 collective-permute-start.18
  100.1 1.8 collective-permute-done.23.refs_9_.refs_7_
  102.2 15.6 %work_far.1 = (bf16[2,128,768]{2,1,0:T(8,128)(2,1)}, bf16[4,128,768]{2,1,0:T(8,128)(2,1)}, bf16[2,128,768]{2,1,0:T(8,128)(2,1)}, bf16[4,128,768]{2,1,0:T(8,128)(...) custom-call(s32[16,4]{1,0:T(8,128)} %copy.29.refs_0_, ...), custom_call_target="tpu_custom_call" | custom-call | flops 7247757312 | bytes 17301504 | tf_op jit(solution)/shard_map/work_far/pallas_call | solution.py:334
  117.8 1.3 collective-permute-start.21
  119.0 1.4 collective-permute-start.24
  120.7 1.8 collective-permute-start.29
  123.4 9.5 %work_last.1 = (bf16[1,128,768]{2,1,0:T(8,128)(2,1)}, bf16[2,128,768]{2,1,0:T(8,128)(2,1)}, bf16[1,128,768]{2,1,0:T(8,128)(2,1)}, bf16[2,128,768]{2,1,0:T(8,128)...) custom-call(s32[16,4]{1,0:T(8,128)} %copy.29.refs_0_, ...), custom_call_target="tpu_custom_call" | custom-call | flops 3623878656 | bytes 11796480 | tf_op jit(solution)/shard_map/work_last/pallas_call | solution.py:334
  133.0 1.2 collective-permute-start.25
  134.2 1.6 collective-permute-start.31
  135.8 3.4 %collective-permute-done.30.refs_27_.refs_29_.refs_19_.refs_13_ = bf16[4,128,768]{2,1,0:T(8,128)(2,1)} collective-permute-done((bf16[4,128,768]{2,1,0:T(8,128)(2,1)}, bf16[4,128,768]{2,1,0:T(8,128)(2,1)}, u32[]{:S(2)}, u32[]{:S(2)}) %collective-permute-start.30) | collective-permute-done | bytes 786464 | tf_op jit(solution)/shard_map/ppermute | solution.py:439
  139.2 5.3 %collective-permute-done.22.refs_7_.refs_4_ = bf16[2,128,768]{2,1,0:T(8,128)(2,1)} collective-permute-done((bf16[2,128,768]{2,1,0:T(8,128)(2,1)}, bf16[2,128,768]{2,1,0:T(8,128)(2,1)}, u32[]{:S(2)}, u32[]{:S(2)}) %collective-permute-start.22) | collective-permute-done | bytes 393248 | tf_op jit(solution)/shard_map/ppermute | solution.py:439
  144.5 1.3 collective-permute-done.25.refs_15_.refs_10_
  145.8 1.8 collective-permute-done.31.refs_31_.refs_22_
  147.6 4.4 %merge_1.1 = (bf16[4,128,768]{2,1,0:T(8,128)(2,1)}, bf16[4,128,768]{2,1,0:T(8,128)(2,1)}, bf16[4,128,768]{2,1,0:T(8,128)(2,1)}, bf16[4,128,768]{2,1,0:T(8,128)(2,1)}) custom-call(bf16[1,128,768]{2,1,0:T(8,128)(2,1)} %get-tuple-element.69.refs_0_, bf16[2,128,768]{2,1,0:T(8,128)(2,1)} %copy-done.2, bf16[2,128,768]{2,1,0:T(8,128)(2,1)} %get-tuple-element.70.refs_2_.refs_4_, ...), custom_call_target="tpu_custom_call" | custom-call | bytes 9437184 | tf_op jit(solution)/shard_map/merge_1/pallas_call | solution.py:145
  152.1 1.1 collective-permute-start.32
  153.3 1.8 collective-permute-start.34
  155.2 11.3 %work_kept.1 = (bf16[4,128,768]{2,1,0:T(8,128)(2,1)}, bf16[4,128,768]{2,1,0:T(8,128)(2,1)}, bf16[4,128,768]{2,1,0:T(8,128)(2,1)}, bf16[4,128,768]{2,1,0:T(8,128)(2,1)}, bf16[8,2,256,256]{3,2,1,0:T(8,128)(2,1)}) custom-call(s32[16,4]{1,0:T(8,128)} %copy.29.refs_0_, s32[2,8]{1,0:T(2,128)} %constant.77.clone.refs_1_, bf16[16,2,16,256]{3,2,1,0:T(8,128)(2,1)} %copy-done.6, ...), custom_call_target="tpu_custom_call" | custom-call | flops 4831838208 | bytes 13631488 | tf_op jit(solution)/shard_map/work_kept/pallas_call | solution.py:334
  167.3 3.6 %merge_2.1 = (bf16[2,128,768]{2,1,0:T(8,128)(2,1)}, bf16[2,128,768]{2,1,0:T(8,128)(2,1)}, bf16[2,128,768]{2,1,0:T(8,128)(2,1)}, bf16[2,128,768]{2,1,0:T(8,128)(2,1)}) custom-call(bf16[4,128,768]{2,1,0:T(8,128)(2,1)} %get-tuple-element.67.refs_0_.refs_3_.refs_1_, bf16[4,128,768]{2,1,0:T(8,128)(2,1)} %copy-done.1, bf16[4,128,768]{2,1,0:T(8,128)(2,1)} %copy-done, ...), custom_call_target="tpu_custom_call" | custom-call | bytes 6291456 | tf_op jit(solution)/shard_map/merge_2/pallas_call | solution.py:145
  171.0 1.9 collective-permute-start.36
  173.5 1.6 collective-permute-start.38
  175.1 1.7 collective-permute-start.39
  176.7 6.2 %collective-permute-done.36.refs_3_.refs_4_ = bf16[2,128,768]{2,1,0:T(8,128)(2,1)S(1)} collective-permute-done((bf16[2,128,768]{2,1,0:T(8,128)(2,1)}, bf16[2,128,768]{2,1,0:T(8,128)(2,1)S(1)}, u32[]{:S(2)}, u32[]{:S(2)}) %collective-permute-start.36) | collective-permute-done | bytes 393248 | tf_op jit(solution)/shard_map/ppermute | solution.py:439
  183.8 2.9 %merge_3.1 = (bf16[1,128,768]{2,1,0:T(8,128)(2,1)}, bf16[1,128,768]{2,1,0:T(8,128)(2,1)}, bf16[1,128,768]{2,1,0:T(8,128)(2,1)}, bf16[1,128,768]{2,1,0:T(8,128)(2,1)}) custom-call(bf16[4,128,768]{2,1,0:T(8,128)(2,1)} %get-tuple-element.67.refs_0_.refs_3_.refs_1_, bf16[4,128,768]{2,1,0:T(8,128)(2,1)} %copy-done.1, bf16[4,128,768]{2,1,0:T(8,128)(2,1)} %copy-done, ...), custom_call_target="tpu_custom_call" | custom-call | bytes 3932160 | tf_op jit(solution)/shard_map/merge_3/pallas_call | solution.py:145
  186.6 1.2 collective-permute-start.40
  188.2 1.9 collective-permute-start.42
  191.1 1.6 collective-permute-done.40.refs_5_
  192.7 2.3 collective-permute-done.41.refs_10_
  195.0 1.6 collective-permute-done.43.refs_20_
  197.3 4.4 %leave_rows.1 = bf16[8,96,768]{2,1,0:T(8,128)(2,1)} custom-call(bf16[768,512]{1,0:T(8,128)(2,1)} %get-tuple-element.60.refs_0_, bf16[4,128,768]{2,1,0:T(8,128)(2,1)} %get-tuple-element.67.refs_0_.refs_3_.refs_1_, bf16[2,128,768]{2,1,0:T(8,128)(2,1)} %copy-done.2, bf16[4,128,768]{2,1,0:T(8,128)(2,1)} %copy-done, bf16[2,128,768]{2,1,0:T(8,128)(2,1)} %copy-done.4, ...), custom_call_target="tpu_custom_call" | custom-call | tf_op jit(solution)/shard_map/leave_rows/pallas_call | solution.py:115
  201.7 21.8 %all-to-all-start.1 = ((bf16[8,96,768]{2,1,0:T(8,128)(2,1)}), bf16[8,96,768]{2,1,0:T(8,128)(2,1)}, u32[]{:S(2)}, u32[]{:S(2)}) async-start(bf16[8,96,768]{2,1,0:T(8,128)(2,1)} %leave_rows.1), calls=%async_computation.1 | async-start | bytes 2359296 | tf_op jit(solution)/shard_map/all_to_all | solution.py:574
  223.5 15.5 %panel_grad.1 = bf16[16,256,768]{2,1,0:T(8,128)(2,1)} custom-call(s32[16,4]{1,0:T(8,128)} %copy.29.refs_0_, bf16[2,4,128,768]{3,2,1,0:T(8,128)(2,1)} %pad_maximum_fusion.refs_5_.refs_1_, bf16[2,4,128,768]{3,2,1,0:T(8,128)(2,1)} %collective-permute-done.12.refs_0_.refs_7_.refs_5_.refs_2_, ...), custom_call_target="tpu_custom_call" | custom-call | flops 6442450944 | bytes 27262976 | tf_op jit(solution)/shard_map/panel_grad/pallas_call | solution.py:408
  239.0 1.1 all-to-all-done.1.back_ref
  240.1 3.0 %home_rows.1 = bf16[512,768]{1,0:T(8,128)(2,1)} custom-call(bf16[8,96,768]{2,1,0:T(8,128)(2,1)} %all-to-all-done.1.back_ref, s32[1,512]{1,0:T(1,128)} %get-tuple-element.107.rank_ref), custom_call_target="tpu_custom_call" | custom-call | tf_op jit(solution)/shard_map/home_rows/pallas_call | solution.py:167
  (96 shorter events, 14.6 us)
Async XLA Ops:
  5.7 24.5 %all-to-all-start = ((bf16[8,112,768]{2,1,0:T(8,128)(2,1)}), bf16[8,112,768]{2,1,0:T(8,128)(2,1)}, u32[]{:S(2)}, u32[]{:S(2)}) async-start(bf16[8,112,768]{2,1,0:T(8,128)(2,1)} %get-tuple-element.58), calls=%async_computation | async-start | bytes 2752512 | tf_op jit(solution)/shard_map/all_to_all | solution.py:460
  11.5 2.8 %collective-permute-start = (bf16[1,2,16,256]{3,2,1,0:T(8,128)(2,1)S(1)}, bf16[1,2,16,256]{3,2,1,0:T(8,128)(2,1)S(1)}, u32[]{:S(2)}, u32[]{:S(2)}) collective-permute-start(bf16[1,2,16,256]{3,2,1,0:T(8,128)(2,1)S(1)} %fusion), channel_id=1, source_target_pairs={{0,1},{1,0},{2,3},{3,2},{4,5},{5,4},{6,7},{7,6},{8,9},{9,8},{10,11... | collective-permute-start | bytes 49160 | tf_op jit(solution)/shard_map/ppermute | solution.py:439
  14.3 4.9 %collective-permute-start.1 = (bf16[2,2,16,256]{3,2,1,0:T(8,128)(2,1)S(1)}, bf16[2,2,16,256]{3,2,1,0:T(8,128)(2,1)S(1)}, u32[]{:S(2)}, u32[]{:S(2)}) collective-permute-start(bf16[2,2,16,256]{3,2,1,0:T(8,128)(2,1)S(1)} %pad_maximum_fusion.4), channel_id=1, source_target_pairs={{0,3},{1,2},{2,1},{3,0},{4,7},{5,6},{6,5},{7,4},{8,11},{9,10},{10,... | collective-permute-start | bytes 98312 | tf_op jit(solution)/shard_map/ppermute | solution.py:439
  19.2 3.6 %collective-permute-start.2 = (bf16[4,2,16,256]{3,2,1,0:T(8,128)(2,1)S(1)}, bf16[4,2,16,256]{3,2,1,0:T(8,128)(2,1)S(1)}, u32[]{:S(2)}, u32[]{:S(2)}) collective-permute-start(bf16[4,2,16,256]{3,2,1,0:T(8,128)(2,1)S(1)} %pad_maximum_fusion.3), channel_id=1, source_target_pairs={{0,4},{1,5},{2,6},{3,7},{4,0},{5,1},{6,2},{7,3},{8,12},{9,13},{10,... | collective-permute-start | bytes 196616 | tf_op jit(solution)/shard_map/ppermute | solution.py:439
  22.8 5.6 %collective-permute-start.3 = (bf16[8,2,16,256]{3,2,1,0:T(8,128)(2,1)S(1)}, bf16[8,2,16,256]{3,2,1,0:T(8,128)(2,1)S(1)}, u32[]{:S(2)}, u32[]{:S(2)}) collective-permute-start(bf16[8,2,16,256]{3,2,1,0:T(8,128)(2,1)S(1)} %pad_maximum_fusion.2), channel_id=1, source_target_pairs={{0,12},{1,13},{2,14},{3,15},{4,8},{5,9},{6,10},{7,11},{8,4},{9,5},... | collective-permute-start | bytes 393224 | tf_op jit(solution)/shard_map/ppermute | solution.py:439
  28.4 1.8 copy-start.6
  33.8 18.6 %copy-start.8 = (bf16[2,128,768]{2,1,0:T(8,128)(2,1)S(1)}, bf16[2,128,768]{2,1,0:T(8,128)(2,1)}, u32[]{:S(2)}) copy-start(bf16[2,128,768]{2,1,0:T(8,128)(2,1)} %get-tuple-element.61) | copy-start | bytes 1179652
  33.8 11.9 %collective-permute-start.6 = (bf16[2,128,768]{2,1,0:T(8,128)(2,1)}, bf16[2,128,768]{2,1,0:T(8,128)(2,1)S(1)}, u32[]{:S(2)}, u32[]{:S(2)}) collective-permute-start(bf16[2,128,768]{2,1,0:T(8,128)(2,1)} %get-tuple-element.61), channel_id=1, source_target_pairs={{0,3},{1,2},{2,1},{3,0},{4,7},{5,6},{6,5},{7,4},{8,11},{9,10},{10,... | collective-permute-start | bytes 1179656 | tf_op jit(solution)/shard_map/ppermute | solution.py:439
  37.6 9.0 %collective-permute-start.4 = (bf16[2,128,768]{2,1,0:T(8,128)(2,1)}, bf16[2,128,768]{2,1,0:T(8,128)(2,1)S(1)}, u32[]{:S(2)}, u32[]{:S(2)}) collective-permute-start(bf16[2,128,768]{2,1,0:T(8,128)(2,1)} %get-tuple-element.61), channel_id=1, source_target_pairs={{0,1},{1,0},{2,3},{3,2},{4,5},{5,4},{6,7},{7,6},{8,9},{9,8},{10,11... | collective-permute-start | bytes 1179656 | tf_op jit(solution)/shard_map/ppermute | solution.py:439
  37.6 10.7 %collective-permute-start.10 = (bf16[2,128,768]{2,1,0:T(8,128)(2,1)}, bf16[2,128,768]{2,1,0:T(8,128)(2,1)S(1)}, u32[]{:S(2)}, u32[]{:S(2)}) collective-permute-start(bf16[2,128,768]{2,1,0:T(8,128)(2,1)} %get-tuple-element.62), channel_id=1, source_target_pairs={{0,12},{1,13},{2,14},{3,15},{4,8},{5,9},{6,10},{7,11},{8,4},{9,5},... | collective-permute-start | bytes 1179656 | tf_op jit(solution)/shard_map/ppermute | solution.py:439
  40.3 10.1 %collective-permute-start.8 = (bf16[2,128,768]{2,1,0:T(8,128)(2,1)}, bf16[2,128,768]{2,1,0:T(8,128)(2,1)S(1)}, u32[]{:S(2)}, u32[]{:S(2)}) collective-permute-start(bf16[2,128,768]{2,1,0:T(8,128)(2,1)} %get-tuple-element.62), channel_id=1, source_target_pairs={{0,4},{1,5},{2,6},{3,7},{4,0},{5,1},{6,2},{7,3},{8,12},{9,13},{10,... | collective-permute-start | bytes 1179656 | tf_op jit(solution)/shard_map/ppermute | solution.py:439
  45.7 6.7 %collective-permute-start.7 = (bf16[128,768]{1,0:T(8,128)(2,1)S(1)}, bf16[128,768]{1,0:T(8,128)(2,1)S(1)}, u32[]{:S(2)}, u32[]{:S(2)}) collective-permute-start(bf16[128,768]{1,0:T(8,128)(2,1)S(1)} %slice_bitcast_fusion.2), channel_id=1, source_target_pairs={{0,1},{1,0},{2,3},{3,2},{4,5},{5,4},{6,7},{7,6},{8,9},{9,8},{10,11... | collective-permute-start | bytes 589832 | tf_op jit(solution)/shard_map/ppermute | solution.py:439
  46.6 5.8 %collective-permute-start.5 = (bf16[128,768]{1,0:T(8,128)(2,1)S(1)}, bf16[128,768]{1,0:T(8,128)(2,1)S(1)}, u32[]{:S(2)}, u32[]{:S(2)}) collective-permute-start(bf16[128,768]{1,0:T(8,128)(2,1)S(1)} %slice_bitcast_fusion.3), channel_id=1, source_target_pairs={{0,3},{1,2},{2,1},{3,0},{4,7},{5,6},{6,5},{7,4},{8,11},{9,10},{10,... | collective-permute-start | bytes 589832 | tf_op jit(solution)/shard_map/ppermute | solution.py:439
  48.3 7.5 %collective-permute-start.11 = (bf16[128,768]{1,0:T(8,128)(2,1)S(1)}, bf16[128,768]{1,0:T(8,128)(2,1)S(1)}, u32[]{:S(2)}, u32[]{:S(2)}) collective-permute-start(bf16[128,768]{1,0:T(8,128)(2,1)S(1)} %slice_bitcast_fusion), channel_id=1, source_target_pairs={{0,4},{1,5},{2,6},{3,7},{4,0},{5,1},{6,2},{7,3},{8,12},{9,13},{10,... | collective-permute-start | bytes 589832 | tf_op jit(solution)/shard_map/ppermute | solution.py:439
  50.4 5.8 %collective-permute-start.9 = (bf16[128,768]{1,0:T(8,128)(2,1)S(1)}, bf16[128,768]{1,0:T(8,128)(2,1)S(1)}, u32[]{:S(2)}, u32[]{:S(2)}) collective-permute-start(bf16[128,768]{1,0:T(8,128)(2,1)S(1)} %slice_bitcast_fusion.1), channel_id=1, source_target_pairs={{0,12},{1,13},{2,14},{3,15},{4,8},{5,9},{6,10},{7,11},{8,4},{9,5},... | collective-permute-start | bytes 589832 | tf_op jit(solution)/shard_map/ppermute | solution.py:439
  52.4 3.8 %copy-start.7 = (bf16[2,128,768]{2,1,0:T(8,128)(2,1)S(1)}, bf16[2,128,768]{2,1,0:T(8,128)(2,1)}, u32[]{:S(2)}) copy-start(bf16[2,128,768]{2,1,0:T(8,128)(2,1)} %get-tuple-element.62) | copy-start | bytes 1179652
  53.8 33.0 %collective-permute-start.12 = (bf16[2,4,128,768]{3,2,1,0:T(8,128)(2,1)}, bf16[2,4,128,768]{3,2,1,0:T(8,128)(2,1)}, u32[]{:S(2)}, u32[]{:S(2)}) collective-permute-start(bf16[2,4,128,768]{3,2,1,0:T(8,128)(2,1)} %pad_maximum_fusion.refs_5_.refs_1_), channel_id=1, source_target_pairs={{0,4},{1,5},{2,6},{3,7},{4,0},{5,1},{6,2},{7,3},{8,12},{9,13},{10,... | collective-permute-start | bytes 4718600 | tf_op jit(solution)/shard_map/ppermute | solution.py:439
  56.3 6.8 %copy-start.13 = (bf16[16,256]{1,0:T(8,128)(2,1)S(1)}, bf16[16,256]{1,0:T(8,128)(2,1)}, u32[]{:S(2)}) copy-start(bf16[16,256]{1,0:T(8,128)(2,1)} %param.13) | copy-start | bytes 24580
  57.7 32.8 %collective-permute-start.13 = (bf16[2,4,128,768]{3,2,1,0:T(8,128)(2,1)}, bf16[2,4,128,768]{3,2,1,0:T(8,128)(2,1)}, u32[]{:S(2)}, u32[]{:S(2)}) collective-permute-start(bf16[2,4,128,768]{3,2,1,0:T(8,128)(2,1)} %pad_maximum_fusion.1.refs_6_), channel_id=1, source_target_pairs={{0,1},{1,0},{2,3},{3,2},{4,5},{5,4},{6,7},{7,6},{8,9},{9,8},{10,11... | collective-permute-start | bytes 4718600 | tf_op jit(solution)/shard_map/ppermute | solution.py:439
  58.5 33.1 %collective-permute-start.14 = (bf16[2,4,128,768]{3,2,1,0:T(8,128)(2,1)}, bf16[2,4,128,768]{3,2,1,0:T(8,128)(2,1)}, u32[]{:S(2)}, u32[]{:S(2)}) collective-permute-start(bf16[2,4,128,768]{3,2,1,0:T(8,128)(2,1)} %pad_maximum_fusion.refs_5_.refs_1_), channel_id=1, source_target_pairs={{0,12},{1,13},{2,14},{3,15},{4,8},{5,9},{6,10},{7,11},{8,4},{9,5},... | collective-permute-start | bytes 4718600 | tf_op jit(solution)/shard_map/ppermute | solution.py:439
  60.4 33.1 %collective-permute-start.15 = (bf16[2,4,128,768]{3,2,1,0:T(8,128)(2,1)}, bf16[2,4,128,768]{3,2,1,0:T(8,128)(2,1)}, u32[]{:S(2)}, u32[]{:S(2)}) collective-permute-start(bf16[2,4,128,768]{3,2,1,0:T(8,128)(2,1)} %pad_maximum_fusion.1.refs_6_), channel_id=1, source_target_pairs={{0,3},{1,2},{2,1},{3,0},{4,7},{5,6},{6,5},{7,4},{8,11},{9,10},{10,... | collective-permute-start | bytes 4718600 | tf_op jit(solution)/shard_map/ppermute | solution.py:439
  74.0 24.9 %collective-permute-start.20 = (bf16[2,128,768]{2,1,0:T(8,128)(2,1)}, bf16[2,128,768]{2,1,0:T(8,128)(2,1)S(1)}, u32[]{:S(2)}, u32[]{:S(2)}) collective-permute-start(bf16[2,128,768]{2,1,0:T(8,128)(2,1)} %get-tuple-element.68), channel_id=1, source_target_pairs={{0,1},{1,0},{2,3},{3,2},{4,5},{5,4},{6,7},{7,6},{8,9},{9,8},{10,11... | collective-permute-start | bytes 1179656 | tf_op jit(solution)/shard_map/ppermute | solution.py:439
  86.8 15.1 %collective-permute-start.23 = (bf16[2,128,768]{2,1,0:T(8,128)(2,1)}, bf16[2,128,768]{2,1,0:T(8,128)(2,1)S(1)}, u32[]{:S(2)}, u32[]{:S(2)}) collective-permute-start(bf16[2,128,768]{2,1,0:T(8,128)(2,1)} %get-tuple-element.75), channel_id=1, source_target_pairs={{0,3},{1,2},{2,1},{3,0},{4,7},{5,6},{6,5},{7,4},{8,11},{9,10},{10,... | collective-permute-start | bytes 1179656 | tf_op jit(solution)/shard_map/ppermute | solution.py:439
  96.3 22.7 %collective-permute-start.16 = (bf16[4,128,768]{2,1,0:T(8,128)(2,1)}, bf16[4,128,768]{2,1,0:T(8,128)(2,1)}, u32[]{:S(2)}, u32[]{:S(2)}) collective-permute-start(bf16[4,128,768]{2,1,0:T(8,128)(2,1)} %get-tuple-element.63), channel_id=1, source_target_pairs={{0,12},{1,13},{2,14},{3,15},{4,8},{5,9},{6,10},{7,11},{8,4},{9,5},... | collective-permute-start | bytes 2359304 | tf_op jit(solution)/shard_map/ppermute | solution.py:439
  96.9 23.6 %collective-permute-start.17 = (bf16[4,128,768]{2,1,0:T(8,128)(2,1)}, bf16[4,128,768]{2,1,0:T(8,128)(2,1)}, u32[]{:S(2)}, u32[]{:S(2)}) collective-permute-start(bf16[4,128,768]{2,1,0:T(8,128)(2,1)} %get-tuple-element.64), channel_id=1, source_target_pairs={{0,4},{1,5},{2,6},{3,7},{4,0},{5,1},{6,2},{7,3},{8,12},{9,13},{10,... | collective-permute-start | bytes 2359304 | tf_op jit(solution)/shard_map/ppermute | solution.py:439
  96.9 20.9 %collective-permute-start.26 = (bf16[2,128,768]{2,1,0:T(8,128)(2,1)}, bf16[2,128,768]{2,1,0:T(8,128)(2,1)}, u32[]{:S(2)}, u32[]{:S(2)}) collective-permute-start(bf16[2,128,768]{2,1,0:T(8,128)(2,1)} %get-tuple-element.81), channel_id=1, source_target_pairs={{0,4},{1,5},{2,6},{3,7},{4,0},{5,1},{6,2},{7,3},{8,12},{9,13},{10,... | collective-permute-start | bytes 1179656 | tf_op jit(solution)/shard_map/ppermute | solution.py:439
  98.9 18.9 %copy-start.2 = (bf16[2,128,768]{2,1,0:T(8,128)(2,1)}, bf16[2,128,768]{2,1,0:T(8,128)(2,1)S(1)}, u32[]{:S(2)}) copy-start(bf16[2,128,768]{2,1,0:T(8,128)(2,1)S(1)} %collective-permute-done.20.refs_1_.refs_2_) | copy-start | bytes 1179652
  98.9 21.8 %collective-permute-start.18 = (bf16[4,128,768]{2,1,0:T(8,128)(2,1)}, bf16[4,128,768]{2,1,0:T(8,128)(2,1)}, u32[]{:S(2)}, u32[]{:S(2)}) collective-permute-start(bf16[4,128,768]{2,1,0:T(8,128)(2,1)} %get-tuple-element.65), channel_id=1, source_target_pairs={{0,3},{1,2},{2,1},{3,0},{4,7},{5,6},{6,5},{7,4},{8,11},{9,10},{10,... | collective-permute-start | bytes 2359304 | tf_op jit(solution)/shard_map/ppermute | solution.py:439
  101.9 15.9 %copy-start.3 = (bf16[2,128,768]{2,1,0:T(8,128)(2,1)}, bf16[2,128,768]{2,1,0:T(8,128)(2,1)S(1)}, u32[]{:S(2)}) copy-start(bf16[2,128,768]{2,1,0:T(8,128)(2,1)S(1)} %collective-permute-done.23.refs_9_.refs_7_) | copy-start | bytes 1179652
  101.9 20.6 %collective-permute-start.19 = (bf16[4,128,768]{2,1,0:T(8,128)(2,1)}, bf16[4,128,768]{2,1,0:T(8,128)(2,1)}, u32[]{:S(2)}, u32[]{:S(2)}) collective-permute-start(bf16[4,128,768]{2,1,0:T(8,128)(2,1)} %get-tuple-element.66), channel_id=1, source_target_pairs={{0,1},{1,0},{2,3},{3,2},{4,5},{5,4},{6,7},{7,6},{8,9},{9,8},{10,11... | collective-permute-start | bytes 2359304 | tf_op jit(solution)/shard_map/ppermute | solution.py:439
  117.8 15.2 %collective-permute-start.21 = (bf16[4,128,768]{2,1,0:T(8,128)(2,1)}, bf16[4,128,768]{2,1,0:T(8,128)(2,1)S(1)}, u32[]{:S(2)}, u32[]{:S(2)}) collective-permute-start(bf16[4,128,768]{2,1,0:T(8,128)(2,1)} %get-tuple-element.71), channel_id=1, source_target_pairs={{0,1},{1,0},{2,3},{3,2},{4,5},{5,4},{6,7},{7,6},{8,9},{9,8},{10,11... | collective-permute-start | bytes 2359304 | tf_op jit(solution)/shard_map/ppermute | solution.py:439
  119.0 15.1 %collective-permute-start.24 = (bf16[4,128,768]{2,1,0:T(8,128)(2,1)}, bf16[4,128,768]{2,1,0:T(8,128)(2,1)}, u32[]{:S(2)}, u32[]{:S(2)}) collective-permute-start(bf16[4,128,768]{2,1,0:T(8,128)(2,1)} %get-tuple-element.77), channel_id=1, source_target_pairs={{0,3},{1,2},{2,1},{3,0},{4,7},{5,6},{6,5},{7,4},{8,11},{9,10},{10,... | collective-permute-start | bytes 2359304 | tf_op jit(solution)/shard_map/ppermute | solution.py:439
  120.5 13.7 %collective-permute-start.27 = (bf16[4,128,768]{2,1,0:T(8,128)(2,1)}, bf16[4,128,768]{2,1,0:T(8,128)(2,1)}, u32[]{:S(2)}, u32[]{:S(2)}) collective-permute-start(bf16[4,128,768]{2,1,0:T(8,128)(2,1)} %get-tuple-element.83), channel_id=1, source_target_pairs={{0,4},{1,5},{2,6},{3,7},{4,0},{5,1},{6,2},{7,3},{8,12},{9,13},{10,... | collective-permute-start | bytes 2359304 | tf_op jit(solution)/shard_map/ppermute | solution.py:439
  120.7 12.2 %collective-permute-start.29 = (bf16[2,128,768]{2,1,0:T(8,128)(2,1)}, bf16[2,128,768]{2,1,0:T(8,128)(2,1)}, u32[]{:S(2)}, u32[]{:S(2)}) collective-permute-start(bf16[2,128,768]{2,1,0:T(8,128)(2,1)} %get-tuple-element.87), channel_id=1, source_target_pairs={{0,12},{1,13},{2,14},{3,15},{4,8},{5,9},{6,10},{7,11},{8,4},{9,5},... | collective-permute-start | bytes 1179656 | tf_op jit(solution)/shard_map/ppermute | solution.py:439
  122.5 16.7 %collective-permute-start.30 = (bf16[4,128,768]{2,1,0:T(8,128)(2,1)}, bf16[4,128,768]{2,1,0:T(8,128)(2,1)}, u32[]{:S(2)}, u32[]{:S(2)}) collective-permute-start(bf16[4,128,768]{2,1,0:T(8,128)(2,1)} %get-tuple-element.89), channel_id=1, source_target_pairs={{0,12},{1,13},{2,14},{3,15},{4,8},{5,9},{6,10},{7,11},{8,4},{9,5},... | collective-permute-start | bytes 2359304 | tf_op jit(solution)/shard_map/ppermute | solution.py:439
  132.9 11.6 %collective-permute-start.22 = (bf16[2,128,768]{2,1,0:T(8,128)(2,1)}, bf16[2,128,768]{2,1,0:T(8,128)(2,1)}, u32[]{:S(2)}, u32[]{:S(2)}) collective-permute-start(bf16[2,128,768]{2,1,0:T(8,128)(2,1)} %get-tuple-element.73), channel_id=1, source_target_pairs={{0,1},{1,0},{2,3},{3,2},{4,5},{5,4},{6,7},{7,6},{8,9},{9,8},{10,11... | collective-permute-start | bytes 1179656 | tf_op jit(solution)/shard_map/ppermute | solution.py:439
  133.0 14.7 %copy-start.1 = (bf16[4,128,768]{2,1,0:T(8,128)(2,1)}, bf16[4,128,768]{2,1,0:T(8,128)(2,1)S(1)}, u32[]{:S(2)}) copy-start(bf16[4,128,768]{2,1,0:T(8,128)(2,1)S(1)} %collective-permute-done.21.refs_3_.refs_5_.refs_1_) | copy-start | bytes 2359300
  133.0 12.8 %collective-permute-start.25 = (bf16[2,128,768]{2,1,0:T(8,128)(2,1)}, bf16[2,128,768]{2,1,0:T(8,128)(2,1)}, u32[]{:S(2)}, u32[]{:S(2)}) collective-permute-start(bf16[2,128,768]{2,1,0:T(8,128)(2,1)} %get-tuple-element.79), channel_id=1, source_target_pairs={{0,3},{1,2},{2,1},{3,0},{4,7},{5,6},{6,5},{7,4},{8,11},{9,10},{10,... | collective-permute-start | bytes 1179656 | tf_op jit(solution)/shard_map/ppermute | solution.py:439
  134.2 11.6 %collective-permute-start.28 = (bf16[2,128,768]{2,1,0:T(8,128)(2,1)}, bf16[2,128,768]{2,1,0:T(8,128)(2,1)}, u32[]{:S(2)}, u32[]{:S(2)}) collective-permute-start(bf16[2,128,768]{2,1,0:T(8,128)(2,1)} %get-tuple-element.85), channel_id=1, source_target_pairs={{0,4},{1,5},{2,6},{3,7},{4,0},{5,1},{6,2},{7,3},{8,12},{9,13},{10,... | collective-permute-start | bytes 1179656 | tf_op jit(solution)/shard_map/ppermute | solution.py:439
  134.2 13.4 %collective-permute-start.31 = (bf16[2,128,768]{2,1,0:T(8,128)(2,1)}, bf16[2,128,768]{2,1,0:T(8,128)(2,1)}, u32[]{:S(2)}, u32[]{:S(2)}) collective-permute-start(bf16[2,128,768]{2,1,0:T(8,128)(2,1)} %get-tuple-element.91), channel_id=1, source_target_pairs={{0,12},{1,13},{2,14},{3,15},{4,8},{5,9},{6,10},{7,11},{8,4},{9,5},... | collective-permute-start | bytes 1179656 | tf_op jit(solution)/shard_map/ppermute | solution.py:439
  152.1 14.3 %collective-permute-start.32 = (bf16[4,128,768]{2,1,0:T(8,128)(2,1)}, bf16[4,128,768]{2,1,0:T(8,128)(2,1)S(1)}, u32[]{:S(2)}, u32[]{:S(2)}) collective-permute-start(bf16[4,128,768]{2,1,0:T(8,128)(2,1)} %get-tuple-element.92), channel_id=1, source_target_pairs={{0,3},{1,2},{2,1},{3,0},{4,7},{5,6},{6,5},{7,4},{8,11},{9,10},{10,... | collective-permute-start | bytes 2359304 | tf_op jit(solution)/shard_map/ppermute | solution.py:439
  153.2 13.3 %collective-permute-start.33 = (bf16[4,128,768]{2,1,0:T(8,128)(2,1)}, bf16[4,128,768]{2,1,0:T(8,128)(2,1)}, u32[]{:S(2)}, u32[]{:S(2)}) collective-permute-start(bf16[4,128,768]{2,1,0:T(8,128)(2,1)} %get-tuple-element.94), channel_id=1, source_target_pairs={{0,1},{1,0},{2,3},{3,2},{4,5},{5,4},{6,7},{7,6},{8,9},{9,8},{10,11... | collective-permute-start | bytes 2359304 | tf_op jit(solution)/shard_map/ppermute | solution.py:439
  153.3 13.5 %collective-permute-start.34 = (bf16[4,128,768]{2,1,0:T(8,128)(2,1)}, bf16[4,128,768]{2,1,0:T(8,128)(2,1)}, u32[]{:S(2)}, u32[]{:S(2)}) collective-permute-start(bf16[4,128,768]{2,1,0:T(8,128)(2,1)} %get-tuple-element.96), channel_id=1, source_target_pairs={{0,12},{1,13},{2,14},{3,15},{4,8},{5,9},{6,10},{7,11},{8,4},{9,5},... | collective-permute-start | bytes 2359304 | tf_op jit(solution)/shard_map/ppermute | solution.py:439
  155.1 11.6 %collective-permute-start.35 = (bf16[4,128,768]{2,1,0:T(8,128)(2,1)}, bf16[4,128,768]{2,1,0:T(8,128)(2,1)}, u32[]{:S(2)}, u32[]{:S(2)}) collective-permute-start(bf16[4,128,768]{2,1,0:T(8,128)(2,1)} %get-tuple-element.98), channel_id=1, source_target_pairs={{0,4},{1,5},{2,6},{3,7},{4,0},{5,1},{6,2},{7,3},{8,12},{9,13},{10,... | collective-permute-start | bytes 2359304 | tf_op jit(solution)/shard_map/ppermute | solution.py:439
  166.4 0.9 copy-start
  171.0 11.9 %collective-permute-start.36 = (bf16[2,128,768]{2,1,0:T(8,128)(2,1)}, bf16[2,128,768]{2,1,0:T(8,128)(2,1)S(1)}, u32[]{:S(2)}, u32[]{:S(2)}) collective-permute-start(bf16[2,128,768]{2,1,0:T(8,128)(2,1)} %get-tuple-element.99), channel_id=1, source_target_pairs={{0,4},{1,5},{2,6},{3,7},{4,0},{5,1},{6,2},{7,3},{8,12},{9,13},{10,... | collective-permute-start | bytes 1179656 | tf_op jit(solution)/shard_map/ppermute | solution.py:439
  172.9 10.0 %collective-permute-start.37 = (bf16[2,128,768]{2,1,0:T(8,128)(2,1)}, bf16[2,128,768]{2,1,0:T(8,128)(2,1)S(1)}, u32[]{:S(2)}, u32[]{:S(2)}) collective-permute-start(bf16[2,128,768]{2,1,0:T(8,128)(2,1)} %get-tuple-element.100), channel_id=1, source_target_pairs={{0,12},{1,13},{2,14},{3,15},{4,8},{5,9},{6,10},{7,11},{8,4},{9,5},... | collective-permute-start | bytes 1179656 | tf_op jit(solution)/shard_map/ppermute | solution.py:439
  173.5 9.4 %collective-permute-start.38 = (bf16[2,128,768]{2,1,0:T(8,128)(2,1)}, bf16[2,128,768]{2,1,0:T(8,128)(2,1)}, u32[]{:S(2)}, u32[]{:S(2)}) collective-permute-start(bf16[2,128,768]{2,1,0:T(8,128)(2,1)} %get-tuple-element.101), channel_id=1, source_target_pairs={{0,1},{1,0},{2,3},{3,2},{4,5},{5,4},{6,7},{7,6},{8,9},{9,8},{10,11... | collective-permute-start | bytes 1179656 | tf_op jit(solution)/shard_map/ppermute | solution.py:439
  175.1 8.2 %collective-permute-start.39 = (bf16[2,128,768]{2,1,0:T(8,128)(2,1)}, bf16[2,128,768]{2,1,0:T(8,128)(2,1)}, u32[]{:S(2)}, u32[]{:S(2)}) collective-permute-start(bf16[2,128,768]{2,1,0:T(8,128)(2,1)} %get-tuple-element.102), channel_id=1, source_target_pairs={{0,3},{1,2},{2,1},{3,0},{4,7},{5,6},{6,5},{7,4},{8,11},{9,10},{10,... | collective-permute-start | bytes 1179656 | tf_op jit(solution)/shard_map/ppermute | solution.py:439
  182.9 0.8 copy-start.4
  182.9 0.9 copy-start.5
  186.6 6.0 %collective-permute-start.40 = (bf16[1,128,768]{2,1,0:T(8,128)(2,1)}, bf16[1,128,768]{2,1,0:T(8,128)(2,1)S(1)}, u32[]{:S(2)}, u32[]{:S(2)}) collective-permute-start(bf16[1,128,768]{2,1,0:T(8,128)(2,1)} %get-tuple-element.103), channel_id=1, source_target_pairs={{0,12},{1,13},{2,14},{3,15},{4,8},{5,9},{6,10},{7,11},{8,4},{9,5},... | collective-permute-start | bytes 589832 | tf_op jit(solution)/shard_map/ppermute | solution.py:439
  187.9 7.1 %collective-permute-start.41 = (bf16[1,128,768]{2,1,0:T(8,128)(2,1)}, bf16[1,128,768]{2,1,0:T(8,128)(2,1)S(1)}, u32[]{:S(2)}, u32[]{:S(2)}) collective-permute-start(bf16[1,128,768]{2,1,0:T(8,128)(2,1)} %get-tuple-element.104), channel_id=1, source_target_pairs={{0,4},{1,5},{2,6},{3,7},{4,0},{5,1},{6,2},{7,3},{8,12},{9,13},{10,... | collective-permute-start | bytes 589832 | tf_op jit(solution)/shard_map/ppermute | solution.py:439
  188.2 6.8 %collective-permute-start.42 = (bf16[1,128,768]{2,1,0:T(8,128)(2,1)}, bf16[1,128,768]{2,1,0:T(8,128)(2,1)S(1)}, u32[]{:S(2)}, u32[]{:S(2)}) collective-permute-start(bf16[1,128,768]{2,1,0:T(8,128)(2,1)} %get-tuple-element.105), channel_id=1, source_target_pairs={{0,3},{1,2},{2,1},{3,0},{4,7},{5,6},{6,5},{7,4},{8,11},{9,10},{10,... | collective-permute-start | bytes 589832 | tf_op jit(solution)/shard_map/ppermute | solution.py:439
  190.1 6.5 %collective-permute-start.43 = (bf16[1,128,768]{2,1,0:T(8,128)(2,1)}, bf16[1,128,768]{2,1,0:T(8,128)(2,1)S(1)}, u32[]{:S(2)}, u32[]{:S(2)}) collective-permute-start(bf16[1,128,768]{2,1,0:T(8,128)(2,1)} %get-tuple-element.106), channel_id=1, source_target_pairs={{0,1},{1,0},{2,3},{3,2},{4,5},{5,4},{6,7},{7,6},{8,9},{9,8},{10,11... | collective-permute-start | bytes 589832 | tf_op jit(solution)/shard_map/ppermute | solution.py:439
  192.7 4.0 %copy-start.9 = (bf16[1,128,768]{2,1,0:T(8,128)(2,1)}, bf16[1,128,768]{2,1,0:T(8,128)(2,1)S(1)}, u32[]{:S(2)}) copy-start(bf16[1,128,768]{2,1,0:T(8,128)(2,1)S(1)} %collective-permute-done.40.refs_5_) | copy-start | bytes 589828
  195.0 1.6 copy-start.10
  195.0 1.6 copy-start.11
  196.6 0.7 copy-start.12
  201.7 38.4 %all-to-all-start.1 = ((bf16[8,96,768]{2,1,0:T(8,128)(2,1)}), bf16[8,96,768]{2,1,0:T(8,128)(2,1)}, u32[]{:S(2)}, u32[]{:S(2)}) async-start(bf16[8,96,768]{2,1,0:T(8,128)(2,1)} %leave_rows.1), calls=%async_computation.1 | async-start | bytes 2359296 | tf_op jit(solution)/shard_map/all_to_all | solution.py:574

commit v5 on v4

--- a/solution.py
+++ b/solution.py
@@ -366,7 +366,7 @@
     table_ref = refs[0]
     x_refs = refs[1 : 1 + n_arrays]
     s_refs = refs[1 + n_arrays : 1 + n_arrays + n_signals]
-    grad_ref, x_all, s_all, total_ref, x_sem, s_sem = refs[1 + n_arrays + n_signals :]
+    grad_ref, x_all, s_all, total_ref, grad_buf, x_sem, s_sem, grad_sem = refs[1 + n_arrays + n_signals :]
     rows = x_all.shape[1] // STREAMS
     for rel, pieces in enumerate(parts):
         for pair, (sources, signal, unit) in enumerate(pieces):
@@ -397,7 +397,12 @@
         return carry
 
     lax.fori_loop(0, len(parts), batch, 0)
-    grad_ref[...] = total_ref[...].astype(BF)
+    stores = [pltpu.make_async_copy(grad_buf.at[p], grad_ref.at[p], grad_sem.at[p]) for p in range(grad_buf.shape[0])]
+    for p, store in enumerate(stores):
+        grad_buf[p] = total_ref[p].astype(BF)
+        store.start()
+    for store in stores:
+        store.wait()
 
 
 def panel_sum(table, arrays, signals, parts, shape):
@@ -408,14 +413,16 @@
     return pl.pallas_call(
         functools.partial(panel_body, parts, len(arrays), len(signals)),
         in_specs=[scalar] + [loose] * (len(arrays) + len(signals)),
-        out_specs=pl.BlockSpec(memory_space=pltpu.VMEM),
+        out_specs=loose,
         out_shape=jax.ShapeDtypeStruct(shape, BF),
         scratch_shapes=[
             pltpu.VMEM((len(parts), rows, width), BF),
             pltpu.VMEM((len(parts), CAP, lanes, rows), BF),
             pltpu.VMEM(shape, F32),
+            pltpu.VMEM(shape, BF),
             pltpu.SemaphoreType.DMA((len(parts),)),
             pltpu.SemaphoreType.DMA((len(parts),)),
+            pltpu.SemaphoreType.DMA((count,)),
         ],
         compiler_params=params(LIMIT),
         cost_estimate=pl.CostEstimate(

time: 244 us -> 244 us (level)
  waiting for transfers between devices: 59.4 us -> 62.3 us
where the time goes in v5:
time: 244 us; the launch traced here: 243 us
  Pallas kernels  88.9 us (36%)
  starting transfers between devices  82.2 us (34%)
  waiting for transfers between devices  62.3 us (26%)
  other arithmetic  4.64 us (2%)
  local copies, waits for them, and re-layouts  4.04 us (2%)
    ppermute x44, waiting for transfers between devices, swap(): return lax.ppermute(array, 'label', [(i, i ^ mask) for i in range(owners)])  58.1 us
    ppermute x44, starting transfers between devices, swap(): return lax.ppermute(array, 'label', [(i, i ^ mask) for i in range(owners)])  55.9 us
    pallas_call x4, Pallas kernels, work(): pl.pallas_call(functools.partial(work_body, units, len(arrays), len(out_b...  46.3 us
    all_to_all x1, starting transfers between devices, shards(): lax.all_to_all(leaving, 'dp', split_axis=0, concat_axis=0, tiled=True)  20.5 us
    pallas_call x1, Pallas kernels, panel_sum(): pl.pallas_call(functools.partial(panel_body, parts, len(arrays), len(sign...  14.2 us
    pallas_call x3, Pallas kernels, merge(): pl.pallas_call(functools.partial(merge_body, [[[0] * len(t) for t in b] f...  10.9 us
    all_to_all x1, starting transfers between devices, shards(): lax.all_to_all(outgoing, 'dp', split_axis=0, concat_axis=0, tiled=True)  5.81 us
  transfers between devices with their start and end apart: 46, of which 25 were waited for; matrix products, arithmetic and copies ran while one was open for 3% of the time, Pallas kernels for 26%

profile of v5, /device:TPU:1, one launch (start us, length us, event | category | flops | bytes accessed | tf_op | source)
XLA Modules:
  0.0 243.0 jit_solution(10765391200560226523)
XLA Ops:
  2.0 3.7 %pack_rows.1 = (bf16[8,112,768]{2,1,0:T(8,128)(2,1)}, s32[1,512]{1,0:T(1,128)}) custom-call(bf16[512,768]{1,0:T(8,128)(2,1)} %x_ref.1, s32[1,512]{1,0:T(1,128)} %bitcast.76), custom_call_target="tpu_custom_call" | custom-call | tf_op jit(solution)/shard_map/pack_rows/pallas_call | solution.py:56
  5.7 5.8 %all-to-all-start = ((bf16[8,112,768]{2,1,0:T(8,128)(2,1)}), bf16[8,112,768]{2,1,0:T(8,128)(2,1)}, u32[]{:S(2)}, u32[]{:S(2)}) async-start(bf16[8,112,768]{2,1,0:T(8,128)(2,1)} %get-tuple-element.58), calls=%async_computation | async-start | bytes 2752512 | tf_op jit(solution)/shard_map/all_to_all | solution.py:467
  11.5 1.6 collective-permute-start
  13.2 1.1 collective-permute-done
  14.3 3.6 %collective-permute-start.1 = (bf16[2,2,16,256]{3,2,1,0:T(8,128)(2,1)S(1)}, bf16[2,2,16,256]{3,2,1,0:T(8,128)(2,1)S(1)}, u32[]{:S(2)}, u32[]{:S(2)}) collective-permute-start(bf16[2,2,16,256]{3,2,1,0:T(8,128)(2,1)S(1)} %pad_maximum_fusion.4), channel_id=1, source_target_pairs={{0,3},{1,2},{2,1},{3,0},{4,7},{5,6},{6,5},{7,4},{8,11},{9,10},{10,... | collective-permute-start | bytes 98312 | tf_op jit(solution)/shard_map/ppermute | solution.py:446
  17.9 1.3 collective-permute-done.1
  19.2 1.4 collective-permute-start.2
  20.6 2.2 collective-permute-done.2
  22.8 2.8 %collective-permute-start.3 = (bf16[8,2,16,256]{3,2,1,0:T(8,128)(2,1)S(1)}, bf16[8,2,16,256]{3,2,1,0:T(8,128)(2,1)S(1)}, u32[]{:S(2)}, u32[]{:S(2)}) collective-permute-start(bf16[8,2,16,256]{3,2,1,0:T(8,128)(2,1)S(1)} %pad_maximum_fusion.2), channel_id=1, source_target_pairs={{0,12},{1,13},{2,14},{3,15},{4,8},{5,9},{6,10},{7,11},{8,4},{9,5},... | collective-permute-start | bytes 393224 | tf_op jit(solution)/shard_map/ppermute | solution.py:446
  25.6 2.7 %collective-permute-done.3 = bf16[8,2,16,256]{3,2,1,0:T(8,128)(2,1)S(1)} collective-permute-done((bf16[8,2,16,256]{3,2,1,0:T(8,128)(2,1)S(1)}, bf16[8,2,16,256]{3,2,1,0:T(8,128)(2,1)S(1)}, u32[]{:S(2)}, u32[]{:S(2)}) %collective-permute-start.3) | collective-permute-done | bytes 131104 | tf_op jit(solution)/shard_map/ppermute | solution.py:446
  28.4 1.8 all-to-all-done.arrived_ref
  30.2 3.6 %land_rows.1 = (bf16[768,512]{1,0:T(8,128)(2,1)}, bf16[2,128,768]{2,1,0:T(8,128)(2,1)}, bf16[2,128,768]{2,1,0:T(8,128)(2,1)}) custom-call(bf16[8,112,768]{2,1,0:T(8,128)(2,1)} %all-to-all-done.arrived_ref, bf16[16,2,16,256]{3,2,1,0:T(8,128)(2,1)} %copy-done.6), custom_call_target="tpu_custom_call" | custom-call | tf_op jit(solution)/shard_map/land_rows/pallas_call | solution.py:85
  33.8 3.8 %collective-permute-start.6 = (bf16[2,128,768]{2,1,0:T(8,128)(2,1)}, bf16[2,128,768]{2,1,0:T(8,128)(2,1)S(1)}, u32[]{:S(2)}, u32[]{:S(2)}) collective-permute-start(bf16[2,128,768]{2,1,0:T(8,128)(2,1)} %get-tuple-element.61), channel_id=1, source_target_pairs={{0,3},{1,2},{2,1},{3,0},{4,7},{5,6},{6,5},{7,4},{8,11},{9,10},{10,... | collective-permute-start | bytes 1179656 | tf_op jit(solution)/shard_map/ppermute | solution.py:446
  37.6 2.7 %collective-permute-start.10 = (bf16[2,128,768]{2,1,0:T(8,128)(2,1)}, bf16[2,128,768]{2,1,0:T(8,128)(2,1)S(1)}, u32[]{:S(2)}, u32[]{:S(2)}) collective-permute-start(bf16[2,128,768]{2,1,0:T(8,128)(2,1)} %get-tuple-element.62), channel_id=1, source_target_pairs={{0,12},{1,13},{2,14},{3,15},{4,8},{5,9},{6,10},{7,11},{8,4},{9,5},... | collective-permute-start | bytes 1179656 | tf_op jit(solution)/shard_map/ppermute | solution.py:446
  40.3 5.4 %collective-permute-done.6 = bf16[2,128,768]{2,1,0:T(8,128)(2,1)S(1)} collective-permute-done((bf16[2,128,768]{2,1,0:T(8,128)(2,1)}, bf16[2,128,768]{2,1,0:T(8,128)(2,1)S(1)}, u32[]{:S(2)}, u32[]{:S(2)}) %collective-permute-start.6) | collective-permute-done | bytes 393248 | tf_op jit(solution)/shard_map/ppermute | solution.py:446
  46.6 1.7 collective-permute-start.5
  48.3 2.1 collective-permute-start.11
  50.4 2.0 collective-permute-start.9
  52.4 1.3 pad_maximum_fusion.refs_5_.refs_1_
  53.8 2.0 collective-permute-start.12
  56.3 1.4 pad_maximum_fusion.1.refs_6_
  58.5 1.9 collective-permute-start.14
  63.1 1.6 broadcast_in_dim.37.refs_4_
  64.7 9.4 %work_near.1 = (bf16[1,128,768]{2,1,0:T(8,128)(2,1)}, bf16[2,128,768]{2,1,0:T(8,128)(2,1)}, bf16[1,128,768]{2,1,0:T(8,128)(2,1)}, bf16[2,128,768]{2,1,0:T(8,128)...) custom-call(s32[16,4]{1,0:T(8,128)} %copy.29.refs_0_, ...), custom_call_target="tpu_custom_call" | custom-call | flops 3623878656 | bytes 11796480 | tf_op jit(solution)/shard_map/work_near/pallas_call | solution.py:334
  74.7 12.1 %collective-permute-done.12.refs_0_.refs_7_.refs_5_.refs_2_ = bf16[2,4,128,768]{3,2,1,0:T(8,128)(2,1)} collective-permute-done((bf16[2,4,128,768]{3,2,1,0:T(8,128)(2,1)}, bf16[2,4,128,768]{3,2,1,0:T(8,128)(2,1)}, u32[]{:S(2)}, u32[]{:S(2)}) %collective-permute-start.12) | collective-permute-done | bytes 1572896 | tf_op jit(solution)/shard_map/ppermute | solution.py:446
  86.8 2.3 collective-permute-start.23
  89.1 1.4 collective-permute-done.13.refs_2_.refs_8_.refs_6_.refs_7_
  90.4 1.1 collective-permute-done.14.refs_1_.refs_9_.refs_7_.refs_3_
  91.6 1.9 collective-permute-done.15.refs_3_.refs_10_.refs_8_
  93.5 2.8 %cut_halves.1 = (bf16[4,128,768]{2,1,0:T(8,128)(2,1)}, bf16[4,128,768]{2,1,0:T(8,128)(2,1)}, bf16[4,128,768]{2,1,0:T(8,128)(2,1)}, bf16[4,128,768]{2,1,0:T(8,128)(2,1)}) custom-call(bf16[2,4,128,768]{3,2,1,0:T(8,128)(2,1)} %collective-permute-done.12.refs_0_.refs_7_.refs_5_.refs_2_, ...), custom_call_target="tpu_custom_call" | custom-call | tf_op jit(solution)/shard_map/cut_halves/pallas_call | solution.py:192
  96.9 1.5 collective-permute-start.26
  98.9 1.2 collective-permute-start.18
  100.1 1.8 collective-permute-done.23.refs_9_.refs_7_
  102.2 15.9 %work_far.1 = (bf16[2,128,768]{2,1,0:T(8,128)(2,1)}, bf16[4,128,768]{2,1,0:T(8,128)(2,1)}, bf16[2,128,768]{2,1,0:T(8,128)(2,1)}, bf16[4,128,768]{2,1,0:T(8,128)(...) custom-call(s32[16,4]{1,0:T(8,128)} %copy.29.refs_0_, ...), custom_call_target="tpu_custom_call" | custom-call | flops 7247757312 | bytes 17301504 | tf_op jit(solution)/shard_map/work_far/pallas_call | solution.py:334
  118.2 1.1 collective-permute-start.21
  119.3 1.5 collective-permute-start.24
  120.8 1.4 collective-permute-start.29
  122.2 1.3 collective-permute-start.30
  123.6 9.5 %work_last.1 = (bf16[1,128,768]{2,1,0:T(8,128)(2,1)}, bf16[2,128,768]{2,1,0:T(8,128)(2,1)}, bf16[1,128,768]{2,1,0:T(8,128)(2,1)}, bf16[2,128,768]{2,1,0:T(8,128)...) custom-call(s32[16,4]{1,0:T(8,128)} %copy.29.refs_0_, ...), custom_call_target="tpu_custom_call" | custom-call | flops 3623878656 | bytes 11796480 | tf_op jit(solution)/shard_map/work_last/pallas_call | solution.py:334
  133.1 1.3 collective-permute-start.25
  134.6 1.5 collective-permute-start.31
  136.1 3.8 %collective-permute-done.30.refs_27_.refs_29_.refs_19_.refs_13_ = bf16[4,128,768]{2,1,0:T(8,128)(2,1)} collective-permute-done((bf16[4,128,768]{2,1,0:T(8,128)(2,1)}, bf16[4,128,768]{2,1,0:T(8,128)(2,1)}, u32[]{:S(2)}, u32[]{:S(2)}) %collective-permute-start.30) | collective-permute-done | bytes 786464 | tf_op jit(solution)/shard_map/ppermute | solution.py:446
  139.9 4.5 %collective-permute-done.22.refs_7_.refs_4_ = bf16[2,128,768]{2,1,0:T(8,128)(2,1)} collective-permute-done((bf16[2,128,768]{2,1,0:T(8,128)(2,1)}, bf16[2,128,768]{2,1,0:T(8,128)(2,1)}, u32[]{:S(2)}, u32[]{:S(2)}) %collective-permute-start.22) | collective-permute-done | bytes 393248 | tf_op jit(solution)/shard_map/ppermute | solution.py:446
  144.4 1.6 collective-permute-done.25.refs_15_.refs_10_
  146.0 2.4 collective-permute-done.31.refs_31_.refs_22_
  148.3 4.4 %merge_1.1 = (bf16[4,128,768]{2,1,0:T(8,128)(2,1)}, bf16[4,128,768]{2,1,0:T(8,128)(2,1)}, bf16[4,128,768]{2,1,0:T(8,128)(2,1)}, bf16[4,128,768]{2,1,0:T(8,128)(2,1)}) custom-call(bf16[1,128,768]{2,1,0:T(8,128)(2,1)} %get-tuple-element.69.refs_0_, bf16[2,128,768]{2,1,0:T(8,128)(2,1)} %copy-done.2, bf16[2,128,768]{2,1,0:T(8,128)(2,1)} %get-tuple-element.70.refs_2_.refs_4_, ...), custom_call_target="tpu_custom_call" | custom-call | bytes 9437184 | tf_op jit(solution)/shard_map/merge_1/pallas_call | solution.py:145
  153.5 1.3 collective-permute-start.34
  154.8 11.5 %work_kept.1 = (bf16[4,128,768]{2,1,0:T(8,128)(2,1)}, bf16[4,128,768]{2,1,0:T(8,128)(2,1)}, bf16[4,128,768]{2,1,0:T(8,128)(2,1)}, bf16[4,128,768]{2,1,0:T(8,128)(2,1)}, bf16[8,2,256,256]{3,2,1,0:T(8,128)(2,1)}) custom-call(s32[16,4]{1,0:T(8,128)} %copy.29.refs_0_, s32[2,8]{1,0:T(2,128)} %constant.77.clone.refs_1_, bf16[16,2,16,256]{3,2,1,0:T(8,128)(2,1)} %copy-done.6, ...), custom_call_target="tpu_custom_call" | custom-call | flops 4831838208 | bytes 13631488 | tf_op jit(solution)/shard_map/work_kept/pallas_call | solution.py:334
  167.2 3.6 %merge_2.1 = (bf16[2,128,768]{2,1,0:T(8,128)(2,1)}, bf16[2,128,768]{2,1,0:T(8,128)(2,1)}, bf16[2,128,768]{2,1,0:T(8,128)(2,1)}, bf16[2,128,768]{2,1,0:T(8,128)(2,1)}) custom-call(bf16[4,128,768]{2,1,0:T(8,128)(2,1)} %get-tuple-element.67.refs_0_.refs_3_.refs_1_, bf16[4,128,768]{2,1,0:T(8,128)(2,1)} %copy-done.1, bf16[4,128,768]{2,1,0:T(8,128)(2,1)} %copy-done, ...), custom_call_target="tpu_custom_call" | custom-call | bytes 6291456 | tf_op jit(solution)/shard_map/merge_2/pallas_call | solution.py:145
  170.8 1.5 collective-permute-start.36
  172.4 1.3 collective-permute-start.37
  173.6 1.5 collective-permute-start.38
  175.1 2.1 collective-permute-start.39
  177.2 5.3 %collective-permute-done.36.refs_3_.refs_4_ = bf16[2,128,768]{2,1,0:T(8,128)(2,1)S(1)} collective-permute-done((bf16[2,128,768]{2,1,0:T(8,128)(2,1)}, bf16[2,128,768]{2,1,0:T(8,128)(2,1)S(1)}, u32[]{:S(2)}, u32[]{:S(2)}) %collective-permute-start.36) | collective-permute-done | bytes 393248 | tf_op jit(solution)/shard_map/ppermute | solution.py:446
  183.3 2.9 %merge_3.1 = (bf16[1,128,768]{2,1,0:T(8,128)(2,1)}, bf16[1,128,768]{2,1,0:T(8,128)(2,1)}, bf16[1,128,768]{2,1,0:T(8,128)(2,1)}, bf16[1,128,768]{2,1,0:T(8,128)(2,1)}) custom-call(bf16[4,128,768]{2,1,0:T(8,128)(2,1)} %get-tuple-element.67.refs_0_.refs_3_.refs_1_, bf16[4,128,768]{2,1,0:T(8,128)(2,1)} %copy-done.1, bf16[4,128,768]{2,1,0:T(8,128)(2,1)} %copy-done, ...), custom_call_target="tpu_custom_call" | custom-call | bytes 3932160 | tf_op jit(solution)/shard_map/merge_3/pallas_call | solution.py:145
  186.2 1.7 collective-permute-start.40
  188.4 2.2 collective-permute-start.42
  192.2 2.7 %collective-permute-done.41.refs_10_ = bf16[1,128,768]{2,1,0:T(8,128)(2,1)S(1)} collective-permute-done((bf16[1,128,768]{2,1,0:T(8,128)(2,1)}, bf16[1,128,768]{2,1,0:T(8,128)(2,1)S(1)}, u32[]{:S(2)}, u32[]{:S(2)}) %collective-permute-start.41) | collective-permute-done | bytes 196640 | tf_op jit(solution)/shard_map/ppermute | solution.py:446
  194.9 2.9 %collective-permute-done.43.refs_20_ = bf16[1,128,768]{2,1,0:T(8,128)(2,1)S(1)} collective-permute-done((bf16[1,128,768]{2,1,0:T(8,128)(2,1)}, bf16[1,128,768]{2,1,0:T(8,128)(2,1)S(1)}, u32[]{:S(2)}, u32[]{:S(2)}) %collective-permute-start.43) | collective-permute-done | bytes 196640 | tf_op jit(solution)/shard_map/ppermute | solution.py:446
  198.5 4.4 %leave_rows.1 = bf16[8,96,768]{2,1,0:T(8,128)(2,1)} custom-call(bf16[768,512]{1,0:T(8,128)(2,1)} %get-tuple-element.60.refs_0_, bf16[4,128,768]{2,1,0:T(8,128)(2,1)} %get-tuple-element.67.refs_0_.refs_3_.refs_1_, bf16[2,128,768]{2,1,0:T(8,128)(2,1)} %copy-done.2, bf16[4,128,768]{2,1,0:T(8,128)(2,1)} %copy-done, bf16[2,128,768]{2,1,0:T(8,128)(2,1)} %copy-done.4, ...), custom_call_target="tpu_custom_call" | custom-call | tf_op jit(solution)/shard_map/leave_rows/pallas_call | solution.py:115
  202.9 20.5 %all-to-all-start.1 = ((bf16[8,96,768]{2,1,0:T(8,128)(2,1)}), bf16[8,96,768]{2,1,0:T(8,128)(2,1)}, u32[]{:S(2)}, u32[]{:S(2)}) async-start(bf16[8,96,768]{2,1,0:T(8,128)(2,1)} %leave_rows.1), calls=%async_computation.1 | async-start | bytes 2359296 | tf_op jit(solution)/shard_map/all_to_all | solution.py:581
  223.4 14.2 %panel_grad.1 = bf16[16,256,768]{2,1,0:T(8,128)(2,1)} custom-call(s32[16,4]{1,0:T(8,128)} %copy.29.refs_0_, bf16[2,4,128,768]{3,2,1,0:T(8,128)(2,1)} %pad_maximum_fusion.refs_5_.refs_1_, bf16[2,4,128,768]{3,2,1,0:T(8,128)(2,1)} %collective-permute-done.12.refs_0_.refs_7_.refs_5_.refs_2_, ...), custom_call_target="tpu_custom_call" | custom-call | flops 6442450944 | bytes 27262976 | tf_op jit(solution)/shard_map/panel_grad/pallas_call | solution.py:413
  237.6 2.4 all-to-all-done.1.back_ref
  240.0 3.0 %home_rows.1 = bf16[512,768]{1,0:T(8,128)(2,1)} custom-call(bf16[8,96,768]{2,1,0:T(8,128)(2,1)} %all-to-all-done.1.back_ref, s32[1,512]{1,0:T(1,128)} %get-tuple-element.107.rank_ref), custom_call_target="tpu_custom_call" | custom-call | tf_op jit(solution)/shard_map/home_rows/pallas_call | solution.py:167
  (96 shorter events, 14.0 us)
Async XLA Ops:
  5.7 24.5 %all-to-all-start = ((bf16[8,112,768]{2,1,0:T(8,128)(2,1)}), bf16[8,112,768]{2,1,0:T(8,128)(2,1)}, u32[]{:S(2)}, u32[]{:S(2)}) async-start(bf16[8,112,768]{2,1,0:T(8,128)(2,1)} %get-tuple-element.58), calls=%async_computation | async-start | bytes 2752512 | tf_op jit(solution)/shard_map/all_to_all | solution.py:467
  11.5 2.8 %collective-permute-start = (bf16[1,2,16,256]{3,2,1,0:T(8,128)(2,1)S(1)}, bf16[1,2,16,256]{3,2,1,0:T(8,128)(2,1)S(1)}, u32[]{:S(2)}, u32[]{:S(2)}) collective-permute-start(bf16[1,2,16,256]{3,2,1,0:T(8,128)(2,1)S(1)} %fusion), channel_id=1, source_target_pairs={{0,1},{1,0},{2,3},{3,2},{4,5},{5,4},{6,7},{7,6},{8,9},{9,8},{10,11... | collective-permute-start | bytes 49160 | tf_op jit(solution)/shard_map/ppermute | solution.py:446
  14.3 4.9 %collective-permute-start.1 = (bf16[2,2,16,256]{3,2,1,0:T(8,128)(2,1)S(1)}, bf16[2,2,16,256]{3,2,1,0:T(8,128)(2,1)S(1)}, u32[]{:S(2)}, u32[]{:S(2)}) collective-permute-start(bf16[2,2,16,256]{3,2,1,0:T(8,128)(2,1)S(1)} %pad_maximum_fusion.4), channel_id=1, source_target_pairs={{0,3},{1,2},{2,1},{3,0},{4,7},{5,6},{6,5},{7,4},{8,11},{9,10},{10,... | collective-permute-start | bytes 98312 | tf_op jit(solution)/shard_map/ppermute | solution.py:446
  19.2 3.6 %collective-permute-start.2 = (bf16[4,2,16,256]{3,2,1,0:T(8,128)(2,1)S(1)}, bf16[4,2,16,256]{3,2,1,0:T(8,128)(2,1)S(1)}, u32[]{:S(2)}, u32[]{:S(2)}) collective-permute-start(bf16[4,2,16,256]{3,2,1,0:T(8,128)(2,1)S(1)} %pad_maximum_fusion.3), channel_id=1, source_target_pairs={{0,4},{1,5},{2,6},{3,7},{4,0},{5,1},{6,2},{7,3},{8,12},{9,13},{10,... | collective-permute-start | bytes 196616 | tf_op jit(solution)/shard_map/ppermute | solution.py:446
  22.8 5.6 %collective-permute-start.3 = (bf16[8,2,16,256]{3,2,1,0:T(8,128)(2,1)S(1)}, bf16[8,2,16,256]{3,2,1,0:T(8,128)(2,1)S(1)}, u32[]{:S(2)}, u32[]{:S(2)}) collective-permute-start(bf16[8,2,16,256]{3,2,1,0:T(8,128)(2,1)S(1)} %pad_maximum_fusion.2), channel_id=1, source_target_pairs={{0,12},{1,13},{2,14},{3,15},{4,8},{5,9},{6,10},{7,11},{8,4},{9,5},... | collective-permute-start | bytes 393224 | tf_op jit(solution)/shard_map/ppermute | solution.py:446
  28.4 1.8 copy-start.6
  33.8 18.6 %copy-start.8 = (bf16[2,128,768]{2,1,0:T(8,128)(2,1)S(1)}, bf16[2,128,768]{2,1,0:T(8,128)(2,1)}, u32[]{:S(2)}) copy-start(bf16[2,128,768]{2,1,0:T(8,128)(2,1)} %get-tuple-element.61) | copy-start | bytes 1179652
  33.8 11.9 %collective-permute-start.6 = (bf16[2,128,768]{2,1,0:T(8,128)(2,1)}, bf16[2,128,768]{2,1,0:T(8,128)(2,1)S(1)}, u32[]{:S(2)}, u32[]{:S(2)}) collective-permute-start(bf16[2,128,768]{2,1,0:T(8,128)(2,1)} %get-tuple-element.61), channel_id=1, source_target_pairs={{0,3},{1,2},{2,1},{3,0},{4,7},{5,6},{6,5},{7,4},{8,11},{9,10},{10,... | collective-permute-start | bytes 1179656 | tf_op jit(solution)/shard_map/ppermute | solution.py:446
  37.6 9.0 %collective-permute-start.4 = (bf16[2,128,768]{2,1,0:T(8,128)(2,1)}, bf16[2,128,768]{2,1,0:T(8,128)(2,1)S(1)}, u32[]{:S(2)}, u32[]{:S(2)}) collective-permute-start(bf16[2,128,768]{2,1,0:T(8,128)(2,1)} %get-tuple-element.61), channel_id=1, source_target_pairs={{0,1},{1,0},{2,3},{3,2},{4,5},{5,4},{6,7},{7,6},{8,9},{9,8},{10,11... | collective-permute-start | bytes 1179656 | tf_op jit(solution)/shard_map/ppermute | solution.py:446
  37.6 10.7 %collective-permute-start.10 = (bf16[2,128,768]{2,1,0:T(8,128)(2,1)}, bf16[2,128,768]{2,1,0:T(8,128)(2,1)S(1)}, u32[]{:S(2)}, u32[]{:S(2)}) collective-permute-start(bf16[2,128,768]{2,1,0:T(8,128)(2,1)} %get-tuple-element.62), channel_id=1, source_target_pairs={{0,12},{1,13},{2,14},{3,15},{4,8},{5,9},{6,10},{7,11},{8,4},{9,5},... | collective-permute-start | bytes 1179656 | tf_op jit(solution)/shard_map/ppermute | solution.py:446
  40.3 10.1 %collective-permute-start.8 = (bf16[2,128,768]{2,1,0:T(8,128)(2,1)}, bf16[2,128,768]{2,1,0:T(8,128)(2,1)S(1)}, u32[]{:S(2)}, u32[]{:S(2)}) collective-permute-start(bf16[2,128,768]{2,1,0:T(8,128)(2,1)} %get-tuple-element.62), channel_id=1, source_target_pairs={{0,4},{1,5},{2,6},{3,7},{4,0},{5,1},{6,2},{7,3},{8,12},{9,13},{10,... | collective-permute-start | bytes 1179656 | tf_op jit(solution)/shard_map/ppermute | solution.py:446
  45.7 6.7 %collective-permute-start.7 = (bf16[128,768]{1,0:T(8,128)(2,1)S(1)}, bf16[128,768]{1,0:T(8,128)(2,1)S(1)}, u32[]{:S(2)}, u32[]{:S(2)}) collective-permute-start(bf16[128,768]{1,0:T(8,128)(2,1)S(1)} %slice_bitcast_fusion.2), channel_id=1, source_target_pairs={{0,1},{1,0},{2,3},{3,2},{4,5},{5,4},{6,7},{7,6},{8,9},{9,8},{10,11... | collective-permute-start | bytes 589832 | tf_op jit(solution)/shard_map/ppermute | solution.py:446
  46.6 5.8 %collective-permute-start.5 = (bf16[128,768]{1,0:T(8,128)(2,1)S(1)}, bf16[128,768]{1,0:T(8,128)(2,1)S(1)}, u32[]{:S(2)}, u32[]{:S(2)}) collective-permute-start(bf16[128,768]{1,0:T(8,128)(2,1)S(1)} %slice_bitcast_fusion.3), channel_id=1, source_target_pairs={{0,3},{1,2},{2,1},{3,0},{4,7},{5,6},{6,5},{7,4},{8,11},{9,10},{10,... | collective-permute-start | bytes 589832 | tf_op jit(solution)/shard_map/ppermute | solution.py:446
  48.3 7.5 %collective-permute-start.11 = (bf16[128,768]{1,0:T(8,128)(2,1)S(1)}, bf16[128,768]{1,0:T(8,128)(2,1)S(1)}, u32[]{:S(2)}, u32[]{:S(2)}) collective-permute-start(bf16[128,768]{1,0:T(8,128)(2,1)S(1)} %slice_bitcast_fusion), channel_id=1, source_target_pairs={{0,4},{1,5},{2,6},{3,7},{4,0},{5,1},{6,2},{7,3},{8,12},{9,13},{10,... | collective-permute-start | bytes 589832 | tf_op jit(solution)/shard_map/ppermute | solution.py:446
  50.4 5.8 %collective-permute-start.9 = (bf16[128,768]{1,0:T(8,128)(2,1)S(1)}, bf16[128,768]{1,0:T(8,128)(2,1)S(1)}, u32[]{:S(2)}, u32[]{:S(2)}) collective-permute-start(bf16[128,768]{1,0:T(8,128)(2,1)S(1)} %slice_bitcast_fusion.1), channel_id=1, source_target_pairs={{0,12},{1,13},{2,14},{3,15},{4,8},{5,9},{6,10},{7,11},{8,4},{9,5},... | collective-permute-start | bytes 589832 | tf_op jit(solution)/shard_map/ppermute | solution.py:446
  52.4 3.8 %copy-start.7 = (bf16[2,128,768]{2,1,0:T(8,128)(2,1)S(1)}, bf16[2,128,768]{2,1,0:T(8,128)(2,1)}, u32[]{:S(2)}) copy-start(bf16[2,128,768]{2,1,0:T(8,128)(2,1)} %get-tuple-element.62) | copy-start | bytes 1179652
  53.8 33.0 %collective-permute-start.12 = (bf16[2,4,128,768]{3,2,1,0:T(8,128)(2,1)}, bf16[2,4,128,768]{3,2,1,0:T(8,128)(2,1)}, u32[]{:S(2)}, u32[]{:S(2)}) collective-permute-start(bf16[2,4,128,768]{3,2,1,0:T(8,128)(2,1)} %pad_maximum_fusion.refs_5_.refs_1_), channel_id=1, source_target_pairs={{0,4},{1,5},{2,6},{3,7},{4,0},{5,1},{6,2},{7,3},{8,12},{9,13},{10,... | collective-permute-start | bytes 4718600 | tf_op jit(solution)/shard_map/ppermute | solution.py:446
  56.3 6.8 %copy-start.13 = (bf16[16,256]{1,0:T(8,128)(2,1)S(1)}, bf16[16,256]{1,0:T(8,128)(2,1)}, u32[]{:S(2)}) copy-start(bf16[16,256]{1,0:T(8,128)(2,1)} %param.13) | copy-start | bytes 24580
  57.7 32.8 %collective-permute-start.13 = (bf16[2,4,128,768]{3,2,1,0:T(8,128)(2,1)}, bf16[2,4,128,768]{3,2,1,0:T(8,128)(2,1)}, u32[]{:S(2)}, u32[]{:S(2)}) collective-permute-start(bf16[2,4,128,768]{3,2,1,0:T(8,128)(2,1)} %pad_maximum_fusion.1.refs_6_), channel_id=1, source_target_pairs={{0,1},{1,0},{2,3},{3,2},{4,5},{5,4},{6,7},{7,6},{8,9},{9,8},{10,11... | collective-permute-start | bytes 4718600 | tf_op jit(solution)/shard_map/ppermute | solution.py:446
  58.5 33.1 %collective-permute-start.14 = (bf16[2,4,128,768]{3,2,1,0:T(8,128)(2,1)}, bf16[2,4,128,768]{3,2,1,0:T(8,128)(2,1)}, u32[]{:S(2)}, u32[]{:S(2)}) collective-permute-start(bf16[2,4,128,768]{3,2,1,0:T(8,128)(2,1)} %pad_maximum_fusion.refs_5_.refs_1_), channel_id=1, source_target_pairs={{0,12},{1,13},{2,14},{3,15},{4,8},{5,9},{6,10},{7,11},{8,4},{9,5},... | collective-permute-start | bytes 4718600 | tf_op jit(solution)/shard_map/ppermute | solution.py:446
  60.4 33.1 %collective-permute-start.15 = (bf16[2,4,128,768]{3,2,1,0:T(8,128)(2,1)}, bf16[2,4,128,768]{3,2,1,0:T(8,128)(2,1)}, u32[]{:S(2)}, u32[]{:S(2)}) collective-permute-start(bf16[2,4,128,768]{3,2,1,0:T(8,128)(2,1)} %pad_maximum_fusion.1.refs_6_), channel_id=1, source_target_pairs={{0,3},{1,2},{2,1},{3,0},{4,7},{5,6},{6,5},{7,4},{8,11},{9,10},{10,... | collective-permute-start | bytes 4718600 | tf_op jit(solution)/shard_map/ppermute | solution.py:446
  74.0 24.9 %collective-permute-start.20 = (bf16[2,128,768]{2,1,0:T(8,128)(2,1)}, bf16[2,128,768]{2,1,0:T(8,128)(2,1)S(1)}, u32[]{:S(2)}, u32[]{:S(2)}) collective-permute-start(bf16[2,128,768]{2,1,0:T(8,128)(2,1)} %get-tuple-element.68), channel_id=1, source_target_pairs={{0,1},{1,0},{2,3},{3,2},{4,5},{5,4},{6,7},{7,6},{8,9},{9,8},{10,11... | collective-permute-start | bytes 1179656 | tf_op jit(solution)/shard_map/ppermute | solution.py:446
  86.8 15.1 %collective-permute-start.23 = (bf16[2,128,768]{2,1,0:T(8,128)(2,1)}, bf16[2,128,768]{2,1,0:T(8,128)(2,1)S(1)}, u32[]{:S(2)}, u32[]{:S(2)}) collective-permute-start(bf16[2,128,768]{2,1,0:T(8,128)(2,1)} %get-tuple-element.75), channel_id=1, source_target_pairs={{0,3},{1,2},{2,1},{3,0},{4,7},{5,6},{6,5},{7,4},{8,11},{9,10},{10,... | collective-permute-start | bytes 1179656 | tf_op jit(solution)/shard_map/ppermute | solution.py:446
  96.3 23.0 %collective-permute-start.16 = (bf16[4,128,768]{2,1,0:T(8,128)(2,1)}, bf16[4,128,768]{2,1,0:T(8,128)(2,1)}, u32[]{:S(2)}, u32[]{:S(2)}) collective-permute-start(bf16[4,128,768]{2,1,0:T(8,128)(2,1)} %get-tuple-element.63), channel_id=1, source_target_pairs={{0,12},{1,13},{2,14},{3,15},{4,8},{5,9},{6,10},{7,11},{8,4},{9,5},... | collective-permute-start | bytes 2359304 | tf_op jit(solution)/shard_map/ppermute | solution.py:446
  96.9 23.9 %collective-permute-start.17 = (bf16[4,128,768]{2,1,0:T(8,128)(2,1)}, bf16[4,128,768]{2,1,0:T(8,128)(2,1)}, u32[]{:S(2)}, u32[]{:S(2)}) collective-permute-start(bf16[4,128,768]{2,1,0:T(8,128)(2,1)} %get-tuple-element.64), channel_id=1, source_target_pairs={{0,4},{1,5},{2,6},{3,7},{4,0},{5,1},{6,2},{7,3},{8,12},{9,13},{10,... | collective-permute-start | bytes 2359304 | tf_op jit(solution)/shard_map/ppermute | solution.py:446
  96.9 21.3 %collective-permute-start.26 = (bf16[2,128,768]{2,1,0:T(8,128)(2,1)}, bf16[2,128,768]{2,1,0:T(8,128)(2,1)}, u32[]{:S(2)}, u32[]{:S(2)}) collective-permute-start(bf16[2,128,768]{2,1,0:T(8,128)(2,1)} %get-tuple-element.81), channel_id=1, source_target_pairs={{0,4},{1,5},{2,6},{3,7},{4,0},{5,1},{6,2},{7,3},{8,12},{9,13},{10,... | collective-permute-start | bytes 1179656 | tf_op jit(solution)/shard_map/ppermute | solution.py:446
  98.9 19.3 %copy-start.2 = (bf16[2,128,768]{2,1,0:T(8,128)(2,1)}, bf16[2,128,768]{2,1,0:T(8,128)(2,1)S(1)}, u32[]{:S(2)}) copy-start(bf16[2,128,768]{2,1,0:T(8,128)(2,1)S(1)} %collective-permute-done.20.refs_1_.refs_2_) | copy-start | bytes 1179652
  98.9 21.9 %collective-permute-start.18 = (bf16[4,128,768]{2,1,0:T(8,128)(2,1)}, bf16[4,128,768]{2,1,0:T(8,128)(2,1)}, u32[]{:S(2)}, u32[]{:S(2)}) collective-permute-start(bf16[4,128,768]{2,1,0:T(8,128)(2,1)} %get-tuple-element.65), channel_id=1, source_target_pairs={{0,3},{1,2},{2,1},{3,0},{4,7},{5,6},{6,5},{7,4},{8,11},{9,10},{10,... | collective-permute-start | bytes 2359304 | tf_op jit(solution)/shard_map/ppermute | solution.py:446
  101.9 16.2 %copy-start.3 = (bf16[2,128,768]{2,1,0:T(8,128)(2,1)}, bf16[2,128,768]{2,1,0:T(8,128)(2,1)S(1)}, u32[]{:S(2)}) copy-start(bf16[2,128,768]{2,1,0:T(8,128)(2,1)S(1)} %collective-permute-done.23.refs_9_.refs_7_) | copy-start | bytes 1179652
  101.9 20.3 %collective-permute-start.19 = (bf16[4,128,768]{2,1,0:T(8,128)(2,1)}, bf16[4,128,768]{2,1,0:T(8,128)(2,1)}, u32[]{:S(2)}, u32[]{:S(2)}) collective-permute-start(bf16[4,128,768]{2,1,0:T(8,128)(2,1)} %get-tuple-element.66), channel_id=1, source_target_pairs={{0,1},{1,0},{2,3},{3,2},{4,5},{5,4},{6,7},{7,6},{8,9},{9,8},{10,11... | collective-permute-start | bytes 2359304 | tf_op jit(solution)/shard_map/ppermute | solution.py:446
  118.2 15.0 %collective-permute-start.21 = (bf16[4,128,768]{2,1,0:T(8,128)(2,1)}, bf16[4,128,768]{2,1,0:T(8,128)(2,1)S(1)}, u32[]{:S(2)}, u32[]{:S(2)}) collective-permute-start(bf16[4,128,768]{2,1,0:T(8,128)(2,1)} %get-tuple-element.71), channel_id=1, source_target_pairs={{0,1},{1,0},{2,3},{3,2},{4,5},{5,4},{6,7},{7,6},{8,9},{9,8},{10,11... | collective-permute-start | bytes 2359304 | tf_op jit(solution)/shard_map/ppermute | solution.py:446
  119.3 15.1 %collective-permute-start.24 = (bf16[4,128,768]{2,1,0:T(8,128)(2,1)}, bf16[4,128,768]{2,1,0:T(8,128)(2,1)}, u32[]{:S(2)}, u32[]{:S(2)}) collective-permute-start(bf16[4,128,768]{2,1,0:T(8,128)(2,1)} %get-tuple-element.77), channel_id=1, source_target_pairs={{0,3},{1,2},{2,1},{3,0},{4,7},{5,6},{6,5},{7,4},{8,11},{9,10},{10,... | collective-permute-start | bytes 2359304 | tf_op jit(solution)/shard_map/ppermute | solution.py:446
  120.8 13.8 %collective-permute-start.27 = (bf16[4,128,768]{2,1,0:T(8,128)(2,1)}, bf16[4,128,768]{2,1,0:T(8,128)(2,1)}, u32[]{:S(2)}, u32[]{:S(2)}) collective-permute-start(bf16[4,128,768]{2,1,0:T(8,128)(2,1)} %get-tuple-element.83), channel_id=1, source_target_pairs={{0,4},{1,5},{2,6},{3,7},{4,0},{5,1},{6,2},{7,3},{8,12},{9,13},{10,... | collective-permute-start | bytes 2359304 | tf_op jit(solution)/shard_map/ppermute | solution.py:446
  120.8 12.2 %collective-permute-start.29 = (bf16[2,128,768]{2,1,0:T(8,128)(2,1)}, bf16[2,128,768]{2,1,0:T(8,128)(2,1)}, u32[]{:S(2)}, u32[]{:S(2)}) collective-permute-start(bf16[2,128,768]{2,1,0:T(8,128)(2,1)} %get-tuple-element.87), channel_id=1, source_target_pairs={{0,12},{1,13},{2,14},{3,15},{4,8},{5,9},{6,10},{7,11},{8,4},{9,5},... | collective-permute-start | bytes 1179656 | tf_op jit(solution)/shard_map/ppermute | solution.py:446
  122.2 17.7 %collective-permute-start.30 = (bf16[4,128,768]{2,1,0:T(8,128)(2,1)}, bf16[4,128,768]{2,1,0:T(8,128)(2,1)}, u32[]{:S(2)}, u32[]{:S(2)}) collective-permute-start(bf16[4,128,768]{2,1,0:T(8,128)(2,1)} %get-tuple-element.89), channel_id=1, source_target_pairs={{0,12},{1,13},{2,14},{3,15},{4,8},{5,9},{6,10},{7,11},{8,4},{9,5},... | collective-permute-start | bytes 2359304 | tf_op jit(solution)/shard_map/ppermute | solution.py:446
  133.0 11.4 %collective-permute-start.22 = (bf16[2,128,768]{2,1,0:T(8,128)(2,1)}, bf16[2,128,768]{2,1,0:T(8,128)(2,1)}, u32[]{:S(2)}, u32[]{:S(2)}) collective-permute-start(bf16[2,128,768]{2,1,0:T(8,128)(2,1)} %get-tuple-element.73), channel_id=1, source_target_pairs={{0,1},{1,0},{2,3},{3,2},{4,5},{5,4},{6,7},{7,6},{8,9},{9,8},{10,11... | collective-permute-start | bytes 1179656 | tf_op jit(solution)/shard_map/ppermute | solution.py:446
  133.1 15.2 %copy-start.1 = (bf16[4,128,768]{2,1,0:T(8,128)(2,1)}, bf16[4,128,768]{2,1,0:T(8,128)(2,1)S(1)}, u32[]{:S(2)}) copy-start(bf16[4,128,768]{2,1,0:T(8,128)(2,1)S(1)} %collective-permute-done.21.refs_3_.refs_5_.refs_1_) | copy-start | bytes 2359300
  133.1 12.8 %collective-permute-start.25 = (bf16[2,128,768]{2,1,0:T(8,128)(2,1)}, bf16[2,128,768]{2,1,0:T(8,128)(2,1)}, u32[]{:S(2)}, u32[]{:S(2)}) collective-permute-start(bf16[2,128,768]{2,1,0:T(8,128)(2,1)} %get-tuple-element.79), channel_id=1, source_target_pairs={{0,3},{1,2},{2,1},{3,0},{4,7},{5,6},{6,5},{7,4},{8,11},{9,10},{10,... | collective-permute-start | bytes 1179656 | tf_op jit(solution)/shard_map/ppermute | solution.py:446
  134.4 11.5 %collective-permute-start.28 = (bf16[2,128,768]{2,1,0:T(8,128)(2,1)}, bf16[2,128,768]{2,1,0:T(8,128)(2,1)}, u32[]{:S(2)}, u32[]{:S(2)}) collective-permute-start(bf16[2,128,768]{2,1,0:T(8,128)(2,1)} %get-tuple-element.85), channel_id=1, source_target_pairs={{0,4},{1,5},{2,6},{3,7},{4,0},{5,1},{6,2},{7,3},{8,12},{9,13},{10,... | collective-permute-start | bytes 1179656 | tf_op jit(solution)/shard_map/ppermute | solution.py:446
  134.6 13.7 %collective-permute-start.31 = (bf16[2,128,768]{2,1,0:T(8,128)(2,1)}, bf16[2,128,768]{2,1,0:T(8,128)(2,1)}, u32[]{:S(2)}, u32[]{:S(2)}) collective-permute-start(bf16[2,128,768]{2,1,0:T(8,128)(2,1)} %get-tuple-element.91), channel_id=1, source_target_pairs={{0,12},{1,13},{2,14},{3,15},{4,8},{5,9},{6,10},{7,11},{8,4},{9,5},... | collective-permute-start | bytes 1179656 | tf_op jit(solution)/shard_map/ppermute | solution.py:446
  152.8 13.5 %collective-permute-start.32 = (bf16[4,128,768]{2,1,0:T(8,128)(2,1)}, bf16[4,128,768]{2,1,0:T(8,128)(2,1)S(1)}, u32[]{:S(2)}, u32[]{:S(2)}) collective-permute-start(bf16[4,128,768]{2,1,0:T(8,128)(2,1)} %get-tuple-element.92), channel_id=1, source_target_pairs={{0,3},{1,2},{2,1},{3,0},{4,7},{5,6},{6,5},{7,4},{8,11},{9,10},{10,... | collective-permute-start | bytes 2359304 | tf_op jit(solution)/shard_map/ppermute | solution.py:446
  153.3 13.0 %collective-permute-start.33 = (bf16[4,128,768]{2,1,0:T(8,128)(2,1)}, bf16[4,128,768]{2,1,0:T(8,128)(2,1)}, u32[]{:S(2)}, u32[]{:S(2)}) collective-permute-start(bf16[4,128,768]{2,1,0:T(8,128)(2,1)} %get-tuple-element.94), channel_id=1, source_target_pairs={{0,1},{1,0},{2,3},{3,2},{4,5},{5,4},{6,7},{7,6},{8,9},{9,8},{10,11... | collective-permute-start | bytes 2359304 | tf_op jit(solution)/shard_map/ppermute | solution.py:446
  153.5 13.5 %collective-permute-start.34 = (bf16[4,128,768]{2,1,0:T(8,128)(2,1)}, bf16[4,128,768]{2,1,0:T(8,128)(2,1)}, u32[]{:S(2)}, u32[]{:S(2)}) collective-permute-start(bf16[4,128,768]{2,1,0:T(8,128)(2,1)} %get-tuple-element.96), channel_id=1, source_target_pairs={{0,12},{1,13},{2,14},{3,15},{4,8},{5,9},{6,10},{7,11},{8,4},{9,5},... | collective-permute-start | bytes 2359304 | tf_op jit(solution)/shard_map/ppermute | solution.py:446
  154.8 12.2 %collective-permute-start.35 = (bf16[4,128,768]{2,1,0:T(8,128)(2,1)}, bf16[4,128,768]{2,1,0:T(8,128)(2,1)}, u32[]{:S(2)}, u32[]{:S(2)}) collective-permute-start(bf16[4,128,768]{2,1,0:T(8,128)(2,1)} %get-tuple-element.98), channel_id=1, source_target_pairs={{0,4},{1,5},{2,6},{3,7},{4,0},{5,1},{6,2},{7,3},{8,12},{9,13},{10,... | collective-permute-start | bytes 2359304 | tf_op jit(solution)/shard_map/ppermute | solution.py:446
  166.3 0.9 copy-start
  170.8 11.6 %collective-permute-start.36 = (bf16[2,128,768]{2,1,0:T(8,128)(2,1)}, bf16[2,128,768]{2,1,0:T(8,128)(2,1)S(1)}, u32[]{:S(2)}, u32[]{:S(2)}) collective-permute-start(bf16[2,128,768]{2,1,0:T(8,128)(2,1)} %get-tuple-element.99), channel_id=1, source_target_pairs={{0,4},{1,5},{2,6},{3,7},{4,0},{5,1},{6,2},{7,3},{8,12},{9,13},{10,... | collective-permute-start | bytes 1179656 | tf_op jit(solution)/shard_map/ppermute | solution.py:446
  172.4 10.1 %collective-permute-start.37 = (bf16[2,128,768]{2,1,0:T(8,128)(2,1)}, bf16[2,128,768]{2,1,0:T(8,128)(2,1)S(1)}, u32[]{:S(2)}, u32[]{:S(2)}) collective-permute-start(bf16[2,128,768]{2,1,0:T(8,128)(2,1)} %get-tuple-element.100), channel_id=1, source_target_pairs={{0,12},{1,13},{2,14},{3,15},{4,8},{5,9},{6,10},{7,11},{8,4},{9,5},... | collective-permute-start | bytes 1179656 | tf_op jit(solution)/shard_map/ppermute | solution.py:446
  173.6 8.8 %collective-permute-start.38 = (bf16[2,128,768]{2,1,0:T(8,128)(2,1)}, bf16[2,128,768]{2,1,0:T(8,128)(2,1)}, u32[]{:S(2)}, u32[]{:S(2)}) collective-permute-start(bf16[2,128,768]{2,1,0:T(8,128)(2,1)} %get-tuple-element.101), channel_id=1, source_target_pairs={{0,1},{1,0},{2,3},{3,2},{4,5},{5,4},{6,7},{7,6},{8,9},{9,8},{10,11... | collective-permute-start | bytes 1179656 | tf_op jit(solution)/shard_map/ppermute | solution.py:446
  175.1 8.2 %collective-permute-start.39 = (bf16[2,128,768]{2,1,0:T(8,128)(2,1)}, bf16[2,128,768]{2,1,0:T(8,128)(2,1)}, u32[]{:S(2)}, u32[]{:S(2)}) collective-permute-start(bf16[2,128,768]{2,1,0:T(8,128)(2,1)} %get-tuple-element.102), channel_id=1, source_target_pairs={{0,3},{1,2},{2,1},{3,0},{4,7},{5,6},{6,5},{7,4},{8,11},{9,10},{10,... | collective-permute-start | bytes 1179656 | tf_op jit(solution)/shard_map/ppermute | solution.py:446
  182.4 0.8 copy-start.4
  182.4 0.9 copy-start.5
  186.2 6.0 %collective-permute-start.40 = (bf16[1,128,768]{2,1,0:T(8,128)(2,1)}, bf16[1,128,768]{2,1,0:T(8,128)(2,1)S(1)}, u32[]{:S(2)}, u32[]{:S(2)}) collective-permute-start(bf16[1,128,768]{2,1,0:T(8,128)(2,1)} %get-tuple-element.103), channel_id=1, source_target_pairs={{0,12},{1,13},{2,14},{3,15},{4,8},{5,9},{6,10},{7,11},{8,4},{9,5},... | collective-permute-start | bytes 589832 | tf_op jit(solution)/shard_map/ppermute | solution.py:446
  187.9 7.0 %collective-permute-start.41 = (bf16[1,128,768]{2,1,0:T(8,128)(2,1)}, bf16[1,128,768]{2,1,0:T(8,128)(2,1)S(1)}, u32[]{:S(2)}, u32[]{:S(2)}) collective-permute-start(bf16[1,128,768]{2,1,0:T(8,128)(2,1)} %get-tuple-element.104), channel_id=1, source_target_pairs={{0,4},{1,5},{2,6},{3,7},{4,0},{5,1},{6,2},{7,3},{8,12},{9,13},{10,... | collective-permute-start | bytes 589832 | tf_op jit(solution)/shard_map/ppermute | solution.py:446
  188.4 6.5 %collective-permute-start.42 = (bf16[1,128,768]{2,1,0:T(8,128)(2,1)}, bf16[1,128,768]{2,1,0:T(8,128)(2,1)S(1)}, u32[]{:S(2)}, u32[]{:S(2)}) collective-permute-start(bf16[1,128,768]{2,1,0:T(8,128)(2,1)} %get-tuple-element.105), channel_id=1, source_target_pairs={{0,3},{1,2},{2,1},{3,0},{4,7},{5,6},{6,5},{7,4},{8,11},{9,10},{10,... | collective-permute-start | bytes 589832 | tf_op jit(solution)/shard_map/ppermute | solution.py:446
  190.6 7.2 %collective-permute-start.43 = (bf16[1,128,768]{2,1,0:T(8,128)(2,1)}, bf16[1,128,768]{2,1,0:T(8,128)(2,1)S(1)}, u32[]{:S(2)}, u32[]{:S(2)}) collective-permute-start(bf16[1,128,768]{2,1,0:T(8,128)(2,1)} %get-tuple-element.106), channel_id=1, source_target_pairs={{0,1},{1,0},{2,3},{3,2},{4,5},{5,4},{6,7},{7,6},{8,9},{9,8},{10,11... | collective-permute-start | bytes 589832 | tf_op jit(solution)/shard_map/ppermute | solution.py:446
  192.2 5.6 %copy-start.9 = (bf16[1,128,768]{2,1,0:T(8,128)(2,1)}, bf16[1,128,768]{2,1,0:T(8,128)(2,1)S(1)}, u32[]{:S(2)}) copy-start(bf16[1,128,768]{2,1,0:T(8,128)(2,1)S(1)} %collective-permute-done.40.refs_5_) | copy-start | bytes 589828
  194.9 2.9 %copy-start.10 = (bf16[1,128,768]{2,1,0:T(8,128)(2,1)}, bf16[1,128,768]{2,1,0:T(8,128)(2,1)S(1)}, u32[]{:S(2)}) copy-start(bf16[1,128,768]{2,1,0:T(8,128)(2,1)S(1)} %collective-permute-done.41.refs_10_) | copy-start | bytes 589828
  194.9 2.9 %copy-start.11 = (bf16[1,128,768]{2,1,0:T(8,128)(2,1)}, bf16[1,128,768]{2,1,0:T(8,128)(2,1)S(1)}, u32[]{:S(2)}) copy-start(bf16[1,128,768]{2,1,0:T(8,128)(2,1)S(1)} %collective-permute-done.42.refs_15_) | copy-start | bytes 589828
  197.8 0.7 copy-start.12
  202.9 37.1 %all-to-all-start.1 = ((bf16[8,96,768]{2,1,0:T(8,128)(2,1)}), bf16[8,96,768]{2,1,0:T(8,128)(2,1)}, u32[]{:S(2)}, u32[]{:S(2)}) async-start(bf16[8,96,768]{2,1,0:T(8,128)(2,1)} %leave_rows.1), calls=%async_computation.1 | async-start | bytes 2359296 | tf_op jit(solution)/shard_map/all_to_all | solution.py:581

commit v6 on v4

--- a/solution.py
+++ b/solution.py
@@ -314,7 +314,15 @@
         send(u - 1)
         return carry
 
-    lax.fori_loop(1, total, step, 0)
+    if total <= 6:
+        for u in range(1, total):
+            ready(u)
+            partial(u - 1)
+            signals(u)
+            for copy in store(u - 1):
+                copy.start()
+    else:
+        lax.fori_loop(1, total, step, 0)
     partial(total - 1)
     for copy in store(total - 1):
         copy.start()

time: 244 us -> 243 us (level)
  Pallas kernels: 89.5 us -> 92.9 us
  starting transfers between devices: 83.8 us -> 80.7 us
    pallas_call x4, Pallas kernels: 45.6 us -> 48.6 us  [work(): pl.pallas_call(functools.partial(work_body, units, len(arrays), len(out_b...]
  transfers between devices with their start and end apart: 46 -> 46, of which waited for: 25 -> 25; matrix products, arithmetic and copies ran while one was open for 3% -> 3% of each run, Pallas kernels for 26% -> 28%
where the time goes in v6:
time: 243 us
  Pallas kernels  92.9 us (38%)
  starting transfers between devices  80.7 us (33%)
  waiting for transfers between devices  58.7 us (24%)
  other arithmetic  4.64 us (2%)
  local copies, waits for them, and re-layouts  4.57 us (2%)
    ppermute x44, waiting for transfers between devices, swap(): return lax.ppermute(array, 'label', [(i, i ^ mask) for i in range(owners)])  56.2 us
    ppermute x44, starting transfers between devices, swap(): return lax.ppermute(array, 'label', [(i, i ^ mask) for i in range(owners)])  53.9 us
    pallas_call x4, Pallas kernels, work(): pl.pallas_call(functools.partial(work_body, units, len(arrays), len(out_b...  48.6 us
    all_to_all x1, starting transfers between devices, shards(): lax.all_to_all(leaving, 'dp', split_axis=0, concat_axis=0, tiled=True)  21 us
    pallas_call x1, Pallas kernels, panel_sum(): pl.pallas_call(functools.partial(panel_body, parts, len(arrays), len(sign...  15.9 us
    pallas_call x3, Pallas kernels, merge(): pl.pallas_call(functools.partial(merge_body, [[[0] * len(t) for t in b] f...  10.9 us
    all_to_all x1, starting transfers between devices, shards(): lax.all_to_all(outgoing, 'dp', split_axis=0, concat_axis=0, tiled=True)  5.81 us
  transfers between devices with their start and end apart: 46, of which 25 were waited for; matrix products, arithmetic and copies ran while one was open for 3% of the time, Pallas kernels for 28%

profile of v6, /device:TPU:1, one launch (start us, length us, event | category | flops | bytes accessed | tf_op | source)
XLA Modules:
  0.0 242.5 jit_solution(15080773104089087006)
XLA Ops:
  2.0 3.7 %pack_rows.1 = (bf16[8,112,768]{2,1,0:T(8,128)(2,1)}, s32[1,512]{1,0:T(1,128)}) custom-call(bf16[512,768]{1,0:T(8,128)(2,1)} %x_ref.1, s32[1,512]{1,0:T(1,128)} %bitcast.76), custom_call_target="tpu_custom_call" | custom-call | tf_op jit(solution)/shard_map/pack_rows/pallas_call | solution.py:56
  5.7 5.8 %all-to-all-start = ((bf16[8,112,768]{2,1,0:T(8,128)(2,1)}), bf16[8,112,768]{2,1,0:T(8,128)(2,1)}, u32[]{:S(2)}, u32[]{:S(2)}) async-start(bf16[8,112,768]{2,1,0:T(8,128)(2,1)} %get-tuple-element.58), calls=%async_computation | async-start | bytes 2752512 | tf_op jit(solution)/shard_map/all_to_all | solution.py:468
  11.5 1.6 collective-permute-start
  13.2 1.1 collective-permute-done
  14.3 3.6 %collective-permute-start.1 = (bf16[2,2,16,256]{3,2,1,0:T(8,128)(2,1)S(1)}, bf16[2,2,16,256]{3,2,1,0:T(8,128)(2,1)S(1)}, u32[]{:S(2)}, u32[]{:S(2)}) collective-permute-start(bf16[2,2,16,256]{3,2,1,0:T(8,128)(2,1)S(1)} %pad_maximum_fusion.4), channel_id=1, source_target_pairs={{0,3},{1,2},{2,1},{3,0},{4,7},{5,6},{6,5},{7,4},{8,11},{9,10},{10,... | collective-permute-start | bytes 98312 | tf_op jit(solution)/shard_map/ppermute | solution.py:447
  17.9 1.3 collective-permute-done.1
  19.2 1.4 collective-permute-start.2
  20.6 2.2 collective-permute-done.2
  22.8 2.8 %collective-permute-start.3 = (bf16[8,2,16,256]{3,2,1,0:T(8,128)(2,1)S(1)}, bf16[8,2,16,256]{3,2,1,0:T(8,128)(2,1)S(1)}, u32[]{:S(2)}, u32[]{:S(2)}) collective-permute-start(bf16[8,2,16,256]{3,2,1,0:T(8,128)(2,1)S(1)} %pad_maximum_fusion.2), channel_id=1, source_target_pairs={{0,12},{1,13},{2,14},{3,15},{4,8},{5,9},{6,10},{7,11},{8,4},{9,5},... | collective-permute-start | bytes 393224 | tf_op jit(solution)/shard_map/ppermute | solution.py:447
  25.6 2.7 %collective-permute-done.3 = bf16[8,2,16,256]{3,2,1,0:T(8,128)(2,1)S(1)} collective-permute-done((bf16[8,2,16,256]{3,2,1,0:T(8,128)(2,1)S(1)}, bf16[8,2,16,256]{3,2,1,0:T(8,128)(2,1)S(1)}, u32[]{:S(2)}, u32[]{:S(2)}) %collective-permute-start.3) | collective-permute-done | bytes 131104 | tf_op jit(solution)/shard_map/ppermute | solution.py:447
  28.4 1.8 all-to-all-done.arrived_ref
  30.2 3.6 %land_rows.1 = (bf16[768,512]{1,0:T(8,128)(2,1)}, bf16[2,128,768]{2,1,0:T(8,128)(2,1)}, bf16[2,128,768]{2,1,0:T(8,128)(2,1)}) custom-call(bf16[8,112,768]{2,1,0:T(8,128)(2,1)} %all-to-all-done.arrived_ref, bf16[16,2,16,256]{3,2,1,0:T(8,128)(2,1)} %copy-done.6), custom_call_target="tpu_custom_call" | custom-call | tf_op jit(solution)/shard_map/land_rows/pallas_call | solution.py:85
  33.8 3.8 %collective-permute-start.6 = (bf16[2,128,768]{2,1,0:T(8,128)(2,1)}, bf16[2,128,768]{2,1,0:T(8,128)(2,1)S(1)}, u32[]{:S(2)}, u32[]{:S(2)}) collective-permute-start(bf16[2,128,768]{2,1,0:T(8,128)(2,1)} %get-tuple-element.61), channel_id=1, source_target_pairs={{0,3},{1,2},{2,1},{3,0},{4,7},{5,6},{6,5},{7,4},{8,11},{9,10},{10,... | collective-permute-start | bytes 1179656 | tf_op jit(solution)/shard_map/ppermute | solution.py:447
  37.6 2.7 %collective-permute-start.10 = (bf16[2,128,768]{2,1,0:T(8,128)(2,1)}, bf16[2,128,768]{2,1,0:T(8,128)(2,1)S(1)}, u32[]{:S(2)}, u32[]{:S(2)}) collective-permute-start(bf16[2,128,768]{2,1,0:T(8,128)(2,1)} %get-tuple-element.62), channel_id=1, source_target_pairs={{0,12},{1,13},{2,14},{3,15},{4,8},{5,9},{6,10},{7,11},{8,4},{9,5},... | collective-permute-start | bytes 1179656 | tf_op jit(solution)/shard_map/ppermute | solution.py:447
  40.3 5.4 %collective-permute-done.6 = bf16[2,128,768]{2,1,0:T(8,128)(2,1)S(1)} collective-permute-done((bf16[2,128,768]{2,1,0:T(8,128)(2,1)}, bf16[2,128,768]{2,1,0:T(8,128)(2,1)S(1)}, u32[]{:S(2)}, u32[]{:S(2)}) %collective-permute-start.6) | collective-permute-done | bytes 393248 | tf_op jit(solution)/shard_map/ppermute | solution.py:447
  46.6 1.7 collective-permute-start.5
  48.3 2.1 collective-permute-start.11
  50.4 2.0 collective-permute-start.9
  52.4 1.3 pad_maximum_fusion.refs_5_.refs_1_
  53.8 2.0 collective-permute-start.12
  56.3 1.4 pad_maximum_fusion.1.refs_6_
  58.5 1.9 collective-permute-start.14
  60.4 0.9 collective-permute-start.15
  63.1 1.6 broadcast_in_dim.37.refs_4_
  64.7 10.7 %work_near.1 = (bf16[1,128,768]{2,1,0:T(8,128)(2,1)}, bf16[2,128,768]{2,1,0:T(8,128)(2,1)}, bf16[1,128,768]{2,1,0:T(8,128)(2,1)}, bf16[2,128,768]{2,1,0:T(8,128)...) custom-call(s32[16,4]{1,0:T(8,128)} %copy.29.refs_0_, ...), custom_call_target="tpu_custom_call" | custom-call | flops 3623878656 | bytes 11796480 | tf_op jit(solution)/shard_map/work_near/pallas_call | solution.py:342
  75.8 11.0 %collective-permute-done.12.refs_0_.refs_7_.refs_5_.refs_2_ = bf16[2,4,128,768]{3,2,1,0:T(8,128)(2,1)} collective-permute-done((bf16[2,4,128,768]{3,2,1,0:T(8,128)(2,1)}, bf16[2,4,128,768]{3,2,1,0:T(8,128)(2,1)}, u32[]{:S(2)}, u32[]{:S(2)}) %collective-permute-start.12) | collective-permute-done | bytes 1572896 | tf_op jit(solution)/shard_map/ppermute | solution.py:447
  86.8 2.3 collective-permute-start.23
  89.1 1.4 collective-permute-done.13.refs_2_.refs_8_.refs_6_.refs_7_
  90.4 1.1 collective-permute-done.14.refs_1_.refs_9_.refs_7_.refs_3_
  91.6 1.9 collective-permute-done.15.refs_3_.refs_10_.refs_8_
  93.5 2.8 %cut_halves.1 = (bf16[4,128,768]{2,1,0:T(8,128)(2,1)}, bf16[4,128,768]{2,1,0:T(8,128)(2,1)}, bf16[4,128,768]{2,1,0:T(8,128)(2,1)}, bf16[4,128,768]{2,1,0:T(8,128)(2,1)}) custom-call(bf16[2,4,128,768]{3,2,1,0:T(8,128)(2,1)} %collective-permute-done.12.refs_0_.refs_7_.refs_5_.refs_2_, ...), custom_call_target="tpu_custom_call" | custom-call | tf_op jit(solution)/shard_map/cut_halves/pallas_call | solution.py:192
  96.9 1.5 collective-permute-start.26
  98.9 1.2 collective-permute-start.18
  100.1 1.8 collective-permute-done.23.refs_9_.refs_7_
  102.2 15.8 %work_far.1 = (bf16[2,128,768]{2,1,0:T(8,128)(2,1)}, bf16[4,128,768]{2,1,0:T(8,128)(2,1)}, bf16[2,128,768]{2,1,0:T(8,128)(2,1)}, bf16[4,128,768]{2,1,0:T(8,128)(...) custom-call(s32[16,4]{1,0:T(8,128)} %copy.29.refs_0_, ...), custom_call_target="tpu_custom_call" | custom-call | flops 7247757312 | bytes 17301504 | tf_op jit(solution)/shard_map/work_far/pallas_call | solution.py:342
  118.0 1.2 collective-permute-start.21
  119.2 1.1 collective-permute-start.24
  120.5 2.3 collective-permute-start.29
  123.1 10.3 %work_last.1 = (bf16[1,128,768]{2,1,0:T(8,128)(2,1)}, bf16[2,128,768]{2,1,0:T(8,128)(2,1)}, bf16[1,128,768]{2,1,0:T(8,128)(2,1)}, bf16[2,128,768]{2,1,0:T(8,128)...) custom-call(s32[16,4]{1,0:T(8,128)} %copy.29.refs_0_, ...), custom_call_target="tpu_custom_call" | custom-call | flops 3623878656 | bytes 11796480 | tf_op jit(solution)/shard_map/work_last/pallas_call | solution.py:342
  133.6 1.6 collective-permute-start.25
  135.6 0.9 collective-permute-start.31
  136.5 2.4 %collective-permute-done.30.refs_27_.refs_29_.refs_19_.refs_13_ = bf16[4,128,768]{2,1,0:T(8,128)(2,1)} collective-permute-done((bf16[4,128,768]{2,1,0:T(8,128)(2,1)}, bf16[4,128,768]{2,1,0:T(8,128)(2,1)}, u32[]{:S(2)}, u32[]{:S(2)}) %collective-permute-start.30) | collective-permute-done | bytes 786464 | tf_op jit(solution)/shard_map/ppermute | solution.py:447
  139.0 5.7 %collective-permute-done.22.refs_7_.refs_4_ = bf16[2,128,768]{2,1,0:T(8,128)(2,1)} collective-permute-done((bf16[2,128,768]{2,1,0:T(8,128)(2,1)}, bf16[2,128,768]{2,1,0:T(8,128)(2,1)}, u32[]{:S(2)}, u32[]{:S(2)}) %collective-permute-start.22) | collective-permute-done | bytes 393248 | tf_op jit(solution)/shard_map/ppermute | solution.py:447
  144.7 1.7 collective-permute-done.25.refs_15_.refs_10_
  146.7 1.7 collective-permute-done.31.refs_31_.refs_22_
  148.4 4.4 %merge_1.1 = (bf16[4,128,768]{2,1,0:T(8,128)(2,1)}, bf16[4,128,768]{2,1,0:T(8,128)(2,1)}, bf16[4,128,768]{2,1,0:T(8,128)(2,1)}, bf16[4,128,768]{2,1,0:T(8,128)(2,1)}) custom-call(bf16[1,128,768]{2,1,0:T(8,128)(2,1)} %get-tuple-element.69.refs_0_, bf16[2,128,768]{2,1,0:T(8,128)(2,1)} %copy-done.2, bf16[2,128,768]{2,1,0:T(8,128)(2,1)} %get-tuple-element.70.refs_2_.refs_4_, ...), custom_call_target="tpu_custom_call" | custom-call | bytes 9437184 | tf_op jit(solution)/shard_map/merge_1/pallas_call | solution.py:145
  152.8 1.1 collective-permute-start.32
  154.0 2.2 collective-permute-start.34
  156.3 11.8 %work_kept.1 = (bf16[4,128,768]{2,1,0:T(8,128)(2,1)}, bf16[4,128,768]{2,1,0:T(8,128)(2,1)}, bf16[4,128,768]{2,1,0:T(8,128)(2,1)}, bf16[4,128,768]{2,1,0:T(8,128)(2,1)}, bf16[8,2,256,256]{3,2,1,0:T(8,128)(2,1)}) custom-call(s32[16,4]{1,0:T(8,128)} %copy.29.refs_0_, s32[2,8]{1,0:T(2,128)} %constant.77.clone.refs_1_, bf16[16,2,16,256]{3,2,1,0:T(8,128)(2,1)} %copy-done.6, ...), custom_call_target="tpu_custom_call" | custom-call | flops 4831838208 | bytes 13631488 | tf_op jit(solution)/shard_map/work_kept/pallas_call | solution.py:342
  169.0 3.6 %merge_2.1 = (bf16[2,128,768]{2,1,0:T(8,128)(2,1)}, bf16[2,128,768]{2,1,0:T(8,128)(2,1)}, bf16[2,128,768]{2,1,0:T(8,128)(2,1)}, bf16[2,128,768]{2,1,0:T(8,128)(2,1)}) custom-call(bf16[4,128,768]{2,1,0:T(8,128)(2,1)} %get-tuple-element.67.refs_0_.refs_3_.refs_1_, bf16[4,128,768]{2,1,0:T(8,128)(2,1)} %copy-done.1, bf16[4,128,768]{2,1,0:T(8,128)(2,1)} %copy-done, ...), custom_call_target="tpu_custom_call" | custom-call | bytes 6291456 | tf_op jit(solution)/shard_map/merge_2/pallas_call | solution.py:145
  172.6 1.1 collective-permute-start.36
  174.3 1.3 collective-permute-start.38
  175.6 1.7 collective-permute-start.39
  177.3 5.3 %collective-permute-done.36.refs_3_.refs_4_ = bf16[2,128,768]{2,1,0:T(8,128)(2,1)S(1)} collective-permute-done((bf16[2,128,768]{2,1,0:T(8,128)(2,1)}, bf16[2,128,768]{2,1,0:T(8,128)(2,1)S(1)}, u32[]{:S(2)}, u32[]{:S(2)}) %collective-permute-start.36) | collective-permute-done | bytes 393248 | tf_op jit(solution)/shard_map/ppermute | solution.py:447
  182.7 1.1 collective-permute-done.39.refs_15_.refs_19_
  183.8 2.9 %merge_3.1 = (bf16[1,128,768]{2,1,0:T(8,128)(2,1)}, bf16[1,128,768]{2,1,0:T(8,128)(2,1)}, bf16[1,128,768]{2,1,0:T(8,128)(2,1)}, bf16[1,128,768]{2,1,0:T(8,128)(2,1)}) custom-call(bf16[4,128,768]{2,1,0:T(8,128)(2,1)} %get-tuple-element.67.refs_0_.refs_3_.refs_1_, bf16[4,128,768]{2,1,0:T(8,128)(2,1)} %copy-done.1, bf16[4,128,768]{2,1,0:T(8,128)(2,1)} %copy-done, ...), custom_call_target="tpu_custom_call" | custom-call | bytes 3932160 | tf_op jit(solution)/shard_map/merge_3/pallas_call | solution.py:145
  186.7 2.2 collective-permute-start.40
  188.8 1.1 collective-permute-start.42
  190.5 4.6 %collective-permute-done.40.refs_5_ = bf16[1,128,768]{2,1,0:T(8,128)(2,1)S(1)} collective-permute-done((bf16[1,128,768]{2,1,0:T(8,128)(2,1)}, bf16[1,128,768]{2,1,0:T(8,128)(2,1)S(1)}, u32[]{:S(2)}, u32[]{:S(2)}) %collective-permute-start.40) | collective-permute-done | bytes 196640 | tf_op jit(solution)/shard_map/ppermute | solution.py:447
  195.8 1.1 collective-permute-done.43.refs_20_
  197.6 4.4 %leave_rows.1 = bf16[8,96,768]{2,1,0:T(8,128)(2,1)} custom-call(bf16[768,512]{1,0:T(8,128)(2,1)} %get-tuple-element.60.refs_0_, bf16[4,128,768]{2,1,0:T(8,128)(2,1)} %get-tuple-element.67.refs_0_.refs_3_.refs_1_, bf16[2,128,768]{2,1,0:T(8,128)(2,1)} %copy-done.2, bf16[4,128,768]{2,1,0:T(8,128)(2,1)} %copy-done, bf16[2,128,768]{2,1,0:T(8,128)(2,1)} %copy-done.4, ...), custom_call_target="tpu_custom_call" | custom-call | tf_op jit(solution)/shard_map/leave_rows/pallas_call | solution.py:115
  201.9 21.0 %all-to-all-start.1 = ((bf16[8,96,768]{2,1,0:T(8,128)(2,1)}), bf16[8,96,768]{2,1,0:T(8,128)(2,1)}, u32[]{:S(2)}, u32[]{:S(2)}) async-start(bf16[8,96,768]{2,1,0:T(8,128)(2,1)} %leave_rows.1), calls=%async_computation.1 | async-start | bytes 2359296 | tf_op jit(solution)/shard_map/all_to_all | solution.py:582
  222.9 15.9 %panel_grad.1 = bf16[16,256,768]{2,1,0:T(8,128)(2,1)} custom-call(s32[16,4]{1,0:T(8,128)} %copy.29.refs_0_, bf16[2,4,128,768]{3,2,1,0:T(8,128)(2,1)} %pad_maximum_fusion.refs_5_.refs_1_, bf16[2,4,128,768]{3,2,1,0:T(8,128)(2,1)} %collective-permute-done.12.refs_0_.refs_7_.refs_5_.refs_2_, ...), custom_call_target="tpu_custom_call" | custom-call | flops 6442450944 | bytes 27262976 | tf_op jit(solution)/shard_map/panel_grad/pallas_call | solution.py:416
  239.6 3.0 %home_rows.1 = bf16[512,768]{1,0:T(8,128)(2,1)} custom-call(bf16[8,96,768]{2,1,0:T(8,128)(2,1)} %all-to-all-done.1.back_ref, s32[1,512]{1,0:T(1,128)} %get-tuple-element.107.rank_ref), custom_call_target="tpu_custom_call" | custom-call | tf_op jit(solution)/shard_map/home_rows/pallas_call | solution.py:167
  (96 shorter events, 12.9 us)
Async XLA Ops:
  5.7 24.5 %all-to-all-start = ((bf16[8,112,768]{2,1,0:T(8,128)(2,1)}), bf16[8,112,768]{2,1,0:T(8,128)(2,1)}, u32[]{:S(2)}, u32[]{:S(2)}) async-start(bf16[8,112,768]{2,1,0:T(8,128)(2,1)} %get-tuple-element.58), calls=%async_computation | async-start | bytes 2752512 | tf_op jit(solution)/shard_map/all_to_all | solution.py:468
  11.5 2.8 %collective-permute-start = (bf16[1,2,16,256]{3,2,1,0:T(8,128)(2,1)S(1)}, bf16[1,2,16,256]{3,2,1,0:T(8,128)(2,1)S(1)}, u32[]{:S(2)}, u32[]{:S(2)}) collective-permute-start(bf16[1,2,16,256]{3,2,1,0:T(8,128)(2,1)S(1)} %fusion), channel_id=1, source_target_pairs={{0,1},{1,0},{2,3},{3,2},{4,5},{5,4},{6,7},{7,6},{8,9},{9,8},{10,11... | collective-permute-start | bytes 49160 | tf_op jit(solution)/shard_map/ppermute | solution.py:447
  14.3 4.9 %collective-permute-start.1 = (bf16[2,2,16,256]{3,2,1,0:T(8,128)(2,1)S(1)}, bf16[2,2,16,256]{3,2,1,0:T(8,128)(2,1)S(1)}, u32[]{:S(2)}, u32[]{:S(2)}) collective-permute-start(bf16[2,2,16,256]{3,2,1,0:T(8,128)(2,1)S(1)} %pad_maximum_fusion.4), channel_id=1, source_target_pairs={{0,3},{1,2},{2,1},{3,0},{4,7},{5,6},{6,5},{7,4},{8,11},{9,10},{10,... | collective-permute-start | bytes 98312 | tf_op jit(solution)/shard_map/ppermute | solution.py:447
  19.2 3.6 %collective-permute-start.2 = (bf16[4,2,16,256]{3,2,1,0:T(8,128)(2,1)S(1)}, bf16[4,2,16,256]{3,2,1,0:T(8,128)(2,1)S(1)}, u32[]{:S(2)}, u32[]{:S(2)}) collective-permute-start(bf16[4,2,16,256]{3,2,1,0:T(8,128)(2,1)S(1)} %pad_maximum_fusion.3), channel_id=1, source_target_pairs={{0,4},{1,5},{2,6},{3,7},{4,0},{5,1},{6,2},{7,3},{8,12},{9,13},{10,... | collective-permute-start | bytes 196616 | tf_op jit(solution)/shard_map/ppermute | solution.py:447
  22.8 5.6 %collective-permute-start.3 = (bf16[8,2,16,256]{3,2,1,0:T(8,128)(2,1)S(1)}, bf16[8,2,16,256]{3,2,1,0:T(8,128)(2,1)S(1)}, u32[]{:S(2)}, u32[]{:S(2)}) collective-permute-start(bf16[8,2,16,256]{3,2,1,0:T(8,128)(2,1)S(1)} %pad_maximum_fusion.2), channel_id=1, source_target_pairs={{0,12},{1,13},{2,14},{3,15},{4,8},{5,9},{6,10},{7,11},{8,4},{9,5},... | collective-permute-start | bytes 393224 | tf_op jit(solution)/shard_map/ppermute | solution.py:447
  28.4 1.8 copy-start.6
  33.8 18.6 %copy-start.8 = (bf16[2,128,768]{2,1,0:T(8,128)(2,1)S(1)}, bf16[2,128,768]{2,1,0:T(8,128)(2,1)}, u32[]{:S(2)}) copy-start(bf16[2,128,768]{2,1,0:T(8,128)(2,1)} %get-tuple-element.61) | copy-start | bytes 1179652
  33.8 11.9 %collective-permute-start.6 = (bf16[2,128,768]{2,1,0:T(8,128)(2,1)}, bf16[2,128,768]{2,1,0:T(8,128)(2,1)S(1)}, u32[]{:S(2)}, u32[]{:S(2)}) collective-permute-start(bf16[2,128,768]{2,1,0:T(8,128)(2,1)} %get-tuple-element.61), channel_id=1, source_target_pairs={{0,3},{1,2},{2,1},{3,0},{4,7},{5,6},{6,5},{7,4},{8,11},{9,10},{10,... | collective-permute-start | bytes 1179656 | tf_op jit(solution)/shard_map/ppermute | solution.py:447
  37.6 9.0 %collective-permute-start.4 = (bf16[2,128,768]{2,1,0:T(8,128)(2,1)}, bf16[2,128,768]{2,1,0:T(8,128)(2,1)S(1)}, u32[]{:S(2)}, u32[]{:S(2)}) collective-permute-start(bf16[2,128,768]{2,1,0:T(8,128)(2,1)} %get-tuple-element.61), channel_id=1, source_target_pairs={{0,1},{1,0},{2,3},{3,2},{4,5},{5,4},{6,7},{7,6},{8,9},{9,8},{10,11... | collective-permute-start | bytes 1179656 | tf_op jit(solution)/shard_map/ppermute | solution.py:447
  37.6 10.7 %collective-permute-start.10 = (bf16[2,128,768]{2,1,0:T(8,128)(2,1)}, bf16[2,128,768]{2,1,0:T(8,128)(2,1)S(1)}, u32[]{:S(2)}, u32[]{:S(2)}) collective-permute-start(bf16[2,128,768]{2,1,0:T(8,128)(2,1)} %get-tuple-element.62), channel_id=1, source_target_pairs={{0,12},{1,13},{2,14},{3,15},{4,8},{5,9},{6,10},{7,11},{8,4},{9,5},... | collective-permute-start | bytes 1179656 | tf_op jit(solution)/shard_map/ppermute | solution.py:447
  40.3 10.1 %collective-permute-start.8 = (bf16[2,128,768]{2,1,0:T(8,128)(2,1)}, bf16[2,128,768]{2,1,0:T(8,128)(2,1)S(1)}, u32[]{:S(2)}, u32[]{:S(2)}) collective-permute-start(bf16[2,128,768]{2,1,0:T(8,128)(2,1)} %get-tuple-element.62), channel_id=1, source_target_pairs={{0,4},{1,5},{2,6},{3,7},{4,0},{5,1},{6,2},{7,3},{8,12},{9,13},{10,... | collective-permute-start | bytes 1179656 | tf_op jit(solution)/shard_map/ppermute | solution.py:447
  45.7 6.7 %collective-permute-start.7 = (bf16[128,768]{1,0:T(8,128)(2,1)S(1)}, bf16[128,768]{1,0:T(8,128)(2,1)S(1)}, u32[]{:S(2)}, u32[]{:S(2)}) collective-permute-start(bf16[128,768]{1,0:T(8,128)(2,1)S(1)} %slice_bitcast_fusion.2), channel_id=1, source_target_pairs={{0,1},{1,0},{2,3},{3,2},{4,5},{5,4},{6,7},{7,6},{8,9},{9,8},{10,11... | collective-permute-start | bytes 589832 | tf_op jit(solution)/shard_map/ppermute | solution.py:447
  46.6 5.8 %collective-permute-start.5 = (bf16[128,768]{1,0:T(8,128)(2,1)S(1)}, bf16[128,768]{1,0:T(8,128)(2,1)S(1)}, u32[]{:S(2)}, u32[]{:S(2)}) collective-permute-start(bf16[128,768]{1,0:T(8,128)(2,1)S(1)} %slice_bitcast_fusion.3), channel_id=1, source_target_pairs={{0,3},{1,2},{2,1},{3,0},{4,7},{5,6},{6,5},{7,4},{8,11},{9,10},{10,... | collective-permute-start | bytes 589832 | tf_op jit(solution)/shard_map/ppermute | solution.py:447
  48.3 7.5 %collective-permute-start.11 = (bf16[128,768]{1,0:T(8,128)(2,1)S(1)}, bf16[128,768]{1,0:T(8,128)(2,1)S(1)}, u32[]{:S(2)}, u32[]{:S(2)}) collective-permute-start(bf16[128,768]{1,0:T(8,128)(2,1)S(1)} %slice_bitcast_fusion), channel_id=1, source_target_pairs={{0,4},{1,5},{2,6},{3,7},{4,0},{5,1},{6,2},{7,3},{8,12},{9,13},{10,... | collective-permute-start | bytes 589832 | tf_op jit(solution)/shard_map/ppermute | solution.py:447
  50.4 5.8 %collective-permute-start.9 = (bf16[128,768]{1,0:T(8,128)(2,1)S(1)}, bf16[128,768]{1,0:T(8,128)(2,1)S(1)}, u32[]{:S(2)}, u32[]{:S(2)}) collective-permute-start(bf16[128,768]{1,0:T(8,128)(2,1)S(1)} %slice_bitcast_fusion.1), channel_id=1, source_target_pairs={{0,12},{1,13},{2,14},{3,15},{4,8},{5,9},{6,10},{7,11},{8,4},{9,5},... | collective-permute-start | bytes 589832 | tf_op jit(solution)/shard_map/ppermute | solution.py:447
  52.4 3.8 %copy-start.7 = (bf16[2,128,768]{2,1,0:T(8,128)(2,1)S(1)}, bf16[2,128,768]{2,1,0:T(8,128)(2,1)}, u32[]{:S(2)}) copy-start(bf16[2,128,768]{2,1,0:T(8,128)(2,1)} %get-tuple-element.62) | copy-start | bytes 1179652
  53.8 33.0 %collective-permute-start.12 = (bf16[2,4,128,768]{3,2,1,0:T(8,128)(2,1)}, bf16[2,4,128,768]{3,2,1,0:T(8,128)(2,1)}, u32[]{:S(2)}, u32[]{:S(2)}) collective-permute-start(bf16[2,4,128,768]{3,2,1,0:T(8,128)(2,1)} %pad_maximum_fusion.refs_5_.refs_1_), channel_id=1, source_target_pairs={{0,4},{1,5},{2,6},{3,7},{4,0},{5,1},{6,2},{7,3},{8,12},{9,13},{10,... | collective-permute-start | bytes 4718600 | tf_op jit(solution)/shard_map/ppermute | solution.py:447
  56.3 6.8 %copy-start.13 = (bf16[16,256]{1,0:T(8,128)(2,1)S(1)}, bf16[16,256]{1,0:T(8,128)(2,1)}, u32[]{:S(2)}) copy-start(bf16[16,256]{1,0:T(8,128)(2,1)} %param.13) | copy-start | bytes 24580
  57.7 32.8 %collective-permute-start.13 = (bf16[2,4,128,768]{3,2,1,0:T(8,128)(2,1)}, bf16[2,4,128,768]{3,2,1,0:T(8,128)(2,1)}, u32[]{:S(2)}, u32[]{:S(2)}) collective-permute-start(bf16[2,4,128,768]{3,2,1,0:T(8,128)(2,1)} %pad_maximum_fusion.1.refs_6_), channel_id=1, source_target_pairs={{0,1},{1,0},{2,3},{3,2},{4,5},{5,4},{6,7},{7,6},{8,9},{9,8},{10,11... | collective-permute-start | bytes 4718600 | tf_op jit(solution)/shard_map/ppermute | solution.py:447
  58.5 33.1 %collective-permute-start.14 = (bf16[2,4,128,768]{3,2,1,0:T(8,128)(2,1)}, bf16[2,4,128,768]{3,2,1,0:T(8,128)(2,1)}, u32[]{:S(2)}, u32[]{:S(2)}) collective-permute-start(bf16[2,4,128,768]{3,2,1,0:T(8,128)(2,1)} %pad_maximum_fusion.refs_5_.refs_1_), channel_id=1, source_target_pairs={{0,12},{1,13},{2,14},{3,15},{4,8},{5,9},{6,10},{7,11},{8,4},{9,5},... | collective-permute-start | bytes 4718600 | tf_op jit(solution)/shard_map/ppermute | solution.py:447
  60.4 33.1 %collective-permute-start.15 = (bf16[2,4,128,768]{3,2,1,0:T(8,128)(2,1)}, bf16[2,4,128,768]{3,2,1,0:T(8,128)(2,1)}, u32[]{:S(2)}, u32[]{:S(2)}) collective-permute-start(bf16[2,4,128,768]{3,2,1,0:T(8,128)(2,1)} %pad_maximum_fusion.1.refs_6_), channel_id=1, source_target_pairs={{0,3},{1,2},{2,1},{3,0},{4,7},{5,6},{6,5},{7,4},{8,11},{9,10},{10,... | collective-permute-start | bytes 4718600 | tf_op jit(solution)/shard_map/ppermute | solution.py:447
  75.4 23.5 %collective-permute-start.20 = (bf16[2,128,768]{2,1,0:T(8,128)(2,1)}, bf16[2,128,768]{2,1,0:T(8,128)(2,1)S(1)}, u32[]{:S(2)}, u32[]{:S(2)}) collective-permute-start(bf16[2,128,768]{2,1,0:T(8,128)(2,1)} %get-tuple-element.68), channel_id=1, source_target_pairs={{0,1},{1,0},{2,3},{3,2},{4,5},{5,4},{6,7},{7,6},{8,9},{9,8},{10,11... | collective-permute-start | bytes 1179656 | tf_op jit(solution)/shard_map/ppermute | solution.py:447
  86.8 15.1 %collective-permute-start.23 = (bf16[2,128,768]{2,1,0:T(8,128)(2,1)}, bf16[2,128,768]{2,1,0:T(8,128)(2,1)S(1)}, u32[]{:S(2)}, u32[]{:S(2)}) collective-permute-start(bf16[2,128,768]{2,1,0:T(8,128)(2,1)} %get-tuple-element.75), channel_id=1, source_target_pairs={{0,3},{1,2},{2,1},{3,0},{4,7},{5,6},{6,5},{7,4},{8,11},{9,10},{10,... | collective-permute-start | bytes 1179656 | tf_op jit(solution)/shard_map/ppermute | solution.py:447
  96.3 22.9 %collective-permute-start.16 = (bf16[4,128,768]{2,1,0:T(8,128)(2,1)}, bf16[4,128,768]{2,1,0:T(8,128)(2,1)}, u32[]{:S(2)}, u32[]{:S(2)}) collective-permute-start(bf16[4,128,768]{2,1,0:T(8,128)(2,1)} %get-tuple-element.63), channel_id=1, source_target_pairs={{0,12},{1,13},{2,14},{3,15},{4,8},{5,9},{6,10},{7,11},{8,4},{9,5},... | collective-permute-start | bytes 2359304 | tf_op jit(solution)/shard_map/ppermute | solution.py:447
  96.9 23.5 %collective-permute-start.17 = (bf16[4,128,768]{2,1,0:T(8,128)(2,1)}, bf16[4,128,768]{2,1,0:T(8,128)(2,1)}, u32[]{:S(2)}, u32[]{:S(2)}) collective-permute-start(bf16[4,128,768]{2,1,0:T(8,128)(2,1)} %get-tuple-element.64), channel_id=1, source_target_pairs={{0,4},{1,5},{2,6},{3,7},{4,0},{5,1},{6,2},{7,3},{8,12},{9,13},{10,... | collective-permute-start | bytes 2359304 | tf_op jit(solution)/shard_map/ppermute | solution.py:447
  96.9 21.1 %collective-permute-start.26 = (bf16[2,128,768]{2,1,0:T(8,128)(2,1)}, bf16[2,128,768]{2,1,0:T(8,128)(2,1)}, u32[]{:S(2)}, u32[]{:S(2)}) collective-permute-start(bf16[2,128,768]{2,1,0:T(8,128)(2,1)} %get-tuple-element.81), channel_id=1, source_target_pairs={{0,4},{1,5},{2,6},{3,7},{4,0},{5,1},{6,2},{7,3},{8,12},{9,13},{10,... | collective-permute-start | bytes 1179656 | tf_op jit(solution)/shard_map/ppermute | solution.py:447
  98.9 19.1 %copy-start.2 = (bf16[2,128,768]{2,1,0:T(8,128)(2,1)}, bf16[2,128,768]{2,1,0:T(8,128)(2,1)S(1)}, u32[]{:S(2)}) copy-start(bf16[2,128,768]{2,1,0:T(8,128)(2,1)S(1)} %collective-permute-done.20.refs_1_.refs_2_) | copy-start | bytes 1179652
  98.9 21.6 %collective-permute-start.18 = (bf16[4,128,768]{2,1,0:T(8,128)(2,1)}, bf16[4,128,768]{2,1,0:T(8,128)(2,1)}, u32[]{:S(2)}, u32[]{:S(2)}) collective-permute-start(bf16[4,128,768]{2,1,0:T(8,128)(2,1)} %get-tuple-element.65), channel_id=1, source_target_pairs={{0,3},{1,2},{2,1},{3,0},{4,7},{5,6},{6,5},{7,4},{8,11},{9,10},{10,... | collective-permute-start | bytes 2359304 | tf_op jit(solution)/shard_map/ppermute | solution.py:447
  101.9 16.1 %copy-start.3 = (bf16[2,128,768]{2,1,0:T(8,128)(2,1)}, bf16[2,128,768]{2,1,0:T(8,128)(2,1)S(1)}, u32[]{:S(2)}) copy-start(bf16[2,128,768]{2,1,0:T(8,128)(2,1)S(1)} %collective-permute-done.23.refs_9_.refs_7_) | copy-start | bytes 1179652
  101.9 20.9 %collective-permute-start.19 = (bf16[4,128,768]{2,1,0:T(8,128)(2,1)}, bf16[4,128,768]{2,1,0:T(8,128)(2,1)}, u32[]{:S(2)}, u32[]{:S(2)}) collective-permute-start(bf16[4,128,768]{2,1,0:T(8,128)(2,1)} %get-tuple-element.66), channel_id=1, source_target_pairs={{0,1},{1,0},{2,3},{3,2},{4,5},{5,4},{6,7},{7,6},{8,9},{9,8},{10,11... | collective-permute-start | bytes 2359304 | tf_op jit(solution)/shard_map/ppermute | solution.py:447
  118.0 15.5 %collective-permute-start.21 = (bf16[4,128,768]{2,1,0:T(8,128)(2,1)}, bf16[4,128,768]{2,1,0:T(8,128)(2,1)S(1)}, u32[]{:S(2)}, u32[]{:S(2)}) collective-permute-start(bf16[4,128,768]{2,1,0:T(8,128)(2,1)} %get-tuple-element.71), channel_id=1, source_target_pairs={{0,1},{1,0},{2,3},{3,2},{4,5},{5,4},{6,7},{7,6},{8,9},{9,8},{10,11... | collective-permute-start | bytes 2359304 | tf_op jit(solution)/shard_map/ppermute | solution.py:447
  119.2 16.0 %collective-permute-start.24 = (bf16[4,128,768]{2,1,0:T(8,128)(2,1)}, bf16[4,128,768]{2,1,0:T(8,128)(2,1)}, u32[]{:S(2)}, u32[]{:S(2)}) collective-permute-start(bf16[4,128,768]{2,1,0:T(8,128)(2,1)} %get-tuple-element.77), channel_id=1, source_target_pairs={{0,3},{1,2},{2,1},{3,0},{4,7},{5,6},{6,5},{7,4},{8,11},{9,10},{10,... | collective-permute-start | bytes 2359304 | tf_op jit(solution)/shard_map/ppermute | solution.py:447
  120.4 15.3 %collective-permute-start.27 = (bf16[4,128,768]{2,1,0:T(8,128)(2,1)}, bf16[4,128,768]{2,1,0:T(8,128)(2,1)}, u32[]{:S(2)}, u32[]{:S(2)}) collective-permute-start(bf16[4,128,768]{2,1,0:T(8,128)(2,1)} %get-tuple-element.83), channel_id=1, source_target_pairs={{0,4},{1,5},{2,6},{3,7},{4,0},{5,1},{6,2},{7,3},{8,12},{9,13},{10,... | collective-permute-start | bytes 2359304 | tf_op jit(solution)/shard_map/ppermute | solution.py:447
  120.5 13.0 %collective-permute-start.29 = (bf16[2,128,768]{2,1,0:T(8,128)(2,1)}, bf16[2,128,768]{2,1,0:T(8,128)(2,1)}, u32[]{:S(2)}, u32[]{:S(2)}) collective-permute-start(bf16[2,128,768]{2,1,0:T(8,128)(2,1)} %get-tuple-element.87), channel_id=1, source_target_pairs={{0,12},{1,13},{2,14},{3,15},{4,8},{5,9},{6,10},{7,11},{8,4},{9,5},... | collective-permute-start | bytes 1179656 | tf_op jit(solution)/shard_map/ppermute | solution.py:447
  122.8 16.2 %collective-permute-start.30 = (bf16[4,128,768]{2,1,0:T(8,128)(2,1)}, bf16[4,128,768]{2,1,0:T(8,128)(2,1)}, u32[]{:S(2)}, u32[]{:S(2)}) collective-permute-start(bf16[4,128,768]{2,1,0:T(8,128)(2,1)} %get-tuple-element.89), channel_id=1, source_target_pairs={{0,12},{1,13},{2,14},{3,15},{4,8},{5,9},{6,10},{7,11},{8,4},{9,5},... | collective-permute-start | bytes 2359304 | tf_op jit(solution)/shard_map/ppermute | solution.py:447
  133.5 11.2 %collective-permute-start.22 = (bf16[2,128,768]{2,1,0:T(8,128)(2,1)}, bf16[2,128,768]{2,1,0:T(8,128)(2,1)}, u32[]{:S(2)}, u32[]{:S(2)}) collective-permute-start(bf16[2,128,768]{2,1,0:T(8,128)(2,1)} %get-tuple-element.73), channel_id=1, source_target_pairs={{0,1},{1,0},{2,3},{3,2},{4,5},{5,4},{6,7},{7,6},{8,9},{9,8},{10,11... | collective-permute-start | bytes 1179656 | tf_op jit(solution)/shard_map/ppermute | solution.py:447
  133.6 14.8 %copy-start.1 = (bf16[4,128,768]{2,1,0:T(8,128)(2,1)}, bf16[4,128,768]{2,1,0:T(8,128)(2,1)S(1)}, u32[]{:S(2)}) copy-start(bf16[4,128,768]{2,1,0:T(8,128)(2,1)S(1)} %collective-permute-done.21.refs_3_.refs_5_.refs_1_) | copy-start | bytes 2359300
  133.6 12.8 %collective-permute-start.25 = (bf16[2,128,768]{2,1,0:T(8,128)(2,1)}, bf16[2,128,768]{2,1,0:T(8,128)(2,1)}, u32[]{:S(2)}, u32[]{:S(2)}) collective-permute-start(bf16[2,128,768]{2,1,0:T(8,128)(2,1)} %get-tuple-element.79), channel_id=1, source_target_pairs={{0,3},{1,2},{2,1},{3,0},{4,7},{5,6},{6,5},{7,4},{8,11},{9,10},{10,... | collective-permute-start | bytes 1179656 | tf_op jit(solution)/shard_map/ppermute | solution.py:447
  135.2 11.5 %collective-permute-start.28 = (bf16[2,128,768]{2,1,0:T(8,128)(2,1)}, bf16[2,128,768]{2,1,0:T(8,128)(2,1)}, u32[]{:S(2)}, u32[]{:S(2)}) collective-permute-start(bf16[2,128,768]{2,1,0:T(8,128)(2,1)} %get-tuple-element.85), channel_id=1, source_target_pairs={{0,4},{1,5},{2,6},{3,7},{4,0},{5,1},{6,2},{7,3},{8,12},{9,13},{10,... | collective-permute-start | bytes 1179656 | tf_op jit(solution)/shard_map/ppermute | solution.py:447
  135.6 12.7 %collective-permute-start.31 = (bf16[2,128,768]{2,1,0:T(8,128)(2,1)}, bf16[2,128,768]{2,1,0:T(8,128)(2,1)}, u32[]{:S(2)}, u32[]{:S(2)}) collective-permute-start(bf16[2,128,768]{2,1,0:T(8,128)(2,1)} %get-tuple-element.91), channel_id=1, source_target_pairs={{0,12},{1,13},{2,14},{3,15},{4,8},{5,9},{6,10},{7,11},{8,4},{9,5},... | collective-permute-start | bytes 1179656 | tf_op jit(solution)/shard_map/ppermute | solution.py:447
  152.8 15.3 %collective-permute-start.32 = (bf16[4,128,768]{2,1,0:T(8,128)(2,1)}, bf16[4,128,768]{2,1,0:T(8,128)(2,1)S(1)}, u32[]{:S(2)}, u32[]{:S(2)}) collective-permute-start(bf16[4,128,768]{2,1,0:T(8,128)(2,1)} %get-tuple-element.92), channel_id=1, source_target_pairs={{0,3},{1,2},{2,1},{3,0},{4,7},{5,6},{6,5},{7,4},{8,11},{9,10},{10,... | collective-permute-start | bytes 2359304 | tf_op jit(solution)/shard_map/ppermute | solution.py:447
  153.9 14.2 %collective-permute-start.33 = (bf16[4,128,768]{2,1,0:T(8,128)(2,1)}, bf16[4,128,768]{2,1,0:T(8,128)(2,1)}, u32[]{:S(2)}, u32[]{:S(2)}) collective-permute-start(bf16[4,128,768]{2,1,0:T(8,128)(2,1)} %get-tuple-element.94), channel_id=1, source_target_pairs={{0,1},{1,0},{2,3},{3,2},{4,5},{5,4},{6,7},{7,6},{8,9},{9,8},{10,11... | collective-permute-start | bytes 2359304 | tf_op jit(solution)/shard_map/ppermute | solution.py:447
  154.0 14.1 %collective-permute-start.34 = (bf16[4,128,768]{2,1,0:T(8,128)(2,1)}, bf16[4,128,768]{2,1,0:T(8,128)(2,1)}, u32[]{:S(2)}, u32[]{:S(2)}) collective-permute-start(bf16[4,128,768]{2,1,0:T(8,128)(2,1)} %get-tuple-element.96), channel_id=1, source_target_pairs={{0,12},{1,13},{2,14},{3,15},{4,8},{5,9},{6,10},{7,11},{8,4},{9,5},... | collective-permute-start | bytes 2359304 | tf_op jit(solution)/shard_map/ppermute | solution.py:447
  156.3 11.8 %collective-permute-start.35 = (bf16[4,128,768]{2,1,0:T(8,128)(2,1)}, bf16[4,128,768]{2,1,0:T(8,128)(2,1)}, u32[]{:S(2)}, u32[]{:S(2)}) collective-permute-start(bf16[4,128,768]{2,1,0:T(8,128)(2,1)} %get-tuple-element.98), channel_id=1, source_target_pairs={{0,4},{1,5},{2,6},{3,7},{4,0},{5,1},{6,2},{7,3},{8,12},{9,13},{10,... | collective-permute-start | bytes 2359304 | tf_op jit(solution)/shard_map/ppermute | solution.py:447
  168.1 0.9 copy-start
  172.6 10.0 %collective-permute-start.36 = (bf16[2,128,768]{2,1,0:T(8,128)(2,1)}, bf16[2,128,768]{2,1,0:T(8,128)(2,1)S(1)}, u32[]{:S(2)}, u32[]{:S(2)}) collective-permute-start(bf16[2,128,768]{2,1,0:T(8,128)(2,1)} %get-tuple-element.99), channel_id=1, source_target_pairs={{0,4},{1,5},{2,6},{3,7},{4,0},{5,1},{6,2},{7,3},{8,12},{9,13},{10,... | collective-permute-start | bytes 1179656 | tf_op jit(solution)/shard_map/ppermute | solution.py:447
  173.7 8.9 %collective-permute-start.37 = (bf16[2,128,768]{2,1,0:T(8,128)(2,1)}, bf16[2,128,768]{2,1,0:T(8,128)(2,1)S(1)}, u32[]{:S(2)}, u32[]{:S(2)}) collective-permute-start(bf16[2,128,768]{2,1,0:T(8,128)(2,1)} %get-tuple-element.100), channel_id=1, source_target_pairs={{0,12},{1,13},{2,14},{3,15},{4,8},{5,9},{6,10},{7,11},{8,4},{9,5},... | collective-permute-start | bytes 1179656 | tf_op jit(solution)/shard_map/ppermute | solution.py:447
  174.3 8.3 %collective-permute-start.38 = (bf16[2,128,768]{2,1,0:T(8,128)(2,1)}, bf16[2,128,768]{2,1,0:T(8,128)(2,1)}, u32[]{:S(2)}, u32[]{:S(2)}) collective-permute-start(bf16[2,128,768]{2,1,0:T(8,128)(2,1)} %get-tuple-element.101), channel_id=1, source_target_pairs={{0,1},{1,0},{2,3},{3,2},{4,5},{5,4},{6,7},{7,6},{8,9},{9,8},{10,11... | collective-permute-start | bytes 1179656 | tf_op jit(solution)/shard_map/ppermute | solution.py:447
  175.6 8.2 %collective-permute-start.39 = (bf16[2,128,768]{2,1,0:T(8,128)(2,1)}, bf16[2,128,768]{2,1,0:T(8,128)(2,1)}, u32[]{:S(2)}, u32[]{:S(2)}) collective-permute-start(bf16[2,128,768]{2,1,0:T(8,128)(2,1)} %get-tuple-element.102), channel_id=1, source_target_pairs={{0,3},{1,2},{2,1},{3,0},{4,7},{5,6},{6,5},{7,4},{8,11},{9,10},{10,... | collective-permute-start | bytes 1179656 | tf_op jit(solution)/shard_map/ppermute | solution.py:447
  182.6 1.2 copy-start.4
  182.6 1.2 copy-start.5
  186.7 8.4 %collective-permute-start.40 = (bf16[1,128,768]{2,1,0:T(8,128)(2,1)}, bf16[1,128,768]{2,1,0:T(8,128)(2,1)S(1)}, u32[]{:S(2)}, u32[]{:S(2)}) collective-permute-start(bf16[1,128,768]{2,1,0:T(8,128)(2,1)} %get-tuple-element.103), channel_id=1, source_target_pairs={{0,12},{1,13},{2,14},{3,15},{4,8},{5,9},{6,10},{7,11},{8,4},{9,5},... | collective-permute-start | bytes 589832 | tf_op jit(solution)/shard_map/ppermute | solution.py:447
  188.8 7.0 %collective-permute-start.41 = (bf16[1,128,768]{2,1,0:T(8,128)(2,1)}, bf16[1,128,768]{2,1,0:T(8,128)(2,1)S(1)}, u32[]{:S(2)}, u32[]{:S(2)}) collective-permute-start(bf16[1,128,768]{2,1,0:T(8,128)(2,1)} %get-tuple-element.104), channel_id=1, source_target_pairs={{0,4},{1,5},{2,6},{3,7},{4,0},{5,1},{6,2},{7,3},{8,12},{9,13},{10,... | collective-permute-start | bytes 589832 | tf_op jit(solution)/shard_map/ppermute | solution.py:447
  188.8 7.0 %collective-permute-start.42 = (bf16[1,128,768]{2,1,0:T(8,128)(2,1)}, bf16[1,128,768]{2,1,0:T(8,128)(2,1)S(1)}, u32[]{:S(2)}, u32[]{:S(2)}) collective-permute-start(bf16[1,128,768]{2,1,0:T(8,128)(2,1)} %get-tuple-element.105), channel_id=1, source_target_pairs={{0,3},{1,2},{2,1},{3,0},{4,7},{5,6},{6,5},{7,4},{8,11},{9,10},{10,... | collective-permute-start | bytes 589832 | tf_op jit(solution)/shard_map/ppermute | solution.py:447
  189.9 6.9 %collective-permute-start.43 = (bf16[1,128,768]{2,1,0:T(8,128)(2,1)}, bf16[1,128,768]{2,1,0:T(8,128)(2,1)S(1)}, u32[]{:S(2)}, u32[]{:S(2)}) collective-permute-start(bf16[1,128,768]{2,1,0:T(8,128)(2,1)} %get-tuple-element.106), channel_id=1, source_target_pairs={{0,1},{1,0},{2,3},{3,2},{4,5},{5,4},{6,7},{7,6},{8,9},{9,8},{10,11... | collective-permute-start | bytes 589832 | tf_op jit(solution)/shard_map/ppermute | solution.py:447
  195.1 1.8 copy-start.9
  195.8 1.1 copy-start.10
  195.8 1.1 copy-start.11
  196.9 0.7 copy-start.12
  201.9 37.6 %all-to-all-start.1 = ((bf16[8,96,768]{2,1,0:T(8,128)(2,1)}), bf16[8,96,768]{2,1,0:T(8,128)(2,1)}, u32[]{:S(2)}, u32[]{:S(2)}) async-start(bf16[8,96,768]{2,1,0:T(8,128)(2,1)} %leave_rows.1), calls=%async_computation.1 | async-start | bytes 2359296 | tf_op jit(solution)/shard_map/all_to_all | solution.py:582
